TPU v7x, 32 devices: a whole 2x2x4 slice. The times are simulated.
32 devices in a mesh: space: 8 (over z, x), mem: 4 (over y, core).
Axes of the slice: x: 2, y: 2, z: 4, core: 2. Of those that a mesh axis runs over, the one named last changes fastest.
Arguments:
- state: float32 [64, 3, 128, 256], P('mem', None, 'space'), may hold values from -6 to 6
- depth: float32 [128, 256], P('space'), may hold values from 0.5 to 2
- obs_cells: int32 [4, 512, 128], P(None, 'space'), may hold values from 0 to 4095, as said below
- obs_weights: float32 [4, 512, 128], P(None, 'space'), may hold values from 0 to 0.5
- owner_map: int32 [512, 1], P('space'), may hold values from 0 to 7; in each aligned block of 64 rows (0 to 63, 64 to 127, ...) at most 16 rows name the same one
- obs_values: float32 [8, 8, 16, 128], P('space'), may hold values from -8 to 8
- obs_precision: float32 [8, 8, 16, 128], P('space'), may hold values from 0.5 to 6
Outputs:
- analysis: float32 [64, 3, 128, 256], P('mem', None, 'space')
Inputs may be any that keep to these rules, and one draw needn't show every extreme that they name: The cells of block b lie in the rows of space device b // 64; obs_cells is the offset within those rows. `owner_map`: among the 64 blocks of one space device no owner is named more than 16 times, and in some device one owner is named exactly 16 times.
All inputs are finite; a program needn't handle non-finite values.
Results may differ from a plain program's by a relative error of at most 0.00012.
Values sent between devices are 32-bit elements; how exact they have to be, the bound alone decides.
No kernel may reach another device: no remote copies, remote signals or barrier semaphores. Data moves between devices by JAX's collectives and lax.ppermute only.
A program may use at most 64 MiB of HBM per device.

v0:
```python
import math

import jax
import jax.numpy as jnp
from jax import lax
from jax.sharding import PartitionSpec as P

M = 64
STEPS = 2


mass_rate = 0.2
wave_rate = 0.2
turn_rate = 0.1


def with_halo(cells, sides, width):
    for axis, dim in sides:
        count = lax.axis_size(axis)
        ends = count - 1
        head = lax.slice_in_dim(cells, 0, width, axis=dim)
        tail = lax.slice_in_dim(cells, cells.shape[dim] - width, cells.shape[dim], axis=dim)
        cells = jnp.concatenate(
            [
                lax.ppermute(tail, axis, [(i, (i + 1) % count) for i in range(ends)]),
                cells,
                lax.ppermute(head, axis, [((i + 1) % count, i) for i in range(ends)]),
            ],
            axis=dim,
        )
    return cells


def diff_cols(field):
    return jnp.roll(field, -1, axis=-1) - jnp.roll(field, 1, axis=-1)


def gram_terms(values, seen, weight, scale):
    middle = jnp.mean(values, axis=0)
    factor = weight * scale
    scaled = (values - middle[None]) * factor[None]
    depart = (seen - middle) * factor
    gram = jnp.einsum("mrk,nrk->mn", scaled, scaled, precision=lax.Precision.HIGHEST)
    proj = jnp.einsum("mrk,rk->m", scaled, depart, precision=lax.Precision.HIGHEST)
    return (gram, proj)


def make_mixing(lower, proj, members):
    eye = jnp.eye(members, dtype=jnp.float32)
    first = lax.linalg.triangular_solve(lower, proj[:, None], left_side=True, lower=True)
    mean_weights = lax.linalg.triangular_solve(
        lower, first, left_side=True, lower=True, transpose_a=True
    )[:, 0]
    inverse_lower = lax.linalg.triangular_solve(lower, eye, left_side=True, lower=True)
    spread = math.sqrt(members - 1) * inverse_lower.T
    coef = mean_weights[:, None] + spread
    return coef + (1.0 - jnp.sum(coef, axis=0))[None, :] / members


def local(state, depth, obs_cells, obs_weights, owner_map, obs_values, obs_precision):
    local_ensemble, fields, horizontal_sums, vertical_sums = state.shape
    count = lax.axis_size("space")
    quarter = lax.axis_index("mem")
    fluid_elevation, zonal_wind, meridional_wind = (state[:, 0], state[:, 1], state[:, 2])
    for step in range(STEPS):
        flux_rimmed = with_halo(depth * zonal_wind, (("space", 1),), 1)
        fluid_elevation = fluid_elevation - mass_rate * (
            flux_rimmed[:, 2:] - flux_rimmed[:, :-2] + diff_cols(depth * meridional_wind)
        )
        height_rimmed = with_halo(fluid_elevation, (("space", 1),), 1)
        east_new = (
            zonal_wind
            - wave_rate * (height_rimmed[:, 2:] - height_rimmed[:, :-2])
            + turn_rate * meridional_wind
        )
        meridional_wind = (
            meridional_wind - wave_rate * diff_cols(fluid_elevation) - turn_rate * zonal_wind
        )
        zonal_wind = east_new
    prior_fields = jnp.stack([fluid_elevation, zonal_wind, meridional_wind], axis=1)
    src_blocks = obs_cells.shape[1]
    obs_width = obs_cells.shape[2]
    flat = fluid_elevation.reshape(local_ensemble, horizontal_sums * vertical_sums)
    predicted = jnp.sum(obs_weights[None] * flat[:, obs_cells], axis=1)
    owners = owner_map[:, 0]
    same = (owners[:, None] == owners[None, :]).astype(jnp.int32)
    order = jnp.arange(src_blocks, dtype=jnp.int32)
    earlier = (order[:, None] < order[None, :]).astype(jnp.int32)
    slots = jnp.sum(same * earlier, axis=0)
    scale = math.sqrt((M - 1) / (count * src_blocks * obs_width))
    got_values, got_weights = (
        lax.all_to_all(obs_values[0], "space", split_axis=0, concat_axis=0, tiled=True),
        lax.all_to_all(obs_precision[0], "space", split_axis=0, concat_axis=0, tiled=True),
    )
    seen_all = got_values[owners, slots]
    weight_all = got_weights[owners, slots]
    member_all = lax.all_to_all(predicted, "mem", split_axis=1, concat_axis=0, tiled=True)
    share = member_all.shape[1]
    seen = lax.dynamic_slice_in_dim(seen_all, quarter * share, share, 0)
    weight = lax.dynamic_slice_in_dim(weight_all, quarter * share, share, 0)
    gram, proj = gram_terms(member_all, seen, weight, scale)
    eye = jnp.eye(M, dtype=jnp.float32)
    gram, proj = lax.psum((gram, proj), ("space", "mem"))
    lower = jnp.linalg.cholesky((M - 1) * eye + gram)
    transform_weights = make_mixing(lower, proj, M)
    my_columns = lax.dynamic_slice_in_dim(
        transform_weights, quarter * local_ensemble, local_ensemble, 1
    )
    prior_vector = prior_fields.reshape(local_ensemble, 3 * horizontal_sums * vertical_sums)
    combined = jnp.einsum(
        "ij,ic->jc",
        my_columns,
        lax.all_gather(prior_vector, "mem", axis=0, tiled=True),
        precision=lax.Precision.HIGHEST,
    )
    return combined.reshape(local_ensemble, 3, horizontal_sums, vertical_sums)


def solution(mesh):
    return jax.shard_map(
        local,
        mesh=mesh,
        in_specs=(
            P("mem", None, "space", None),
            P("space", None),
            P(None, "space", None),
            P(None, "space", None),
            P("space", None),
            P("space", None, None, None),
            P("space", None, None, None),
        ),
        out_specs=P("mem", None, "space", None),
        check_vma=False,
    )
```

profile of v0, /device:TPU:0, one launch (start us, length us, event | category | flops | bytes accessed | tf_op | source)
XLA Modules:
  0.0 259.2 jit_solution(8783960489548435766)
XLA Ops:
  6.5 1.1 bitcast_multiply_fusion.1
  7.7 1.3 collective-permute-start
  9.0 5.5 %collective-permute-start.1 = (f32[16,1,256]{2,1,0:T(1,128)S(1)}, f32[16,1,256]{2,1,0:T(1,128)S(1)}, u32[]{:S(2)}, u32[]{:S(2)}) collective-permute-start(f32[16,1,256]{2,1,0:T(1,128)S(1)} %get-tuple-element.40), channel_id=1, source_target_pairs={{0,4},{4,8},{8,12},{12,16},{16,20},{20,24},{24,28},{1,5},{5,9},{9,... | collective-permute-start | bytes 49160 | tf_op jit(solution)/shard_map/ppermute | solution.py:25
  14.5 6.2 %all-to-all-start.1 = ((f32[8,16,128]{2,1,0:T(8,128)}), f32[8,16,128]{2,1,0:T(8,128)S(1)}, u32[]{:S(2)}, u32[]{:S(2)}) async-start(f32[8,16,128]{2,1,0:T(8,128)} %bitcast.97), calls=%async_computation.1 | async-start | bytes 131072 | tf_op jit(solution)/shard_map/all_to_all | solution.py:93
  20.7 0.0 all-gather.2.cloned.1.call-start
  20.8 0.1 fusion.55
  20.9 0.1 fusion.54
  21.0 0.0 collective-permute-done
  21.0 0.0 collective-permute-done.1
  21.0 1.1 fusion.20
  22.2 0.1 fusion.52
  22.4 1.3 collective-permute-start.2
  23.7 4.5 %collective-permute-start.3 = (f32[16,1,256]{2,1,0:T(1,128)S(1)}, f32[16,1,256]{2,1,0:T(1,128)S(1)}, u32[]{:S(2)}, u32[]{:S(2)}) collective-permute-start(f32[16,1,256]{2,1,0:T(1,128)S(1)} %get-tuple-element.30), channel_id=1, source_target_pairs={{0,4},{4,8},{8,12},{12,16},{16,20},{20,24},{24,28},{1,5},{5,9},{9,... | collective-permute-start | bytes 49160 | tf_op jit(solution)/shard_map/ppermute | solution.py:25
  28.2 0.1 fusion.53
  28.3 1.3 collective-permute-done.3
  29.6 0.2 broadcast_multiply_fusion.1
  29.9 0.1 fusion.49
  30.1 1.3 collective-permute-start.4
  31.4 5.4 %collective-permute-start.5 = (f32[16,1,256]{2,1,0:T(1,128)S(1)}, f32[16,1,256]{2,1,0:T(1,128)S(1)}, u32[]{:S(2)}, u32[]{:S(2)}) collective-permute-start(f32[16,1,256]{2,1,0:T(1,128)S(1)} %get-tuple-element.28), channel_id=1, source_target_pairs={{0,4},{4,8},{8,12},{12,16},{16,20},{20,24},{24,28},{1,5},{5,9},{9,... | collective-permute-start | bytes 49160 | tf_op jit(solution)/shard_map/ppermute | solution.py:25
  36.8 0.1 fusion.48
  36.9 1.3 collective-permute-done.5
  38.2 0.2 fusion.12
  38.4 0.1 fusion.47
  38.5 0.0 copy-start.2
  38.6 1.4 collective-permute-start.6
  40.0 5.7 %collective-permute-start.7 = (f32[16,1,256]{2,1,0:T(1,128)S(1)}, f32[16,1,256]{2,1,0:T(1,128)S(1)}, u32[]{:S(2)}, u32[]{:S(2)}) collective-permute-start(f32[16,1,256]{2,1,0:T(1,128)S(1)} %get-tuple-element.18), channel_id=1, source_target_pairs={{0,4},{4,8},{8,12},{12,16},{16,20},{20,24},{24,28},{1,5},{5,9},{9,... | collective-permute-start | bytes 49160 | tf_op jit(solution)/shard_map/ppermute | solution.py:25
  45.8 0.1 fusion.46
  45.9 0.0 collective-permute-done.6
  45.9 1.3 collective-permute-done.7
  47.2 0.2 fusion.8
  47.4 0.1 pad_maximum_fusion
  47.5 0.1 copy.44
  47.5 1.3 copy.49
  48.9 0.0 all-gather.2.cloned.1.call-update
  49.0 0.6 copy.37
  49.6 0.0 copy-start.1
  49.6 108.2 %gather_fusion = f32[32768,16]{1,0:T(8,128)} fusion(f32[16,4096]{0,1:T(8,128)S(1)} %bitcast.87, s32[32768]{0:T(1024)S(1)} %broadcast_clamp_fusion), kind=kCustom, calls=%fused_computation | custom fusion | bytes 4325376 | tf_op jit(solution)/shard_map/gather | solution.py:84
  157.8 0.0 all-to-all-done.1
  157.8 9.1 %all-to-all-start.2 = ((f32[8,16,128]{2,1,0:T(8,128)}), f32[8,16,128]{2,1,0:T(8,128)S(1)}, u32[]{:S(2)}, u32[]{:S(2)}) async-start(f32[8,16,128]{2,1,0:T(8,128)} %bitcast.20), calls=%async_computation.2 | async-start | bytes 131072 | tf_op jit(solution)/shard_map/all_to_all | solution.py:92
  166.9 9.8 %multiply_reduce_fusion = f32[64,128,16]{2,1,0:T(8,128)} fusion(f32[4,64,128,16]{3,2,1,0:T(8,128)} %bitcast.88, f32[4,64,128]{2,1,0:T(8,128)S(1)} %copy-done.1), kind=kLoop, calls=%fused_computation.3 | loop fusion | flops 917504 | bytes 2752512 | tf_op jit(solution)/shard_map/reduce_sum | solution.py:84
  176.8 3.5 %copy.38 = f32[16,64,128]{2,0,1:T(8,128)} copy(f32[16,64,128]{0,2,1:T(8,128)} %bitcast.89) | data formatting | bytes 1048576 | tf_op jit(solution)/shard_map/reduce_sum | solution.py:84
  180.3 0.0 all-to-all-done.2
  180.3 3.5 %all-to-all-start = ((f32[16,64,128]{2,0,1:T(8,128)}), f32[16,64,128]{2,0,1:T(8,128)S(1)}, u32[]{:S(2)}, u32[]{:S(2)}) async-start(f32[16,64,128]{2,0,1:T(8,128)} %copy.38), calls=%async_computation | async-start | bytes 1048576 | tf_op jit(solution)/shard_map/all_to_all | solution.py:97
  183.8 0.1 select_reduce_fusion.1
  183.9 0.9 gather_fusion.1
  184.7 0.9 gather_fusion.2
  185.6 6.9 %all-to-all-done = f32[16,64,128]{2,0,1:T(8,128)S(1)} async-done(((f32[16,64,128]{2,0,1:T(8,128)}), f32[16,64,128]{2,0,1:T(8,128)S(1)}, u32[]{:S(2)}, u32[]{:S(2)}) %all-to-all-start) | async-done | bytes 524320 | tf_op jit(solution)/shard_map/all_to_all | solution.py:97
  192.6 0.2 copy.40
  192.7 0.2 copy.39
  192.9 0.1 reduce_sum.39
  193.0 0.7 convolution_bitcast_fusion
  193.8 0.6 convolution_bitcast_fusion.3
  194.4 40.3 %all-reduce = (f32[64,64]{1,0:T(8,128)S(1)}, f32[64]{0:T(128)S(1)}) all-reduce(f32[64,64]{1,0:T(8,128)S(1)} %convolution_bitcast_fusion, f32[64]{0:T(128)S(1)} %convolution_bitcast_fusion.3), channel_id=1, replica_groups=mesh['space'=8,'mem'=4] {'space','mem'}, use_global_device_ids=true, to_apply=%region_3.4 | all-reduce | flops 4160 | bytes 33280 | tf_op jit(solution)/shard_map/psum | solution.py:103
  234.7 0.1 copy.43
  234.8 5.8 %cholesky.17 = f32[64,64]{1,0:T(8,128)S(1)} custom-call(f32[64,64]{1,0:T(8,128)S(1)} %fusion.32), custom_call_target="Cholesky" | custom-call | tf_op jit(solution)/shard_map/jit(cholesky)/cholesky | solution.py:104
  240.7 0.7 compare_reduce_fusion
  241.4 0.7 fusion.28
  242.1 4.9 %custom-call.10 = f32[1,64,64]{1,2,0:T(8,128)S(1)} custom-call(f32[1,64,64]{2,1,0:T(8,128)S(1)} %fusion.28), custom_call_target="InvertDiagBlocksLowerTriangular" | custom-call | tf_op jit(solution)/shard_map/triangular_solve | solution.py:51
  247.0 0.2 convolution_bitcast_fusion.2
  247.1 0.2 convolution_bitcast_fusion.1
  247.3 0.3 fusion.57
  247.7 0.1 dynamic-slice
  247.7 3.5 %fusion.33 = f32[16,12288]{1,0:T(8,128)S(1)} fusion(f32[64,12288]{1,0:T(8,128)} %all-gather.2.cloned.1.call-done, f32[64,64]{0,1:T(8,128)S(1)} %get-tuple-element.45, s32[]{:T(128)S(6)} %select_n.31, f32[16]{0:T(128)S(1)} %dynamic-slice), kind=kOutput, calls=%fused_computation.73 | convolution fusion | flops 150995968 | bytes 3940868 | tf_op jit(solution)/shard_map/ij,ic->jc/dot_general | solution.py:110
  251.2 1.1 copy.50
  (24 shorter events, 0.3 us)
Async XLA Ops:
  6.5 23.1 %copy-start = (f32[16,3,16,256]{3,2,1,0:T(8,128)S(1)}, f32[16,3,16,256]{3,2,1,0:T(8,128)}, u32[]{:S(2)}) copy-start(f32[16,3,16,256]{3,2,1,0:T(8,128)} %param.7) | copy-start | bytes 2359300
  6.5 23.1 %copy-start.3 = (f32[16,256]{1,0:T(8,128)S(1)}, f32[16,256]{1,0:T(8,128)}, u32[]{:S(2)}) copy-start(f32[16,256]{1,0:T(8,128)} %param.8) | copy-start | bytes 49156
  7.7 13.3 %collective-permute-start = (f32[16,1,256]{2,1,0:T(1,128)S(1)}, f32[16,1,256]{2,1,0:T(1,128)S(1)}, u32[]{:S(2)}, u32[]{:S(2)}) collective-permute-start(f32[16,1,256]{2,1,0:T(1,128)S(1)} %get-tuple-element.39), channel_id=1, source_target_pairs={{4,0},{8,4},{12,8},{16,12},{20,16},{24,20},{28,24},{5,1},{9,5},{13... | collective-permute-start | bytes 49160 | tf_op jit(solution)/shard_map/ppermute | solution.py:27
  9.0 12.0 %collective-permute-start.1 = (f32[16,1,256]{2,1,0:T(1,128)S(1)}, f32[16,1,256]{2,1,0:T(1,128)S(1)}, u32[]{:S(2)}, u32[]{:S(2)}) collective-permute-start(f32[16,1,256]{2,1,0:T(1,128)S(1)} %get-tuple-element.40), channel_id=1, source_target_pairs={{0,4},{4,8},{8,12},{12,16},{16,20},{20,24},{24,28},{1,5},{5,9},{9,... | collective-permute-start | bytes 49160 | tf_op jit(solution)/shard_map/ppermute | solution.py:25
  14.5 143.3 %all-to-all-start.1 = ((f32[8,16,128]{2,1,0:T(8,128)}), f32[8,16,128]{2,1,0:T(8,128)S(1)}, u32[]{:S(2)}, u32[]{:S(2)}) async-start(f32[8,16,128]{2,1,0:T(8,128)} %bitcast.97), calls=%async_computation.1 | async-start | bytes 131072 | tf_op jit(solution)/shard_map/all_to_all | solution.py:93
  20.7 227.0 %all-gather.2.cloned.1.call-start = ((), (), s32[]{:S(2)}) async-start(), calls=%async_computation.3 | async-start | bytes 3932160 | tf_op jit(solution)/shard_map/all_gather | solution.py:113
  22.4 6.0 %collective-permute-start.2 = (f32[16,1,256]{2,1,0:T(1,128)S(1)}, f32[16,1,256]{2,1,0:T(1,128)S(1)}, u32[]{:S(2)}, u32[]{:S(2)}) collective-permute-start(f32[16,1,256]{2,1,0:T(1,128)S(1)} %get-tuple-element.29), channel_id=1, source_target_pairs={{4,0},{8,4},{12,8},{16,12},{20,16},{24,20},{28,24},{5,1},{9,5},{13... | collective-permute-start | bytes 49160 | tf_op jit(solution)/shard_map/ppermute | solution.py:27
  23.7 6.0 %collective-permute-start.3 = (f32[16,1,256]{2,1,0:T(1,128)S(1)}, f32[16,1,256]{2,1,0:T(1,128)S(1)}, u32[]{:S(2)}, u32[]{:S(2)}) collective-permute-start(f32[16,1,256]{2,1,0:T(1,128)S(1)} %get-tuple-element.30), channel_id=1, source_target_pairs={{0,4},{4,8},{8,12},{12,16},{16,20},{20,24},{24,28},{1,5},{5,9},{9,... | collective-permute-start | bytes 49160 | tf_op jit(solution)/shard_map/ppermute | solution.py:25
  30.1 6.8 %collective-permute-start.4 = (f32[16,1,256]{2,1,0:T(1,128)S(1)}, f32[16,1,256]{2,1,0:T(1,128)S(1)}, u32[]{:S(2)}, u32[]{:S(2)}) collective-permute-start(f32[16,1,256]{2,1,0:T(1,128)S(1)} %get-tuple-element.27), channel_id=1, source_target_pairs={{4,0},{8,4},{12,8},{16,12},{20,16},{24,20},{28,24},{5,1},{9,5},{13... | collective-permute-start | bytes 49160 | tf_op jit(solution)/shard_map/ppermute | solution.py:27
  31.4 6.8 %collective-permute-start.5 = (f32[16,1,256]{2,1,0:T(1,128)S(1)}, f32[16,1,256]{2,1,0:T(1,128)S(1)}, u32[]{:S(2)}, u32[]{:S(2)}) collective-permute-start(f32[16,1,256]{2,1,0:T(1,128)S(1)} %get-tuple-element.28), channel_id=1, source_target_pairs={{0,4},{4,8},{8,12},{12,16},{16,20},{20,24},{24,28},{1,5},{5,9},{9,... | collective-permute-start | bytes 49160 | tf_op jit(solution)/shard_map/ppermute | solution.py:25
  38.5 10.4 %copy-start.2 = (s32[4,64,128]{2,1,0:T(8,128)S(1)}, s32[4,64,128]{2,1,0:T(8,128)}, u32[]{:S(2)}) copy-start(s32[4,64,128]{2,1,0:T(8,128)} %param.9) | copy-start | bytes 393220
  38.6 7.3 %collective-permute-start.6 = (f32[16,1,256]{2,1,0:T(1,128)S(1)}, f32[16,1,256]{2,1,0:T(1,128)S(1)}, u32[]{:S(2)}, u32[]{:S(2)}) collective-permute-start(f32[16,1,256]{2,1,0:T(1,128)S(1)} %get-tuple-element.17), channel_id=1, source_target_pairs={{4,0},{8,4},{12,8},{16,12},{20,16},{24,20},{28,24},{5,1},{9,5},{13... | collective-permute-start | bytes 49160 | tf_op jit(solution)/shard_map/ppermute | solution.py:27
  40.0 7.2 %collective-permute-start.7 = (f32[16,1,256]{2,1,0:T(1,128)S(1)}, f32[16,1,256]{2,1,0:T(1,128)S(1)}, u32[]{:S(2)}, u32[]{:S(2)}) collective-permute-start(f32[16,1,256]{2,1,0:T(1,128)S(1)} %get-tuple-element.18), channel_id=1, source_target_pairs={{0,4},{4,8},{8,12},{12,16},{16,20},{20,24},{24,28},{1,5},{5,9},{9,... | collective-permute-start | bytes 49160 | tf_op jit(solution)/shard_map/ppermute | solution.py:25
  49.6 117.4 %copy-start.1 = (f32[4,64,128]{2,1,0:T(8,128)S(1)}, f32[4,64,128]{2,1,0:T(8,128)}, u32[]{:S(2)}) copy-start(f32[4,64,128]{2,1,0:T(8,128)} %param.10) | copy-start | bytes 393220
  157.8 22.4 %all-to-all-start.2 = ((f32[8,16,128]{2,1,0:T(8,128)}), f32[8,16,128]{2,1,0:T(8,128)S(1)}, u32[]{:S(2)}, u32[]{:S(2)}) async-start(f32[8,16,128]{2,1,0:T(8,128)} %bitcast.20), calls=%async_computation.2 | async-start | bytes 131072 | tf_op jit(solution)/shard_map/all_to_all | solution.py:92
  176.8 7.0 %copy-start.4 = (s32[64,1]{0,1:T(1,128)S(1)}, s32[64,1]{0,1:T(1,128)}, u32[]{:S(2)}) copy-start(s32[64,1]{0,1:T(1,128)} %param.11) | copy-start | bytes 772
  180.3 12.3 %all-to-all-start = ((f32[16,64,128]{2,0,1:T(8,128)}), f32[16,64,128]{2,0,1:T(8,128)S(1)}, u32[]{:S(2)}, u32[]{:S(2)}) async-start(f32[16,64,128]{2,0,1:T(8,128)} %copy.38), calls=%async_computation | async-start | bytes 1048576 | tf_op jit(solution)/shard_map/all_to_all | solution.py:97
Sparse Core Ops, SparseCore 0:
  49.0 33.0 all-gather.1
where the time goes:
time: 260 us; the launch traced here: 259 us
  local copies, waits for them, and re-layouts  118 us (45%)
  starting transfers between devices  45.3 us (17%)
  blocking collectives  40.3 us (15%)
  other arithmetic  25.3 us (10%)
  between operations  13.8 us (5%)
  waiting for transfers between devices  10.9 us (4%)
  matrix products  5.47 us (2%)
    gather x1, local copies, waits for them, and re-layouts, local(): predicted = jnp.sum(obs_weights[None] * flat[:, obs_cells], axis=1)  108 us
    psum x1, blocking collectives, local(): gram, proj = lax.psum((gram, proj), ('space', 'mem'))  40.3 us
    ppermute x4, starting transfers between devices, with_halo(): lax.ppermute(tail, axis, [(i, (i + 1) % count) for i in range(ends)])  21.2 us
    reduce_sum x1, other arithmetic, local(): predicted = jnp.sum(obs_weights[None] * flat[:, obs_cells], axis=1)  9.82 us
    all_to_all x1, starting transfers between devices, local(): lax.all_to_all(obs_values[0], 'space', split_axis=0, concat_axis=0, tiled...  9.1 us
    all_to_all x1, waiting for transfers between devices, local(): lax.all_to_all(predicted, 'mem', split_axis=1, concat_axis=0, tiled=True)  6.92 us
    another operation x3, other arithmetic, local(): lower = jnp.linalg.cholesky((M - 1) * eye + gram)  6.6 us
    all_to_all x1, starting transfers between devices, local(): lax.all_to_all(obs_precision[0], 'space', split_axis=0, concat_axis=0, ti...  6.23 us
  transfers between devices with their start and end apart: 12, of which 4 were waited for; matrix products, arithmetic and copies ran while one was open for 55% of the time, Pallas kernels for 0%

commit v1 on v0

v1 whole, which is shorter than its diff:
```python
import functools
import math

import jax
import jax.numpy as jnp
from jax import lax
from jax.experimental import pallas as pl
from jax.experimental.pallas import tpu as pltpu
from jax.sharding import PartitionSpec as P

STEPS = 2
RIM = 2 * STEPS

mass_rate = 0.2
wave_rate = 0.2
turn_rate = 0.1

VMEM = pl.BlockSpec(memory_space=pltpu.VMEM)
SMEM = pl.BlockSpec(memory_space=pltpu.SMEM)
F32 = jnp.float32
BF16 = jnp.bfloat16


def diff_cols(field):
    width = field.shape[-1]
    return pltpu.roll(field, width - 1, 1) - pltpu.roll(field, 1, 1)


def forecast_kernel(inside, state, above, below, depth, height_out, wind_out, h, u, v, flux):
    members, _, rows, cols = state.shape
    total = rows + 2 * RIM
    deep = [above[3 * members, t : t + 1] for t in range(RIM)]
    deep += [depth[t : t + 1] for t in range(rows)]
    deep += [below[3 * members, t : t + 1] for t in range(RIM)]
    deep = [jnp.broadcast_to(d, (members, cols)) for d in deep]

    for field, dst in enumerate((h, u, v)):
        for t in range(RIM):
            dst[t] = above[field * members : (field + 1) * members, t, :]
            dst[RIM + rows + t] = below[field * members : (field + 1) * members, t, :]
        for t in range(rows):
            dst[RIM + t] = state[:, field, t, :]

    for step in range(STEPS):
        low, high = 2 * step, total - 2 * step
        for e in range(low, high):
            flux[e] = deep[e] * u[e]
        for e in range(low + 1, high - 1):
            new = h[e] - mass_rate * (flux[e + 1] - flux[e - 1] + diff_cols(deep[e] * v[e]))
            if e < RIM:
                new = new * inside[0]
            elif e >= RIM + rows:
                new = new * inside[1]
            h[e] = new
        for e in range(low + 2, high - 2):
            east, north, mid = u[e], v[e], h[e]
            u[e] = east - wave_rate * (h[e + 1] - h[e - 1]) + turn_rate * north
            v[e] = north - wave_rate * diff_cols(mid) - turn_rate * east
    for t in range(rows):
        height_out[t] = h[RIM + t]
        wind_out[0, t] = u[RIM + t]
        wind_out[1, t] = v[RIM + t]


def forecast(inside, state, above, below, depth):
    members, _, rows, cols = state.shape
    total = rows + 2 * RIM
    return pl.pallas_call(
        forecast_kernel,
        out_shape=(
            jax.ShapeDtypeStruct((rows, members, cols), F32),
            jax.ShapeDtypeStruct((2, rows, members, cols), F32),
        ),
        in_specs=[SMEM, VMEM, VMEM, VMEM, VMEM],
        out_specs=(VMEM, VMEM),
        scratch_shapes=[pltpu.VMEM((total, members, cols), F32)] * 4,
        compiler_params=pltpu.CompilerParams(vmem_limit_bytes=32 * 1024 * 1024),
        name="forecast",
    )(inside, state, above, below, depth)


def gram_kernel(scale, count_mem, place, owners, *refs):
    pieces = refs[:count_mem]
    cells, weights, got, out, split, seen, factor, lined, used = refs[count_mem:]
    rows, members, cols = pieces[0].shape
    total = members * count_mem
    points, blocks, width = cells.shape
    all_blocks = owners.shape[0]
    slots = got.shape[1] // 2
    quarter = place[0]

    for owner in range(got.shape[0]):
        used[owner] = 0

    def dispatch(b, carry):
        owner = owners[b]
        slot = used[owner]
        used[owner] = slot + 1
        local = b - quarter * blocks

        @pl.when((local >= 0) & (local < blocks))
        def _():
            seen[pl.ds(local, 1)] = got[owner, pl.ds(slot, 1)]
            factor[pl.ds(local, 1)] = got[owner, pl.ds(slot + slots, 1)] * scale

        return carry

    lax.fori_loop(0, all_blocks, dispatch, 0)

    for k, piece in enumerate(pieces):
        who = lax.bitwise_xor(quarter, k)
        for r in range(rows):
            x = piece[r]
            high = x.astype(BF16)
            low = (x - high.astype(F32)).astype(BF16)
            at = pl.ds(pl.multiple_of(r * total + who * members, members), members)
            split[at, 0:cols] = high
            split[at, cols : 2 * cols] = low

    lined[total : 2 * total] = jnp.zeros((total, blocks * width), F32)

    def block(b, carry):
        result = None
        for half in range(points // 2):
            cell = jnp.concatenate(
                [cells[2 * half, pl.ds(b, 1), :], cells[2 * half + 1, pl.ds(b, 1), :]], axis=1
            )
            share = jnp.concatenate(
                [weights[2 * half, pl.ds(b, 1), :], weights[2 * half + 1, pl.ds(b, 1), :]], axis=1
            )
            row = cell // cols
            col = jnp.broadcast_to(cell - row * cols, (cols, 2 * width))
            here = lax.broadcasted_iota(jnp.int32, (cols, 2 * width), 0) == col
            pick = jnp.where(here, 1.0, 0.0).astype(BF16)
            lines = jnp.dot(
                split[...], jnp.concatenate([pick, pick], axis=0), preferred_element_type=F32
            )
            for r in range(rows):
                term = lines[r * total : (r + 1) * total] * jnp.where(row == r, share, 0.0)
                term = term[:, :width] + term[:, width:]
                result = term if result is None else result + term
        middle = jnp.sum(result, axis=0, keepdims=True) * (1.0 / total)
        much = factor[pl.ds(b, 1)]
        at = pl.ds(pl.multiple_of(b * width, width), width)
        lined[0:total, at] = (result - middle) * much
        lined[total : total + 1, at] = (seen[pl.ds(b, 1)] - middle) * much
        return carry

    lax.fori_loop(0, blocks, block, 0, unroll=2)

    x = lined[...]
    gram = lax.dot_general(
        x, x, (((1,), (1,)), ((), ())), precision=lax.Precision.HIGHEST, preferred_element_type=F32
    )
    packed = pack_gram(gram, total)
    for d in range(out.shape[0]):
        out[d] = packed


def pack_gram(gram, total):
    half, quarter = total // 2, total // 4
    span = 2 * total
    top, low = gram[0:half], gram[half:total]
    lane = lax.broadcasted_iota(jnp.int32, (half, span), 1)
    line = lax.broadcasted_iota(jnp.int32, (half, span), 0)
    both = jnp.where(lane <= line, top, pltpu.roll(low, span - half, 1))
    wide = jnp.where(lane < half, both, pltpu.roll(low, half, 1))
    lane_q = lane[0:quarter]
    body = jnp.where(lane_q < total, wide[0:quarter], pltpu.roll(wide[quarter:half], total, 1))
    diag = jnp.sum(jnp.where(lane == line + half, low, 0.0), axis=0, keepdims=True)
    lane_1 = lane[0:8]
    tail = jnp.where(
        lane_1 < total, gram[total : total + 8], pltpu.roll(jnp.broadcast_to(diag, (8, span)), half, 1)
    )
    return jnp.concatenate([body, tail], axis=0)


def unpack_gram(packed, total):
    half, quarter = total // 2, total // 4
    span = 2 * total
    body, tail = packed[0:quarter], packed[quarter : quarter + 1]
    wide = jnp.concatenate([body, pltpu.roll(body, total, 1)], axis=0)
    low = pltpu.roll(wide, span - half, 1)
    lane = lax.broadcasted_iota(jnp.int32, (half, span), 1)
    line = lax.broadcasted_iota(jnp.int32, (half, span), 0)
    first = lane < half
    stacked = jnp.concatenate(
        [jnp.where(first, wide, 0.0), jnp.where(first, low, 0.0), jnp.zeros((total, span), F32)], axis=0
    )
    turned = stacked.T[0:half]
    top = jnp.where(first & (lane <= line), wide, turned)
    diag = pltpu.roll(jnp.broadcast_to(tail, (half, span)), span - half, 1)
    corner = jnp.where(lane > line, wide, turned)
    corner = pltpu.roll(jnp.where(first, corner, 0.0), half, 1)
    corner = jnp.where(lane == line + half, diag, corner)
    bottom = jnp.where(first, low, corner)
    return jnp.concatenate([top, bottom], axis=0), tail


def analysis_kernel(count_mem, place, sums, *refs):
    heights = refs[:count_mem]
    winds = refs[count_mem : 2 * count_mem]
    out, lower, stack = refs[2 * count_mem :]
    rows, members, cols = heights[0].shape
    total = members * count_mem
    span = 2 * total
    quarter = place[0]

    packed = sums[0]
    for d in range(1, sums.shape[0]):
        packed = packed + sums[d]
    system, proj = unpack_gram(packed, total)
    lane = lax.broadcasted_iota(jnp.int32, (total, span), 1)
    line = lax.broadcasted_iota(jnp.int32, (total, span), 0)
    work = jnp.where(
        lane < total,
        system + jnp.where(lane == line, float(total - 1), 0.0),
        jnp.where(lane == line + total, 1.0, 0.0),
    )
    tiles = [work[8 * g : 8 * g + 8] for g in range(total // 8)]
    below = lax.broadcasted_iota(jnp.int32, (8, span), 0)
    for k in range(total):
        g, s = k // 8, k % 8
        pivot = jnp.broadcast_to(tiles[g][s : s + 1], (8, span))
        scaled = pivot / jnp.broadcast_to(pivot[:, k : k + 1], (8, span))
        for t in range(g, total // 8):
            if t == g and s == 7:
                continue
            column = jnp.broadcast_to(tiles[t][:, k : k + 1], (8, span))
            if t == g:
                column = jnp.where(below > s, column, 0.0)
            tiles[t] = tiles[t] - column * scaled
    work = jnp.concatenate(tiles, axis=0)
    diag = jnp.sum(jnp.where(lane == line, work, 0.0), axis=1, keepdims=True)
    inverse = jnp.where(lane < total, pltpu.roll(work, total, 1), 0.0) / jnp.sqrt(diag)
    first = jnp.sum(jnp.where(lane < total, inverse * proj, 0.0), axis=1, keepdims=True)
    mean_weights = jnp.sum(inverse * first, axis=0, keepdims=True)
    lower[...] = inverse
    mine = lower[pl.ds(pl.multiple_of(quarter * members, members), members)]
    coef = mean_weights + math.sqrt(total - 1) * mine
    short = lane[0:members]
    coef = jnp.where(short < total, coef, 0.0)
    mixing = coef + (1.0 - jnp.sum(coef, axis=1, keepdims=True)) * (1.0 / total)
    mixing = mixing[:, 0:total]
    high = mixing.astype(BF16)
    low = (mixing - high.astype(F32)).astype(BF16)
    left = jnp.concatenate([high, high, low], axis=1)

    for field in range(3):
        for r in range(rows):
            for k in range(count_mem):
                who = lax.bitwise_xor(quarter, k)
                x = heights[k][r] if field == 0 else winds[k][field - 1, r]
                upper = x.astype(BF16)
                rest = (x - upper.astype(F32)).astype(BF16)
                at = pl.multiple_of(who * members, members)
                stack[r % 2, pl.ds(at, members), :] = upper
                stack[r % 2, pl.ds(at + total, members), :] = rest
                stack[r % 2, pl.ds(at + 2 * total, members), :] = upper
            out[:, field, r, :] = jnp.dot(left, stack[r % 2], preferred_element_type=F32)


def swap(x, axis, bit):
    count = lax.axis_size(axis)
    return lax.ppermute(x, axis, [(i, i ^ bit) for i in range(count)])


def local(state, depth, obs_cells, obs_weights, owner_map, obs_values, obs_precision):
    members, fields, rows, cols = state.shape
    count = lax.axis_size("space")
    count_mem = lax.axis_size("mem")
    place = lax.axis_index("space")
    quarter = lax.axis_index("mem").astype(jnp.int32).reshape(1)
    total = members * count_mem
    blocks, width = obs_cells.shape[1:]
    share = blocks // count_mem
    scale = math.sqrt((total - 1) / (count * blocks * width))

    def rim(at):
        strip = lax.slice_in_dim(state, at, at + RIM, axis=2)
        strip = strip.transpose(1, 0, 2, 3).reshape(fields * members, RIM, cols)
        return jnp.concatenate([strip, depth[None, at : at + RIM]], axis=0)

    ends = count - 1
    above = lax.ppermute(rim(rows - RIM), "space", [(i, i + 1) for i in range(ends)])
    below = lax.ppermute(rim(0), "space", [(i + 1, i) for i in range(ends)])
    inside = jnp.stack([place > 0, place < ends]).astype(F32)
    held = jnp.concatenate([obs_values[0], obs_precision[0]], axis=1)
    got = lax.all_to_all(held, "space", split_axis=0, concat_axis=0, tiled=True)

    height, wind = forecast(inside, state, above, below, depth)
    bits = [1 << i for i in range(count_mem.bit_length() - 1)]
    heights = {0: height}
    winds = {0: wind}
    for bit in reversed(bits):
        for k in list(heights):
            heights[k ^ bit] = swap(heights[k], "mem", bit)
        for k in list(winds):
            winds[k ^ bit] = swap(winds[k], "mem", bit)
    heights = [heights[k] for k in range(count_mem)]
    winds = [winds[k] for k in range(count_mem)]

    spread = total // 4 + 8
    devices = count * count_mem
    sent = pl.pallas_call(
        functools.partial(gram_kernel, scale, count_mem),
        out_shape=jax.ShapeDtypeStruct((devices, spread, 2 * total), F32),
        grid_spec=pltpu.PrefetchScalarGridSpec(
            num_scalar_prefetch=2,
            grid=(1,),
            in_specs=[pl.BlockSpec((rows, members, cols), lambda i, q, o: (0, 0, 0))] * count_mem
            + [pl.BlockSpec((obs_cells.shape[0], share, width), lambda i, q, o: (0, q[0], 0))] * 2
            + [pl.BlockSpec(got.shape, lambda i, q, o: (0, 0, 0))],
            out_specs=pl.BlockSpec((devices, spread, 2 * total), lambda i, q, o: (0, 0, 0)),
            scratch_shapes=[
                pltpu.VMEM((rows * total, 2 * cols), BF16),
                pltpu.VMEM((share, width), F32),
                pltpu.VMEM((share, width), F32),
                pltpu.VMEM((2 * total, share * width), F32),
                pltpu.SMEM((count,), jnp.int32),
            ],
        ),
        compiler_params=pltpu.CompilerParams(vmem_limit_bytes=48 * 1024 * 1024),
        name="gram",
    )(quarter, owner_map[:, 0], *heights, obs_cells, obs_weights, got)
    sums = lax.all_to_all(sent, ("space", "mem"), split_axis=0, concat_axis=0, tiled=True)

    return pl.pallas_call(
        functools.partial(analysis_kernel, count_mem),
        out_shape=jax.ShapeDtypeStruct(state.shape, F32),
        in_specs=[SMEM, VMEM] + [VMEM] * (2 * count_mem),
        out_specs=VMEM,
        scratch_shapes=[
            pltpu.VMEM((total, 2 * total), F32),
            pltpu.VMEM((2, 3 * total, cols), BF16),
        ],
        compiler_params=pltpu.CompilerParams(vmem_limit_bytes=48 * 1024 * 1024),
        name="analysis",
    )(quarter, sums, *heights, *winds)


def solution(mesh):
    return jax.shard_map(
        local,
        mesh=mesh,
        in_specs=(
            P("mem", None, "space", None),
            P("space", None),
            P(None, "space", None),
            P(None, "space", None),
            P("space", None),
            P("space", None, None, None),
            P("space", None, None, None),
        ),
        out_specs=P("mem", None, "space", None),
        check_vma=False,
    )
```

time: 260 us -> 84.5 us (0.33)
  local copies, waits for them, and re-layouts: 118 us -> 4.43 us
  blocking collectives: 40.3 us -> 0 us
  starting transfers between devices: 45.3 us -> 18.8 us
  Pallas kernels: 0 us -> 26.4 us
  other arithmetic: 25.3 us -> 0.83 us
  waiting for transfers between devices: 10.9 us -> 33.5 us
  between operations: 13.8 us -> 0.13 us
  matrix products: 5.47 us -> 0 us
    gather x3 -> x0, local copies, waits for them, and re-layouts: 110 us -> none  [the longest x1 108 us: local(): predicted = jnp.sum(obs_weights[None] * flat[:, obs_cells], axis=1)]
    psum x1 -> x0, blocking collectives: 40.3 us -> none  [local(): gram, proj = lax.psum((gram, proj), ('space', 'mem'))]
    pallas_call x0 -> x3, Pallas kernels: none -> 26.4 us  [the longest x1 14.2 us: local(): pl.pallas_call(functools.partial(gram_kernel, scale, count_mem), out_shap...]
    ppermute x8, starting transfers between devices: 26.5 us -> 8.95 us  [the longest x1 4.99 us: local(): lax.ppermute(rim(rows - RIM), 'space', [(i, i + 1) for i in range(ends)])]
    another operation x7 -> x0, other arithmetic: 12.5 us -> none  [the longest x3 6.6 us: local(): lower = jnp.linalg.cholesky((M - 1) * eye + gram)]
    ppermute x8, waiting for transfers between devices: 3.96 us -> 16.2 us  [the longest x6 9.2 us: swap(): return lax.ppermute(x, axis, [(i, i ^ bit) for i in range(count)])]
    all_to_all x3 -> x2, waiting for transfers between devices: 6.93 us -> 17.3 us  [the longest x1 9.66 us: local(): lax.all_to_all(sent, ('space', 'mem'), split_axis=0, concat_axis=0, tiled...]
    reduce_sum x3 -> x0, other arithmetic: 9.98 us -> none  [the longest x1 9.82 us: local(): predicted = jnp.sum(obs_weights[None] * flat[:, obs_cells], axis=1)]
  transfers between devices with their start and end apart: 12 -> 10, of which waited for: 4 -> 7; matrix products, arithmetic and copies ran while one was open for 55% -> 1% of each run, Pallas kernels for 0% -> 17%
where the time goes in v1:
time: 84.5 us; the launch traced here: 84 us
  waiting for transfers between devices  33.5 us (40%)
  Pallas kernels  26.4 us (31%)
  starting transfers between devices  18.8 us (22%)
  local copies, waits for them, and re-layouts  4.43 us (5%)
    pallas_call x1, Pallas kernels, local(): pl.pallas_call(functools.partial(gram_kernel, scale, count_mem), out_shap...  14.2 us
    pallas_call x1, Pallas kernels, local(): pl.pallas_call(functools.partial(analysis_kernel, count_mem), out_shape=j...  10.7 us
    all_to_all x1, waiting for transfers between devices, local(): lax.all_to_all(sent, ('space', 'mem'), split_axis=0, concat_axis=0, tiled...  9.66 us
    ppermute x6, waiting for transfers between devices, swap(): return lax.ppermute(x, axis, [(i, i ^ bit) for i in range(count)])  9.2 us
    all_to_all x1, waiting for transfers between devices, local(): got = lax.all_to_all(held, 'space', split_axis=0, concat_axis=0, tiled=True)  7.65 us
    all_to_all x1, starting transfers between devices, local(): got = lax.all_to_all(held, 'space', split_axis=0, concat_axis=0, tiled=True)  7.07 us
    ppermute x1, starting transfers between devices, local(): lax.ppermute(rim(rows - RIM), 'space', [(i, i + 1) for i in range(ends)])  4.99 us
    ppermute x1, waiting for transfers between devices, local(): below = lax.ppermute(rim(0), 'space', [(i + 1, i) for i in range(ends)])  4.13 us
  transfers between devices with their start and end apart: 10, of which 7 were waited for; matrix products, arithmetic and copies ran while one was open for 1% of the time, Pallas kernels for 17%

profile of v1, /device:TPU:0, one launch (start us, length us, event | category | flops | bytes accessed | tf_op | source)
XLA Modules:
  0.0 84.0 jit_solution(5844252232804189395)
XLA Ops:
  0.0 0.7 slice_bitcast_fusion.2
  0.7 1.2 %slice_bitcast_fusion = (f32[3,16,4,256]{3,2,0,1:T(4,128)S(1)}, f32[3,16,4,256]{3,2,0,1:T(4,128)S(1)}) fusion(f32[16,3,16,256]{3,2,1,0:T(8,128)} %state.1), kind=kLoop, calls=%fused_computation.2 | loop fusion | bytes 786432 | tf_op jit(solution)/shard_map/transpose | solution.py:281
  1.9 0.0 copy-start
  2.0 5.0 %collective-permute-start = (f32[49,4,256]{2,1,0:T(4,128)S(1)}, f32[49,4,256]{2,1,0:T(4,128)S(1)}, u32[]{:S(2)}, u32[]{:S(2)}) collective-permute-start(f32[49,4,256]{2,1,0:T(4,128)S(1)} %pad_maximum_fusion), channel_id=1, source_target_pairs={{0,4},{4,8},{8,12},{12,16},{16,20},{20,24},{24,28},{1,5},{5,9},{9,... | collective-permute-start | bytes 602120 | tf_op jit(solution)/shard_map/ppermute | solution.py:285
  7.1 0.0 copy-start.5
  7.1 1.3 %collective-permute-start.1 = (f32[49,4,256]{2,1,0:T(4,128)S(1)}, f32[49,4,256]{2,1,0:T(4,128)S(1)}, u32[]{:S(2)}, u32[]{:S(2)}) collective-permute-start(f32[49,4,256]{2,1,0:T(4,128)S(1)} %pad_maximum_fusion.1), channel_id=1, source_target_pairs={{4,0},{8,4},{12,8},{16,12},{20,16},{24,20},{28,24},{5,1},{9,5},{13... | collective-permute-start | bytes 602120 | tf_op jit(solution)/shard_map/ppermute | solution.py:286
  8.4 0.1 add_convert_fusion.inside
  8.5 0.0 copy-start.7
  8.5 0.0 copy-start.8
  8.5 2.8 %collective-permute-done.above = f32[49,4,256]{2,1,0:T(4,128)S(1)} collective-permute-done((f32[49,4,256]{2,1,0:T(4,128)S(1)}, f32[49,4,256]{2,1,0:T(4,128)S(1)}, u32[]{:S(2)}, u32[]{:S(2)}) %collective-permute-start) | collective-permute-done | bytes 200736 | tf_op jit(solution)/shard_map/ppermute | solution.py:285
  11.3 4.1 %collective-permute-done.1.below = f32[49,4,256]{2,1,0:T(4,128)S(1)} collective-permute-done((f32[49,4,256]{2,1,0:T(4,128)S(1)}, f32[49,4,256]{2,1,0:T(4,128)S(1)}, u32[]{:S(2)}, u32[]{:S(2)}) %collective-permute-start.1) | collective-permute-done | bytes 200736 | tf_op jit(solution)/shard_map/ppermute | solution.py:286
  15.4 0.0 copy-done
  15.4 0.0 copy-done.5
  15.4 1.5 %forecast.1 = (f32[16,16,256]{2,1,0:T(8,128)S(1)}, f32[2,16,16,256]{3,2,1,0:T(8,128)S(1)}) custom-call(f32[2]{0:T(128)S(1)} %add_convert_fusion.inside, f32[16,3,16,256]{3,2,1,0:T(8,128)S(1)} %copy-done, f32[49,4,256]{2,1,0:T(4,128)S(1)} %collective-permute-done.above, f32[49,4,256]{2,1,0:T(4,128)S(1)} %collective-permute-done.1.below, f32[16,256]{1,0:T(8,128)S(1)} %copy-done.5), custom_call_target="tpu_custom_call" | custom-call | tf_op jit(solution)/shard_map/forecast/pallas_call | solution.py:68
  16.9 1.6 %collective-permute-start.3 = (f32[16,16,256]{2,1,0:T(8,128)S(1)}, f32[16,16,256]{2,1,0:T(8,128)S(1)}, u32[]{:S(2)}, u32[]{:S(2)}) collective-permute-start(f32[16,16,256]{2,1,0:T(8,128)S(1)} %get-tuple-element.7.refs_0_), channel_id=1, source_target_pairs={{0,2},{1,3},{2,0},{3,1},{4,6},{5,7},{6,4},{7,5},{8,10},{9,11},{10,... | collective-permute-start | bytes 786440 | tf_op jit(solution)/shard_map/ppermute | solution.py:265
  18.5 0.0 collective-permute-start.2
  18.5 0.5 collective-permute-start.6
  19.0 7.0 %collective-permute-done.3.refs_2_ = f32[16,16,256]{2,1,0:T(8,128)S(1)} collective-permute-done((f32[16,16,256]{2,1,0:T(8,128)S(1)}, f32[16,16,256]{2,1,0:T(8,128)S(1)}, u32[]{:S(2)}, u32[]{:S(2)}) %collective-permute-start.3) | collective-permute-done | bytes 262176 | tf_op jit(solution)/shard_map/ppermute | solution.py:265
  26.0 0.0 collective-permute-start.4
  26.1 0.0 copy-done.7
  26.1 0.0 copy-done.8
  26.1 0.7 pad_maximum_fusion.2
  26.7 0.0 copy-start.3
  26.7 0.0 copy-start.4
  26.7 7.1 %all-to-all-start = ((f32[8,32,128]{2,1,0:T(8,128)}), f32[8,32,128]{2,1,0:T(8,128)S(1)}, u32[]{:S(2)}, u32[]{:S(2)}) async-start(f32[8,32,128]{2,1,0:T(8,128)} %pad_maximum_fusion.2), calls=%async_computation | async-start | bytes 262144 | tf_op jit(solution)/shard_map/all_to_all | solution.py:289
  33.8 7.7 %all-to-all-done.refs_6_ = f32[8,32,128]{2,1,0:T(8,128)S(1)} async-done(((f32[8,32,128]{2,1,0:T(8,128)}), f32[8,32,128]{2,1,0:T(8,128)S(1)}, u32[]{:S(2)}, u32[]{:S(2)}) %all-to-all-start) | async-done | bytes 131104 | tf_op jit(solution)/shard_map/all_to_all | solution.py:289
  41.5 0.0 collective-permute-done.2.refs_1_
  41.5 0.0 collective-permute-done.4.refs_3_
  41.5 0.0 copy-start.6
  41.5 0.0 copy-done.3
  41.5 0.0 copy-done.4
  41.5 0.6 copy-done.6
  42.1 14.2 %gram.1 = f32[32,24,128]{2,1,0:T(8,128)} custom-call(s32[1]{0:T(128)} %bitcast.place, s32[64]{0:T(128)S(1)} %bitcast.16, f32[16,16,256]{2,1,0:T(8,128)S(1)} %get-tuple-element.7.refs_0_, f32[16,16,256]{2,1,0:T(8,128)S(1)} %collective-permute-done.2.refs_1_, f32[16,16,256]{2,1,0:T(8,128)S(1)} %collective-permute-done.3.refs_2_, ...), custom_call_target="tpu_custom_call" | custom-call | tf_op jit(solution)/shard_map/gram/pallas_call | solution.py:305
  56.3 2.8 %all-to-all-start.1 = ((f32[32,24,128]{2,1,0:T(8,128)}), f32[32,24,128]{2,1,0:T(8,128)S(1)}, u32[]{:S(2)}, u32[]{:S(2)}) async-start(f32[32,24,128]{2,1,0:T(8,128)} %gram.1), calls=%async_computation.1 | async-start | bytes 786432 | tf_op jit(solution)/shard_map/all_to_all | solution.py:326
  59.1 0.3 collective-permute-start.5
  59.4 0.0 collective-permute-done.6.refs_6_
  59.4 0.3 collective-permute-start.7
  59.7 1.4 %collective-permute-done.5.refs_5_ = f32[2,16,16,256]{3,2,1,0:T(8,128)S(1)} collective-permute-done((f32[2,16,16,256]{3,2,1,0:T(8,128)S(1)}, f32[2,16,16,256]{3,2,1,0:T(8,128)S(1)}, u32[]{:S(2)}, u32[]{:S(2)}) %collective-permute-start.5) | collective-permute-done | bytes 524320 | tf_op jit(solution)/shard_map/ppermute | solution.py:265
  61.1 0.7 collective-permute-done.7.refs_7_
  61.8 0.0 copy-start.1
  61.8 0.8 copy-done.1
  62.6 9.7 %all-to-all-done.1.sums = f32[32,24,128]{2,1,0:T(8,128)S(1)} async-done(((f32[32,24,128]{2,1,0:T(8,128)}), f32[32,24,128]{2,1,0:T(8,128)S(1)}, u32[]{:S(2)}, u32[]{:S(2)}) %all-to-all-start.1) | async-done | bytes 393248 | tf_op jit(solution)/shard_map/all_to_all | solution.py:326
  72.3 0.0 copy-start.2
  72.3 1.0 %copy-done.2 = f32[2,16,16,256]{3,2,1,0:T(8,128)S(1)} copy-done((f32[2,16,16,256]{3,2,1,0:T(8,128)S(1)}, f32[2,16,16,256]{3,2,1,0:T(8,128)}, u32[]{:S(2)}) %copy-start.2) | copy-done | bytes 524312
  73.3 10.7 %analysis.1 = f32[16,3,16,256]{3,2,1,0:T(8,128)} custom-call(s32[1]{0:T(128)} %bitcast.place, f32[32,24,128]{2,1,0:T(8,128)S(1)} %all-to-all-done.1.sums, f32[16,16,256]{2,1,0:T(8,128)S(1)} %get-tuple-element.7.refs_0_, f32[16,16,256]{2,1,0:T(8,128)S(1)} %collective-permute-done.2.refs_1_, f32[16,16,256]{2,1,0:T(8,128)S(1)} %collective-permute-done.3.refs_2_, ...), custom_call_target="tpu_custom_call" | custom-call | tf_op jit(solution)/shard_map/analysis/pallas_call | solution.py:328
  (4 shorter events, 0.1 us)
Async XLA Ops:
  1.9 13.5 %copy-start = (f32[16,3,16,256]{3,2,1,0:T(8,128)S(1)}, f32[16,3,16,256]{3,2,1,0:T(8,128)}, u32[]{:S(2)}) copy-start(f32[16,3,16,256]{3,2,1,0:T(8,128)} %state.1) | copy-start | bytes 2359300
  2.0 9.3 %collective-permute-start = (f32[49,4,256]{2,1,0:T(4,128)S(1)}, f32[49,4,256]{2,1,0:T(4,128)S(1)}, u32[]{:S(2)}, u32[]{:S(2)}) collective-permute-start(f32[49,4,256]{2,1,0:T(4,128)S(1)} %pad_maximum_fusion), channel_id=1, source_target_pairs={{0,4},{4,8},{8,12},{12,16},{16,20},{20,24},{24,28},{1,5},{5,9},{9,... | collective-permute-start | bytes 602120 | tf_op jit(solution)/shard_map/ppermute | solution.py:285
  7.1 8.4 %copy-start.5 = (f32[16,256]{1,0:T(8,128)S(1)}, f32[16,256]{1,0:T(8,128)}, u32[]{:S(2)}) copy-start(f32[16,256]{1,0:T(8,128)} %depth.1) | copy-start | bytes 49156
  7.1 8.3 %collective-permute-start.1 = (f32[49,4,256]{2,1,0:T(4,128)S(1)}, f32[49,4,256]{2,1,0:T(4,128)S(1)}, u32[]{:S(2)}, u32[]{:S(2)}) collective-permute-start(f32[49,4,256]{2,1,0:T(4,128)S(1)} %pad_maximum_fusion.1), channel_id=1, source_target_pairs={{4,0},{8,4},{12,8},{16,12},{20,16},{24,20},{28,24},{5,1},{9,5},{13... | collective-permute-start | bytes 602120 | tf_op jit(solution)/shard_map/ppermute | solution.py:286
  8.5 17.6 %copy-start.7 = (f32[1,8,16,128]{3,2,1,0:T(8,128)S(1)}, f32[1,8,16,128]{3,2,1,0:T(8,128)}, u32[]{:S(2)}) copy-start(f32[1,8,16,128]{3,2,1,0:T(8,128)} %param.13) | copy-start | bytes 196612
  8.5 17.6 %copy-start.8 = (f32[1,8,16,128]{3,2,1,0:T(8,128)S(1)}, f32[1,8,16,128]{3,2,1,0:T(8,128)}, u32[]{:S(2)}) copy-start(f32[1,8,16,128]{3,2,1,0:T(8,128)} %param.12) | copy-start | bytes 196612
  16.9 9.1 %collective-permute-start.3 = (f32[16,16,256]{2,1,0:T(8,128)S(1)}, f32[16,16,256]{2,1,0:T(8,128)S(1)}, u32[]{:S(2)}, u32[]{:S(2)}) collective-permute-start(f32[16,16,256]{2,1,0:T(8,128)S(1)} %get-tuple-element.7.refs_0_), channel_id=1, source_target_pairs={{0,2},{1,3},{2,0},{3,1},{4,6},{5,7},{6,4},{7,5},{8,10},{9,11},{10,... | collective-permute-start | bytes 786440 | tf_op jit(solution)/shard_map/ppermute | solution.py:265
  18.5 23.0 %collective-permute-start.2 = (f32[16,16,256]{2,1,0:T(8,128)S(1)}, f32[16,16,256]{2,1,0:T(8,128)S(1)}, u32[]{:S(2)}, u32[]{:S(2)}) collective-permute-start(f32[16,16,256]{2,1,0:T(8,128)S(1)} %get-tuple-element.7.refs_0_), channel_id=1, source_target_pairs={{0,1},{1,0},{2,3},{3,2},{4,5},{5,4},{6,7},{7,6},{8,9},{9,8},{10,11... | collective-permute-start | bytes 786440 | tf_op jit(solution)/shard_map/ppermute | solution.py:265
  18.5 40.9 %collective-permute-start.6 = (f32[2,16,16,256]{3,2,1,0:T(8,128)S(1)}, f32[2,16,16,256]{3,2,1,0:T(8,128)S(1)}, u32[]{:S(2)}, u32[]{:S(2)}) collective-permute-start(f32[2,16,16,256]{3,2,1,0:T(8,128)S(1)} %get-tuple-element.8.refs_4_), channel_id=1, source_target_pairs={{0,2},{1,3},{2,0},{3,1},{4,6},{5,7},{6,4},{7,5},{8,10},{9,11},{10,... | collective-permute-start | bytes 1572872 | tf_op jit(solution)/shard_map/ppermute | solution.py:265
  26.0 15.4 %collective-permute-start.4 = (f32[16,16,256]{2,1,0:T(8,128)S(1)}, f32[16,16,256]{2,1,0:T(8,128)S(1)}, u32[]{:S(2)}, u32[]{:S(2)}) collective-permute-start(f32[16,16,256]{2,1,0:T(8,128)S(1)} %collective-permute-done.3.refs_2_), channel_id=1, source_target_pairs={{0,1},{1,0},{2,3},{3,2},{4,5},{5,4},{6,7},{7,6},{8,9},{9,8},{10,11... | collective-permute-start | bytes 786440 | tf_op jit(solution)/shard_map/ppermute | solution.py:265
  26.7 14.7 %copy-start.3 = (s32[4,64,128]{2,1,0:T(8,128)S(1)}, s32[4,64,128]{2,1,0:T(8,128)}, u32[]{:S(2)}) copy-start(s32[4,64,128]{2,1,0:T(8,128)} %refs_4_.1) | copy-start | bytes 393220
  26.7 14.8 %copy-start.4 = (f32[4,64,128]{2,1,0:T(8,128)S(1)}, f32[4,64,128]{2,1,0:T(8,128)}, u32[]{:S(2)}) copy-start(f32[4,64,128]{2,1,0:T(8,128)} %refs_5_.1) | copy-start | bytes 393220
  26.7 14.7 %all-to-all-start = ((f32[8,32,128]{2,1,0:T(8,128)}), f32[8,32,128]{2,1,0:T(8,128)S(1)}, u32[]{:S(2)}, u32[]{:S(2)}) async-start(f32[8,32,128]{2,1,0:T(8,128)} %pad_maximum_fusion.2), calls=%async_computation | async-start | bytes 262144 | tf_op jit(solution)/shard_map/all_to_all | solution.py:289
  41.5 0.7 copy-start.6
  56.3 15.9 %all-to-all-start.1 = ((f32[32,24,128]{2,1,0:T(8,128)}), f32[32,24,128]{2,1,0:T(8,128)S(1)}, u32[]{:S(2)}, u32[]{:S(2)}) async-start(f32[32,24,128]{2,1,0:T(8,128)} %gram.1), calls=%async_computation.1 | async-start | bytes 786432 | tf_op jit(solution)/shard_map/all_to_all | solution.py:326
  59.1 2.0 %collective-permute-start.5 = (f32[2,16,16,256]{3,2,1,0:T(8,128)S(1)}, f32[2,16,16,256]{3,2,1,0:T(8,128)S(1)}, u32[]{:S(2)}, u32[]{:S(2)}) collective-permute-start(f32[2,16,16,256]{3,2,1,0:T(8,128)S(1)} %get-tuple-element.8.refs_4_), channel_id=1, source_target_pairs={{0,1},{1,0},{2,3},{3,2},{4,5},{5,4},{6,7},{7,6},{8,9},{9,8},{10,11... | collective-permute-start | bytes 1572872 | tf_op jit(solution)/shard_map/ppermute | solution.py:265
  59.4 2.4 %collective-permute-start.7 = (f32[2,16,16,256]{3,2,1,0:T(8,128)S(1)}, f32[2,16,16,256]{3,2,1,0:T(8,128)S(1)}, u32[]{:S(2)}, u32[]{:S(2)}) collective-permute-start(f32[2,16,16,256]{3,2,1,0:T(8,128)S(1)} %collective-permute-done.6.refs_6_), channel_id=1, source_target_pairs={{0,1},{1,0},{2,3},{3,2},{4,5},{5,4},{6,7},{7,6},{8,9},{9,8},{10,11... | collective-permute-start | bytes 1572872 | tf_op jit(solution)/shard_map/ppermute | solution.py:265
  61.8 0.8 copy-start.1
  72.3 1.0 %copy-start.2 = (f32[2,16,16,256]{3,2,1,0:T(8,128)S(1)}, f32[2,16,16,256]{3,2,1,0:T(8,128)}, u32[]{:S(2)}) copy-start(f32[2,16,16,256]{3,2,1,0:T(8,128)} %copy-done.1) | copy-start | bytes 1572868

commit v2 on v1

v2 whole, which is shorter than its diff:
```python
import functools
import math

import jax
import jax.numpy as jnp
from jax import lax
from jax.experimental import pallas as pl
from jax.experimental.pallas import tpu as pltpu
from jax.sharding import PartitionSpec as P

mass_rate = 0.2
wave_rate = 0.2
turn_rate = 0.1

VMEM = pl.BlockSpec(memory_space=pltpu.VMEM)
SMEM = pl.BlockSpec(memory_space=pltpu.SMEM)
F32 = jnp.float32
BF16 = jnp.bfloat16


def diff_cols(field):
    width = field.shape[-1]
    return pltpu.roll(field, width - 1, 1) - pltpu.roll(field, 1, 1)


def edge_kernel(peers, state, depth, values, precision, above, below, *held):
    members, _, rows, cols = state.shape
    width = values.shape[-1]
    for out, sign, at in ((above, 1.0, range(4)), (below, -1.0, range(rows - 1, rows - 5, -1))):
        deep = [jnp.broadcast_to(depth[t : t + 1], (members, cols)) for t in at]
        h = [state[:, 0, t, :] for t in at]
        u = [state[:, 1, t, :] for t in at]
        v = [state[:, 2, t, :] for t in at]
        flux = [d * e for d, e in zip(deep, u)]
        first = h[0] - mass_rate * (sign * flux[1] + diff_cols(deep[0] * v[0]))
        second, third = (
            h[i] - mass_rate * (sign * (flux[i + 1] - flux[i - 1]) + diff_cols(deep[i] * v[i]))
            for i in (1, 2)
        )
        east = u[0] - wave_rate * sign * second + turn_rate * v[0]
        east_next = u[1] - wave_rate * sign * third + turn_rate * v[1]
        north = v[0] - turn_rate * u[0] - wave_rate * diff_cols(first)
        twice = first - mass_rate * (
            sign * deep[1] * (east_next + sign * wave_rate * first) + diff_cols(deep[0] * north)
        )
        for i, part in enumerate((flux[0], first, east, twice)):
            out[i * members : (i + 1) * members] = part
        out[4 * members : 4 * members + 8] = jnp.concatenate(
            [deep[0][0:1], deep[1][0:1], jnp.zeros((6, cols), F32)], axis=0
        )
    for j, out in enumerate(held):
        peer = lax.bitwise_xor(lax.axis_index("space"), peers * lax.axis_index("mem") + j)
        out[:, 0:width] = values[0, peer]
        out[:, width : 2 * width] = precision[0, peer]


def edges(peers, state, depth, values, precision):
    members, _, _, cols = state.shape
    rim = jax.ShapeDtypeStruct((4 * members + 8, cols), F32)
    held = jax.ShapeDtypeStruct((values.shape[2], cols), F32)
    return pl.pallas_call(
        functools.partial(edge_kernel, peers),
        out_shape=(rim, rim) + (held,) * peers,
        in_specs=[VMEM] * 4,
        out_specs=(VMEM,) * (2 + peers),
        name="edges",
    )(state, depth, values, precision)


def forecast_kernel(last, state, depth, above, below, *refs):
    held = refs[:-6]
    height_out, wind_out, h, u, v, flux = refs[-6:]
    members, _, rows, cols = state.shape
    slots = held[0].shape[0]
    deep = [jnp.broadcast_to(depth[t : t + 1], (members, cols)) for t in range(rows)]
    sides = []
    place = lax.axis_index("space")
    for ref, sign, edge, inside in (
        (above, -1.0, 0, place > 0),
        (below, 1.0, rows - 1, place < last),
    ):
        parts = [ref[i * members : (i + 1) * members] for i in range(4)]
        deeps = [
            jnp.broadcast_to(ref[4 * members + i : 4 * members + i + 1], (members, cols))
            for i in range(2)
        ]
        sides.append((parts, deeps, sign, edge, inside.astype(F32)))

    def outer(edge):
        return 0 if edge == 0 else rows + 1

    for t in range(rows):
        h[t + 1] = state[:, 0, t, :]
        u[t] = state[:, 1, t, :]
        v[t] = state[:, 2, t, :]
        flux[t + 1] = deep[t] * u[t]
    deltas = []
    for (first_flux, _, _, _), _, sign, edge, _ in sides:
        deltas.append(sign * mass_rate * flux[edge + 1])
        flux[outer(edge)] = first_flux

    def new_heights():
        for t in range(rows):
            h[t + 1] = h[t + 1] - mass_rate * (flux[t + 2] - flux[t] + diff_cols(deep[t] * v[t]))

    def new_winds(put):
        for t in range(rows):
            east, north = u[t], v[t]
            put(
                t,
                east - wave_rate * (h[t + 2] - h[t]) + turn_rate * north,
                north - wave_rate * diff_cols(h[t + 1]) - turn_rate * east,
            )

    def keep(t, east, north):
        u[t], v[t] = east, north
        flux[t + 1] = deep[t] * east

    def emit(t, east, north):
        wind_out[0, t] = east
        wind_out[1, t] = north

    new_heights()
    for delta, ((_, first, east, _), deeps, sign, edge, inside) in zip(deltas, sides):
        h[outer(edge)] = (first + delta) * inside
        flux[outer(edge)] = deeps[0] * (east + sign * wave_rate * h[edge + 1])
    new_winds(keep)
    rims = []
    for delta, ((_, _, _, twice), deeps, sign, edge, inside) in zip(deltas, sides):
        turned = wave_rate * diff_cols(deeps[0] * diff_cols(delta))
        change = wave_rate * deeps[1] * delta - sign * flux[edge + 1] - turned
        rims.append((edge, (twice + delta - mass_rate * change) * inside))
    new_heights()
    for edge, rim in rims:
        h[outer(edge)] = rim
    new_winds(emit)
    for t in range(rows):
        height_out[t] = h[t + 1]
    for j, piece in enumerate(held):
        at = j * slots
        height_out[rows + at // members, at % members : at % members + slots, :] = piece[...]


def forecast(last, state, depth, above, below, held):
    members, _, rows, cols = state.shape
    extra = -(-len(held) * held[0].shape[0] // members)
    return pl.pallas_call(
        functools.partial(forecast_kernel, last),
        out_shape=(
            jax.ShapeDtypeStruct((rows + extra, members, cols), F32),
            jax.ShapeDtypeStruct((2, rows, members, cols), F32),
        ),
        in_specs=[VMEM] * (4 + len(held)),
        out_specs=(VMEM, VMEM),
        scratch_shapes=[
            pltpu.VMEM((rows + 2, members, cols), F32),
            pltpu.VMEM((rows, members, cols), F32),
            pltpu.VMEM((rows, members, cols), F32),
            pltpu.VMEM((rows + 2, members, cols), F32),
        ],
        compiler_params=pltpu.CompilerParams(vmem_limit_bytes=32 * 1024 * 1024),
        name="forecast",
    )(state, depth, above, below, *held)


def interpolate(pieces, cells, weights, split, put):
    rows = split.shape[0] // (len(pieces) * pieces[0].shape[1])
    _, members, cols = pieces[0].shape
    total = members * len(pieces)
    points, blocks, width = cells.shape
    quarter = lax.axis_index("mem")
    blocks = blocks // lax.axis_size("mem")
    for k, piece in enumerate(pieces):
        who = lax.bitwise_xor(lax.rem(quarter, len(pieces)), k)
        for r in range(rows):
            x = piece[r]
            high = x.astype(BF16)
            low = (x - high.astype(F32)).astype(BF16)
            at = pl.ds(pl.multiple_of(r * total + who * members, members), members)
            split[at, 0:cols] = high
            split[at, cols : 2 * cols] = low

    def block(b, carry):
        result = None
        line = pl.ds(quarter * blocks + b, 1)
        for half in range(points // 2):
            cell = jnp.concatenate(
                [cells[2 * half, line, :], cells[2 * half + 1, line, :]], axis=1
            )
            share = jnp.concatenate(
                [weights[2 * half, line, :], weights[2 * half + 1, line, :]], axis=1
            )
            row = cell // cols
            col = jnp.broadcast_to(cell - row * cols, (cols, 2 * width))
            here = lax.broadcasted_iota(jnp.int32, (cols, 2 * width), 0) == col
            pick = jnp.where(here, 1.0, 0.0).astype(BF16)
            lines = jnp.dot(
                split[...], jnp.concatenate([pick, pick], axis=0), preferred_element_type=F32
            )
            for r in range(rows):
                term = lines[r * total : (r + 1) * total] * jnp.where(row == r, share, 0.0)
                term = term[:, :width] + term[:, width:]
                result = term if result is None else result + term
        put(b, result)
        return carry

    lax.fori_loop(0, blocks, block, 0, unroll=2)


def predict_kernel(count, *refs):
    pieces = refs[:count]
    cells, weights, out, split = refs[count:]

    def put(b, result):
        out[b] = result

    interpolate(pieces, cells, weights, split, put)


def gram_kernel(scale, count, count_mem, owners, *refs):
    pieces = refs[:count_mem]
    early = refs[count_mem : count_mem + count_mem // count - 1]
    cells, weights, out, split, got, seen, factor, lined, used = refs[-9:]
    _, members, cols = pieces[0].shape
    total = members * count_mem
    part = members * count
    rows = split.shape[0] // part
    all_blocks = owners.shape[0]
    blocks, width = all_blocks // count_mem, cells.shape[2]
    slots = got.shape[1]
    peers = got.shape[0] // count_mem
    space, quarter = lax.axis_index("space"), lax.axis_index("mem")

    for owner in range(got.shape[0]):
        used[owner] = 0
    for k, piece in enumerate(pieces):
        who = lax.bitwise_xor(quarter, k)
        for j in range(peers):
            at = j * slots
            got[who * peers + j] = piece[
                rows + at // members, at % members : at % members + slots, :
            ]

    def dispatch(b, carry):
        owner = owners[b]
        slot = used[owner]
        used[owner] = slot + 1
        at = b - quarter * blocks

        @pl.when((at >= 0) & (at < blocks))
        def _():
            line = got[lax.bitwise_xor(owner, space), pl.ds(slot, 1)]
            seen[pl.ds(at, 1)] = line[:, 0:width]
            factor[pl.ds(at, 1)] = line[:, width : 2 * width] * scale

        return carry

    lax.fori_loop(0, all_blocks, dispatch, 0)

    mine = quarter // count
    groups = count_mem // count
    for g in range(groups - 1):
        base = pl.multiple_of(lax.bitwise_xor(mine, g) * part, part)
        for b in range(blocks):
            lined[pl.ds(base, part), b * width : (b + 1) * width] = early[g][b]
    final = pl.multiple_of(lax.bitwise_xor(mine, groups - 1) * part, part)

    def put(b, result):
        at = pl.ds(pl.multiple_of(b * width, width), width)
        lined[pl.ds(final, part), at] = result

    interpolate(pieces[count_mem - count :], cells, weights, split, put)
    lined[total : 2 * total] = jnp.zeros((total, blocks * width), F32)
    for b in range(blocks):
        at = pl.ds(b * width, width)
        values = lined[0:total, at]
        much = factor[b : b + 1]
        middle = jnp.sum(values, axis=0, keepdims=True) * (1.0 / total)
        lined[0:total, at] = (values - middle) * much
        lined[total : total + 1, at] = (seen[b : b + 1] - middle) * much

    x = lined[...]
    gram = lax.dot_general(
        x, x, (((1,), (1,)), ((), ())), precision=lax.Precision.HIGHEST, preferred_element_type=F32
    )
    packed = pack_gram(gram, total)
    spread = out.shape[1]
    for d in range(out.shape[0]):
        for r in range(spread):
            out[d, r] = packed[r : r + 1]


def pack_gram(gram, total):
    half, quarter = total // 2, total // 4
    span = 2 * total
    top, low = gram[0:half], gram[half:total]
    lane = lax.broadcasted_iota(jnp.int32, (half, span), 1)
    line = lax.broadcasted_iota(jnp.int32, (half, span), 0)
    both = jnp.where(lane <= line, top, pltpu.roll(low, span - half, 1))
    wide = jnp.where(lane < half, both, pltpu.roll(low, half, 1))
    lane_q = lane[0:quarter]
    body = jnp.where(lane_q < total, wide[0:quarter], pltpu.roll(wide[quarter:half], total, 1))
    diag = jnp.sum(jnp.where(lane == line + half, low, 0.0), axis=0, keepdims=True)
    lane_1 = lane[0:8]
    tail = jnp.where(
        lane_1 < total, gram[total : total + 8], pltpu.roll(jnp.broadcast_to(diag, (8, span)), half, 1)
    )
    return jnp.concatenate([body, tail], axis=0)


def unpack_gram(packed, total):
    half, quarter = total // 2, total // 4
    span = 2 * total
    body, tail = packed[0:quarter], packed[quarter : quarter + 1]
    wide = jnp.concatenate([body, pltpu.roll(body, total, 1)], axis=0)
    low = pltpu.roll(wide, span - half, 1)
    lane = lax.broadcasted_iota(jnp.int32, (half, span), 1)
    line = lax.broadcasted_iota(jnp.int32, (half, span), 0)
    first = lane < half
    stacked = jnp.concatenate(
        [jnp.where(first, wide, 0.0), jnp.where(first, low, 0.0), jnp.zeros((total, span), F32)], axis=0
    )
    turned = stacked.T[0:half]
    top = jnp.where(first & (lane <= line), wide, turned)
    diag = pltpu.roll(jnp.broadcast_to(tail, (half, span)), span - half, 1)
    corner = jnp.where(lane > line, wide, turned)
    corner = pltpu.roll(jnp.where(first, corner, 0.0), half, 1)
    corner = jnp.where(lane == line + half, diag, corner)
    bottom = jnp.where(first, low, corner)
    return jnp.concatenate([top, bottom], axis=0), tail


def factor_inverse(system, total):
    span = 2 * total
    lane = lax.broadcasted_iota(jnp.int32, (total, span), 1)
    line = lax.broadcasted_iota(jnp.int32, (total, span), 0)
    work = jnp.where(lane < total, system, jnp.where(lane == line + total, 1.0, 0.0))
    tiles = [work[8 * g : 8 * g + 8] for g in range(total // 8)]
    step = 4
    below = lax.broadcasted_iota(jnp.int32, (8, span), 0)

    def lanes(x, k):
        return jnp.broadcast_to(x[:, k : k + 1], (8, span))

    def lines(x, s):
        return jnp.broadcast_to(x[s : s + 1], (8, span))

    for k in range(0, total, step):
        g, s = k // 8, k % 8
        columns = {t: [lanes(tiles[t], k + i) for i in range(step)] for t in range(g, total // 8)}
        pivots = [lines(tiles[g], s + i) for i in range(step)]
        block = [[lines(columns[g][j], s + i) for j in range(i + 1)] for i in range(step)]
        for j in range(step):
            scale = 1.0 / block[j][j]
            ratio = [None] * step
            for i in range(j + 1, step):
                ratio[i] = block[i][j] * scale
            for i in range(j + 1, step):
                for n in range(j + 1, i + 1):
                    block[i][n] = block[i][n] - ratio[i] * block[n][j]
                pivots[i] = pivots[i] - ratio[i] * pivots[j]
            scaled = pivots[j] * scale
            for t in columns:
                for i in range(j + 1, step):
                    columns[t][i] = columns[t][i] - ratio[i] * columns[t][j]
            for t in columns:
                column = columns[t][j]
                if t == g:
                    if s + j == 7:
                        continue
                    column = jnp.where(below > s + j, column, 0.0)
                tiles[t] = tiles[t] - column * scaled
    work = jnp.concatenate(tiles, axis=0)
    diag = jnp.sum(jnp.where(lane == line, work, 0.0), axis=1, keepdims=True)
    return jnp.where(lane < total, pltpu.roll(work, total, 1), 0.0) / jnp.sqrt(diag)


def mixing_columns(packed, total, members, count_mem, lower):
    span = 2 * total
    quarter = lax.axis_index("mem")
    system, proj = unpack_gram(packed, total)
    lane = lax.broadcasted_iota(jnp.int32, (total, span), 1)
    line = lax.broadcasted_iota(jnp.int32, (total, span), 0)
    inverse = factor_inverse(system + jnp.where(lane == line, float(total - 1), 0.0), total)
    first = jnp.sum(jnp.where(lane < total, inverse * proj, 0.0), axis=1, keepdims=True)
    mean_weights = jnp.sum(inverse * first, axis=0, keepdims=True)
    lower[...] = inverse
    mine = lower[pl.ds(pl.multiple_of(quarter * members, members), members)]
    coef = mean_weights + math.sqrt(total - 1) * mine
    short = lane[0:members]
    coef = jnp.where(short < total, coef, 0.0)
    mixing = coef + (1.0 - jnp.sum(coef, axis=1, keepdims=True)) * (1.0 / total)
    bit = 1
    while bit < count_mem:
        size = bit * members
        turned = jnp.where(
            lax.rem(short // size, 2) == 0, pltpu.roll(mixing, span - size, 1), pltpu.roll(mixing, size, 1)
        )
        swapped = (lax.rem(quarter // bit, 2) == 1).astype(F32)
        mixing = mixing + swapped * (turned - mixing)
        bit *= 2
    return mixing[:, 0:total]


def analysis_kernel(count_mem, sums, *refs):
    heights = refs[:count_mem]
    winds = refs[count_mem : 2 * count_mem]
    out, lower = refs[2 * count_mem :]
    _, members, cols = heights[0].shape
    rows = winds[0].shape[1]
    total = members * count_mem

    packed = sums[0]
    for d in range(1, sums.shape[0]):
        packed = packed + sums[d]
    packed = jnp.concatenate([packed[r] for r in range(packed.shape[0])], axis=0)
    mixing = mixing_columns(packed, total, members, count_mem, lower)
    high = mixing.astype(BF16)
    low = (mixing - high.astype(F32)).astype(BF16)
    left = jnp.concatenate([high, high, low], axis=1)
    for field in range(3):
        for r in range(rows):
            pieces = [heights[k][r] if field == 0 else winds[k][field - 1, r] for k in range(count_mem)]
            upper = [x.astype(BF16) for x in pieces]
            rest = [(x - y.astype(F32)).astype(BF16) for x, y in zip(pieces, upper)]
            stack = jnp.concatenate(upper + rest + upper, axis=0)
            out[:, field, r, :] = jnp.dot(left, stack, preferred_element_type=F32)


def swap(x, axis, bit):
    count = lax.axis_size(axis)
    return lax.ppermute(x, axis, [(i, i ^ bit) for i in range(count)])


def after(x, *others):
    return lax.optimization_barrier((x,) + others)[0]


def cost(flops, size):
    return pl.CostEstimate(flops=flops, bytes_accessed=size, transcendentals=0)


def local(state, depth, obs_cells, obs_weights, owner_map, obs_values, obs_precision):
    members, fields, rows, cols = state.shape
    count = lax.axis_size("space")
    count_mem = lax.axis_size("mem")
    total = members * count_mem
    blocks, width = obs_cells.shape[1:]
    share = blocks // count_mem
    peers = count // count_mem
    scale = math.sqrt((total - 1) / (count * blocks * width))

    to_above, to_below, *held = edges(peers, state, depth, obs_values, obs_precision)
    ends = count - 1
    below = lax.ppermute(to_above, "space", [(i + 1, i) for i in range(ends)])
    above = lax.ppermute(to_below, "space", [(i, i + 1) for i in range(ends)])
    held = [
        lax.ppermute(
            piece,
            ("space", "mem"),
            [
                (s * count_mem + q, (s ^ (peers * q + j)) * count_mem + q)
                for s in range(count)
                for q in range(count_mem)
            ],
        )
        for j, piece in enumerate(held)
    ]
    height, wind = forecast(ends, state, depth, above, below, held)

    group = 2
    early_shape = (share, group * members, width)
    split = pltpu.VMEM((rows * group * members, 2 * cols), BF16)
    params = pltpu.CompilerParams(vmem_limit_bytes=20 * 1024 * 1024)
    flops = 4 * obs_cells.shape[0] * share * width * rows * members * group * cols

    def predict(k):
        return pl.pallas_call(
            functools.partial(predict_kernel, group),
            out_shape=jax.ShapeDtypeStruct(early_shape, F32),
            in_specs=[VMEM] * (group + 2),
            out_specs=VMEM,
            scratch_shapes=[split],
            compiler_params=params,
            cost_estimate=cost(flops, 4 * height.size * group),
            name="predict",
        )(*[heights[i] for i in range(k, k + group)], obs_cells, obs_weights)

    heights = {0: height}
    winds = {0: wind}
    far = [1 << i for i in range(1, count_mem.bit_length() - 1)]
    for bit in far:
        heights[bit] = swap(height, "mem", bit)
    heights[1] = swap(height, "mem", 1)
    early = [predict(0)]
    for bit in far:
        heights[bit] = after(heights[bit], early[0])
        for k in range(1, bit):
            heights[bit + k] = swap(heights[bit], "mem", k) if k == 1 else swap(heights[bit + 1], "mem", k - 1)
    for bit in far:
        winds[bit] = swap(after(wind, heights[bit]), "mem", bit)
    winds[1] = swap(wind, "mem", 1)
    for bit in far:
        for k in range(1, bit):
            winds[bit + k] = swap(winds[bit], "mem", k) if k == 1 else swap(winds[bit + 1], "mem", k - 1)
    early += [predict(k) for k in range(group, count_mem - group, group)]
    heights = [heights[k] for k in range(count_mem)]
    winds = [winds[k] for k in range(count_mem)]

    owners = owner_map[:, 0]
    spread = total // 4 + 1
    devices = count * count_mem
    sent = pl.pallas_call(
        functools.partial(gram_kernel, scale, group, count_mem),
        out_shape=jax.ShapeDtypeStruct((devices, spread, 1, 2 * total), F32),
        in_specs=[SMEM] + [VMEM] * (count_mem + len(early) + 2),
        out_specs=VMEM,
        scratch_shapes=[
            split,
            pltpu.VMEM((count, obs_values.shape[2], cols), F32),
            pltpu.VMEM((share, width), F32),
            pltpu.VMEM((share, width), F32),
            pltpu.VMEM((2 * total, share * width), F32),
            pltpu.SMEM((count,), jnp.int32),
        ],
        compiler_params=params,
        cost_estimate=cost(flops, 4 * height.size * count_mem),
        name="gram",
    )(owners, *heights, *early, obs_cells, obs_weights)
    sums = lax.all_to_all(sent, ("space", "mem"), split_axis=0, concat_axis=0, tiled=True)

    return pl.pallas_call(
        functools.partial(analysis_kernel, count_mem),
        out_shape=jax.ShapeDtypeStruct(state.shape, F32),
        in_specs=[VMEM] * (1 + 2 * count_mem),
        out_specs=VMEM,
        scratch_shapes=[pltpu.VMEM((total, 2 * total), F32)],
        compiler_params=params,
        name="analysis",
    )(sums, *heights, *winds)


def solution(mesh):
    return jax.shard_map(
        local,
        mesh=mesh,
        in_specs=(
            P("mem", None, "space", None),
            P("space", None),
            P(None, "space", None),
            P(None, "space", None),
            P("space", None),
            P("space", None, None, None),
            P("space", None, None, None),
        ),
        out_specs=P("mem", None, "space", None),
        check_vma=False,
    )
```

time: 84.5 us -> 63.6 us (0.75)
  waiting for transfers between devices: 33.5 us -> 13.7 us
  starting transfers between devices: 18.8 us -> 23.6 us
  local copies, waits for them, and re-layouts: 4.43 us -> 1.69 us
  Pallas kernels: 26.4 us -> 24.3 us
    ppermute x6, starting transfers between devices: 2.67 us -> 10.6 us  [swap(): return lax.ppermute(x, axis, [(i, i ^ bit) for i in range(count)])]
    all_to_all x1 -> x0, waiting for transfers between devices: 7.65 us -> none  [local(): got = lax.all_to_all(held, 'space', split_axis=0, concat_axis=0, tiled=True)]
    all_to_all x1 -> x0, starting transfers between devices: 7.07 us -> none  [local(): got = lax.all_to_all(held, 'space', split_axis=0, concat_axis=0, tiled=True)]
    ppermute x6, waiting for transfers between devices: 9.2 us -> 2.62 us  [swap(): return lax.ppermute(x, axis, [(i, i ^ bit) for i in range(count)])]
    pallas_call x1, Pallas kernels: 10.7 us -> 5.09 us  [local(): pl.pallas_call(functools.partial(analysis_kernel, count_mem), out_shape=j...]
    ppermute x2 -> x4, waiting for transfers between devices: 6.95 us -> 1.93 us  [the longest x2 1.93 us: local(): lax.ppermute(piece, ('space', 'mem'), [(s * count_mem + q, (s ^ peers * q...]
    ppermute x2 -> x4, starting transfers between devices: 6.28 us -> 10.1 us  [the longest x1 4.83 us: local(): above = lax.ppermute(to_below, 'space', [(i, i + 1) for i in range(ends)])]
    pallas_call x2 -> x4, Pallas kernels: 15.7 us -> 19.2 us  [the longest x1 9.74 us: local(): pl.pallas_call(functools.partial(gram_kernel, scale, group, count_mem), o...]
  transfers between devices with their start and end apart: 10 -> 11, of which waited for: 7 -> 4; matrix products, arithmetic and copies ran while one was open for 1% -> 0% of each run, Pallas kernels for 17% -> 25%
where the time goes in v2:
time: 63.6 us; the launch traced here: 63.3 us
  Pallas kernels  24.3 us (38%)
  starting transfers between devices  23.6 us (37%)
  waiting for transfers between devices  13.7 us (22%)
  local copies, waits for them, and re-layouts  1.69 us (3%)
    ppermute x6, starting transfers between devices, swap(): return lax.ppermute(x, axis, [(i, i ^ bit) for i in range(count)])  10.6 us
    pallas_call x1, Pallas kernels, local(): pl.pallas_call(functools.partial(gram_kernel, scale, group, count_mem), o...  9.74 us
    all_to_all x1, waiting for transfers between devices, local(): lax.all_to_all(sent, ('space', 'mem'), split_axis=0, concat_axis=0, tiled...  9.12 us
    pallas_call x1, Pallas kernels, predict(): pl.pallas_call(functools.partial(predict_kernel, group), out_shape=jax.Sh...  6.37 us
    pallas_call x1, Pallas kernels, local(): pl.pallas_call(functools.partial(analysis_kernel, count_mem), out_shape=j...  5.09 us
    ppermute x1, starting transfers between devices, local(): above = lax.ppermute(to_below, 'space', [(i, i + 1) for i in range(ends)])  4.83 us
    ppermute x2, starting transfers between devices, local(): lax.ppermute(piece, ('space', 'mem'), [(s * count_mem + q, (s ^ peers * q...  4.02 us
    all_to_all x1, starting transfers between devices, local(): lax.all_to_all(sent, ('space', 'mem'), split_axis=0, concat_axis=0, tiled...  2.87 us
  transfers between devices with their start and end apart: 11, of which 4 were waited for; matrix products, arithmetic and copies ran while one was open for 0% of the time, Pallas kernels for 25%

profile of v2, /device:TPU:0, one launch (start us, length us, event | category | flops | bytes accessed | tf_op | source)
XLA Modules:
  0.0 63.3 jit_solution(1039387634125853777)
XLA Ops:
  0.0 0.0 copy-start
  0.0 0.0 copy-start.3
  0.0 2.2 %edges.1 = (f32[72,256]{1,0:T(8,128)}, f32[72,256]{1,0:T(8,128)}, f32[16,256]{1,0:T(8,128)}, f32[16,256]{1,0:T(8,128)}) custom-call(f32[16,3,16,256]{3,2,1,0:T(8,128)} %state.3, f32[16,256]{1,0:T(8,128)} %depth.3, f32[1,8,16,128]{3,2,1,0:T(8,128)} %values.1, f32[1,8,16,128]{3,2,1,0:T(8,128)} %precision.1), custom_call_target="tpu_custom_call" | custom-call | tf_op jit(solution)/shard_map/edges/pallas_call | solution.py:61
  2.2 4.8 %collective-permute-start = (f32[72,256]{1,0:T(8,128)}, f32[72,256]{1,0:T(8,128)S(1)}, u32[]{:S(2)}, u32[]{:S(2)}) collective-permute-start(f32[72,256]{1,0:T(8,128)} %get-tuple-element.13), channel_id=1, source_target_pairs={{0,4},{4,8},{8,12},{12,16},{16,20},{20,24},{24,28},{1,5},{5,9},{9,... | collective-permute-start | bytes 221192 | tf_op jit(solution)/shard_map/ppermute | solution.py:456
  7.0 1.3 %collective-permute-start.1 = (f32[72,256]{1,0:T(8,128)}, f32[72,256]{1,0:T(8,128)S(1)}, u32[]{:S(2)}, u32[]{:S(2)}) collective-permute-start(f32[72,256]{1,0:T(8,128)} %get-tuple-element.14), channel_id=1, source_target_pairs={{4,0},{8,4},{12,8},{16,12},{20,16},{24,20},{28,24},{5,1},{9,5},{13... | collective-permute-start | bytes 221192 | tf_op jit(solution)/shard_map/ppermute | solution.py:455
  8.3 1.4 %collective-permute-start.2 = (f32[16,256]{1,0:T(8,128)}, f32[16,256]{1,0:T(8,128)S(1)}, u32[]{:S(2)}, u32[]{:S(2)}) collective-permute-start(f32[16,256]{1,0:T(8,128)} %get-tuple-element.15), channel_id=1, source_target_pairs={{0,0},{1,9},{2,18},{3,27},{4,4},{5,13},{6,22},{7,31},{8,8},{9,1},{... | collective-permute-start | bytes 49160 | tf_op jit(solution)/shard_map/ppermute | solution.py:458
  9.7 0.0 copy-start.4
  9.7 0.0 copy-start.5
  9.7 2.6 %collective-permute-start.3 = (f32[16,256]{1,0:T(8,128)}, f32[16,256]{1,0:T(8,128)S(1)}, u32[]{:S(2)}, u32[]{:S(2)}) collective-permute-start(f32[16,256]{1,0:T(8,128)} %get-tuple-element.16), channel_id=1, source_target_pairs={{0,4},{1,13},{2,22},{3,31},{4,0},{5,9},{6,18},{7,27},{8,12},{9,5},... | collective-permute-start | bytes 49160 | tf_op jit(solution)/shard_map/ppermute | solution.py:458
  12.3 0.0 collective-permute-done.2.refs_0_
  12.3 1.9 %collective-permute-done.3.refs_1_ = f32[16,256]{1,0:T(8,128)S(1)} collective-permute-done((f32[16,256]{1,0:T(8,128)}, f32[16,256]{1,0:T(8,128)S(1)}, u32[]{:S(2)}, u32[]{:S(2)}) %collective-permute-start.3) | collective-permute-done | bytes 16416 | tf_op jit(solution)/shard_map/ppermute | solution.py:458
  14.2 0.0 collective-permute-done.above
  14.3 0.0 collective-permute-done.1.below
  14.3 0.0 copy-done
  14.3 0.0 copy-done.3
  14.3 0.9 %forecast.1 = (f32[18,16,256]{2,1,0:T(8,128)S(1)}, f32[2,16,16,256]{3,2,1,0:T(8,128)S(1)}) custom-call(f32[16,3,16,256]{3,2,1,0:T(8,128)S(1)} %copy-done, f32[16,256]{1,0:T(8,128)S(1)} %copy-done.3, f32[72,256]{1,0:T(8,128)S(1)} %collective-permute-done.above, f32[72,256]{1,0:T(8,128)S(1)} %collective-permute-done.1.below, ...), custom_call_target="tpu_custom_call" | custom-call | tf_op jit(solution)/shard_map/forecast/pallas_call | solution.py:147
  15.2 2.4 %collective-permute-start.4 = (f32[18,16,256]{2,1,0:T(8,128)S(1)}, f32[18,16,256]{2,1,0:T(8,128)S(1)}, u32[]{:S(2)}, u32[]{:S(2)}) collective-permute-start(f32[18,16,256]{2,1,0:T(8,128)S(1)} %get-tuple-element.17.refs_0_), channel_id=1, source_target_pairs={{0,1},{1,0},{2,3},{3,2},{4,5},{5,4},{6,7},{7,6},{8,9},{9,8},{10,11... | collective-permute-start | bytes 884744 | tf_op jit(solution)/shard_map/ppermute | solution.py:432
  17.6 5.8 %collective-permute-start.5 = (f32[18,16,256]{2,1,0:T(8,128)S(1)}, f32[18,16,256]{2,1,0:T(8,128)S(1)}, u32[]{:S(2)}, u32[]{:S(2)}) collective-permute-start(f32[18,16,256]{2,1,0:T(8,128)S(1)} %get-tuple-element.17.refs_0_), channel_id=1, source_target_pairs={{0,2},{1,3},{2,0},{3,1},{4,6},{5,7},{6,4},{7,5},{8,10},{9,11},{10,... | collective-permute-start | bytes 884744 | tf_op jit(solution)/shard_map/ppermute | solution.py:432
  23.4 0.0 collective-permute-done.4.refs_1_
  23.4 0.0 copy-done.4
  23.4 0.0 copy-done.5
  23.4 6.4 %predict.1.refs_4_ = f32[16,32,128]{2,1,0:T(8,128)S(1)} custom-call(f32[18,16,256]{2,1,0:T(8,128)S(1)} %get-tuple-element.17.refs_0_, f32[18,16,256]{2,1,0:T(8,128)S(1)} %collective-permute-done.4.refs_1_, s32[4,64,128]{2,1,0:T(8,128)S(1)} %copy-done.4, f32[4,64,128]{2,1,0:T(8,128)S(1)} %copy-done.5), custom_call_target="tpu_custom_call" | custom-call | flops 4294967296 | bytes 589824 | tf_op jit(solution)/shard_map/predict/pallas_call | solution.py:478
  29.8 1.2 %collective-permute-done.5.refs_2_ = f32[18,16,256]{2,1,0:T(8,128)S(1)} collective-permute-done((f32[18,16,256]{2,1,0:T(8,128)S(1)}, f32[18,16,256]{2,1,0:T(8,128)S(1)}, u32[]{:S(2)}, u32[]{:S(2)}) %collective-permute-start.5) | collective-permute-done | bytes 294944 | tf_op jit(solution)/shard_map/ppermute | solution.py:432
  31.0 0.0 collective-permute-start.6
  31.0 0.0 copy-start.6
  31.0 1.8 %collective-permute-start.8 = (f32[2,16,16,256]{3,2,1,0:T(8,128)S(1)}, f32[2,16,16,256]{3,2,1,0:T(8,128)S(1)}, u32[]{:S(2)}, u32[]{:S(2)}) collective-permute-start(f32[2,16,16,256]{3,2,1,0:T(8,128)S(1)} %get-tuple-element.20.refs_4_), channel_id=1, source_target_pairs={{0,2},{1,3},{2,0},{3,1},{4,6},{5,7},{6,4},{7,5},{8,10},{9,11},{10,... | collective-permute-start | bytes 1572872 | tf_op jit(solution)/shard_map/ppermute | solution.py:432
  32.8 0.0 collective-permute-done.6.refs_3_
  32.8 0.0 copy-done.6
  32.8 9.7 %gram.1 = f32[32,17,1,128]{3,2,1,0:T(1,128)} custom-call(s32[64]{0:T(128)S(1)} %bitcast.1, f32[18,16,256]{2,1,0:T(8,128)S(1)} %get-tuple-element.17.refs_0_, f32[18,16,256]{2,1,0:T(8,128)S(1)} %collective-permute-done.4.refs_1_, f32[18,16,256]{2,1,0:T(8,128)S(1)} %collective-permute-done.5.refs_2_, f32[18,16,256]{2,1,0:T(8,128)S(1)} %collective-permute-done.6.refs_3_, ...), custom_call_target="tpu_custom_call" | custom-call | flops 4294967296 | bytes 1179648 | tf_op jit(solution)/shard_map/gram/pallas_call | solution.py:513
  42.5 0.0 copy-start.1
  42.5 0.7 %copy-done.1 = f32[18,16,256]{2,1,0:T(8,128)} copy-done((f32[18,16,256]{2,1,0:T(8,128)}, f32[18,16,256]{2,1,0:T(8,128)S(1)}, u32[]{:S(2)}) %copy-start.1) | copy-done | bytes 294936
  43.2 2.9 %all-to-all-start = ((f32[32,17,1,128]{3,2,1,0:T(1,128)}), f32[32,17,1,128]{3,2,1,0:T(1,128)S(1)}, u32[]{:S(2)}, u32[]{:S(2)}) async-start(f32[32,17,1,128]{3,2,1,0:T(1,128)} %gram.1), calls=%async_computation | async-start | bytes 557056 | tf_op jit(solution)/shard_map/all_to_all | solution.py:530
  46.1 0.3 collective-permute-start.7
  46.4 0.0 collective-permute-done.8.refs_6_
  46.4 0.3 collective-permute-start.9
  46.7 1.4 %collective-permute-done.7.refs_5_ = f32[2,16,16,256]{3,2,1,0:T(8,128)S(1)} collective-permute-done((f32[2,16,16,256]{3,2,1,0:T(8,128)S(1)}, f32[2,16,16,256]{3,2,1,0:T(8,128)S(1)}, u32[]{:S(2)}, u32[]{:S(2)}) %collective-permute-start.7) | collective-permute-done | bytes 524320 | tf_op jit(solution)/shard_map/ppermute | solution.py:432
  48.1 9.1 %all-to-all-done.sums = f32[32,17,1,128]{3,2,1,0:T(1,128)S(1)} async-done(((f32[32,17,1,128]{3,2,1,0:T(1,128)}), f32[32,17,1,128]{3,2,1,0:T(1,128)S(1)}, u32[]{:S(2)}, u32[]{:S(2)}) %all-to-all-start) | async-done | bytes 278560 | tf_op jit(solution)/shard_map/all_to_all | solution.py:530
  57.2 0.0 collective-permute-done.9.refs_7_
  57.2 0.0 copy-start.2
  57.2 1.0 %copy-done.2 = f32[18,16,256]{2,1,0:T(8,128)S(1)} copy-done((f32[18,16,256]{2,1,0:T(8,128)S(1)}, f32[18,16,256]{2,1,0:T(8,128)}, u32[]{:S(2)}) %copy-start.2) | copy-done | bytes 294936
  58.2 5.1 %analysis.1 = f32[16,3,16,256]{3,2,1,0:T(8,128)} custom-call(f32[32,17,1,128]{3,2,1,0:T(1,128)S(1)} %all-to-all-done.sums, f32[18,16,256]{2,1,0:T(8,128)S(1)} %get-tuple-element.17.refs_0_, f32[18,16,256]{2,1,0:T(8,128)S(1)} %collective-permute-done.4.refs_1_, f32[18,16,256]{2,1,0:T(8,128)S(1)} %collective-permute-done.5.refs_2_, ...), custom_call_target="tpu_custom_call" | custom-call | tf_op jit(solution)/shard_map/analysis/pallas_call | solution.py:532
Async XLA Ops:
  0.0 14.3 %copy-start = (f32[16,3,16,256]{3,2,1,0:T(8,128)S(1)}, f32[16,3,16,256]{3,2,1,0:T(8,128)}, u32[]{:S(2)}) copy-start(f32[16,3,16,256]{3,2,1,0:T(8,128)} %state.3) | copy-start | bytes 2359300
  0.0 14.3 %copy-start.3 = (f32[16,256]{1,0:T(8,128)S(1)}, f32[16,256]{1,0:T(8,128)}, u32[]{:S(2)}) copy-start(f32[16,256]{1,0:T(8,128)} %depth.3) | copy-start | bytes 49156
  2.2 12.1 %collective-permute-start = (f32[72,256]{1,0:T(8,128)}, f32[72,256]{1,0:T(8,128)S(1)}, u32[]{:S(2)}, u32[]{:S(2)}) collective-permute-start(f32[72,256]{1,0:T(8,128)} %get-tuple-element.13), channel_id=1, source_target_pairs={{0,4},{4,8},{8,12},{12,16},{16,20},{20,24},{24,28},{1,5},{5,9},{9,... | collective-permute-start | bytes 221192 | tf_op jit(solution)/shard_map/ppermute | solution.py:456
  7.0 7.3 %collective-permute-start.1 = (f32[72,256]{1,0:T(8,128)}, f32[72,256]{1,0:T(8,128)S(1)}, u32[]{:S(2)}, u32[]{:S(2)}) collective-permute-start(f32[72,256]{1,0:T(8,128)} %get-tuple-element.14), channel_id=1, source_target_pairs={{4,0},{8,4},{12,8},{16,12},{20,16},{24,20},{28,24},{5,1},{9,5},{13... | collective-permute-start | bytes 221192 | tf_op jit(solution)/shard_map/ppermute | solution.py:455
  8.3 4.0 %collective-permute-start.2 = (f32[16,256]{1,0:T(8,128)}, f32[16,256]{1,0:T(8,128)S(1)}, u32[]{:S(2)}, u32[]{:S(2)}) collective-permute-start(f32[16,256]{1,0:T(8,128)} %get-tuple-element.15), channel_id=1, source_target_pairs={{0,0},{1,9},{2,18},{3,27},{4,4},{5,13},{6,22},{7,31},{8,8},{9,1},{... | collective-permute-start | bytes 49160 | tf_op jit(solution)/shard_map/ppermute | solution.py:458
  9.7 13.7 %copy-start.4 = (s32[4,64,128]{2,1,0:T(8,128)S(1)}, s32[4,64,128]{2,1,0:T(8,128)}, u32[]{:S(2)}) copy-start(s32[4,64,128]{2,1,0:T(8,128)} %refs_5_.1) | copy-start | bytes 393220
  9.7 13.7 %copy-start.5 = (f32[4,64,128]{2,1,0:T(8,128)S(1)}, f32[4,64,128]{2,1,0:T(8,128)}, u32[]{:S(2)}) copy-start(f32[4,64,128]{2,1,0:T(8,128)} %refs_6_.1) | copy-start | bytes 393220
  9.7 4.6 %collective-permute-start.3 = (f32[16,256]{1,0:T(8,128)}, f32[16,256]{1,0:T(8,128)S(1)}, u32[]{:S(2)}, u32[]{:S(2)}) collective-permute-start(f32[16,256]{1,0:T(8,128)} %get-tuple-element.16), channel_id=1, source_target_pairs={{0,4},{1,13},{2,22},{3,31},{4,0},{5,9},{6,18},{7,27},{8,12},{9,5},... | collective-permute-start | bytes 49160 | tf_op jit(solution)/shard_map/ppermute | solution.py:458
  15.2 8.2 %collective-permute-start.4 = (f32[18,16,256]{2,1,0:T(8,128)S(1)}, f32[18,16,256]{2,1,0:T(8,128)S(1)}, u32[]{:S(2)}, u32[]{:S(2)}) collective-permute-start(f32[18,16,256]{2,1,0:T(8,128)S(1)} %get-tuple-element.17.refs_0_), channel_id=1, source_target_pairs={{0,1},{1,0},{2,3},{3,2},{4,5},{5,4},{6,7},{7,6},{8,9},{9,8},{10,11... | collective-permute-start | bytes 884744 | tf_op jit(solution)/shard_map/ppermute | solution.py:432
  17.6 13.4 %collective-permute-start.5 = (f32[18,16,256]{2,1,0:T(8,128)S(1)}, f32[18,16,256]{2,1,0:T(8,128)S(1)}, u32[]{:S(2)}, u32[]{:S(2)}) collective-permute-start(f32[18,16,256]{2,1,0:T(8,128)S(1)} %get-tuple-element.17.refs_0_), channel_id=1, source_target_pairs={{0,2},{1,3},{2,0},{3,1},{4,6},{5,7},{6,4},{7,5},{8,10},{9,11},{10,... | collective-permute-start | bytes 884744 | tf_op jit(solution)/shard_map/ppermute | solution.py:432
  31.0 1.8 %collective-permute-start.6 = (f32[18,16,256]{2,1,0:T(8,128)S(1)}, f32[18,16,256]{2,1,0:T(8,128)S(1)}, u32[]{:S(2)}, u32[]{:S(2)}) collective-permute-start(f32[18,16,256]{2,1,0:T(8,128)S(1)} %collective-permute-done.5.refs_2_), channel_id=1, source_target_pairs={{0,1},{1,0},{2,3},{3,2},{4,5},{5,4},{6,7},{7,6},{8,9},{9,8},{10,11... | collective-permute-start | bytes 884744 | tf_op jit(solution)/shard_map/ppermute | solution.py:432
  31.0 1.8 %copy-start.6 = (s32[64,1]{0,1:T(1,128)S(1)}, s32[64,1]{0,1:T(1,128)}, u32[]{:S(2)}) copy-start(s32[64,1]{0,1:T(1,128)} %param.11) | copy-start | bytes 772
  31.0 15.4 %collective-permute-start.8 = (f32[2,16,16,256]{3,2,1,0:T(8,128)S(1)}, f32[2,16,16,256]{3,2,1,0:T(8,128)S(1)}, u32[]{:S(2)}, u32[]{:S(2)}) collective-permute-start(f32[2,16,16,256]{3,2,1,0:T(8,128)S(1)} %get-tuple-element.20.refs_4_), channel_id=1, source_target_pairs={{0,2},{1,3},{2,0},{3,1},{4,6},{5,7},{6,4},{7,5},{8,10},{9,11},{10,... | collective-permute-start | bytes 1572872 | tf_op jit(solution)/shard_map/ppermute | solution.py:432
  42.5 0.7 %copy-start.1 = (f32[18,16,256]{2,1,0:T(8,128)}, f32[18,16,256]{2,1,0:T(8,128)S(1)}, u32[]{:S(2)}) copy-start(f32[18,16,256]{2,1,0:T(8,128)S(1)} %collective-permute-done.6.refs_3_) | copy-start | bytes 884740
  43.2 14.0 %all-to-all-start = ((f32[32,17,1,128]{3,2,1,0:T(1,128)}), f32[32,17,1,128]{3,2,1,0:T(1,128)S(1)}, u32[]{:S(2)}, u32[]{:S(2)}) async-start(f32[32,17,1,128]{3,2,1,0:T(1,128)} %gram.1), calls=%async_computation | async-start | bytes 557056 | tf_op jit(solution)/shard_map/all_to_all | solution.py:530
  46.1 2.0 %collective-permute-start.7 = (f32[2,16,16,256]{3,2,1,0:T(8,128)S(1)}, f32[2,16,16,256]{3,2,1,0:T(8,128)S(1)}, u32[]{:S(2)}, u32[]{:S(2)}) collective-permute-start(f32[2,16,16,256]{3,2,1,0:T(8,128)S(1)} %get-tuple-element.20.refs_4_), channel_id=1, source_target_pairs={{0,1},{1,0},{2,3},{3,2},{4,5},{5,4},{6,7},{7,6},{8,9},{9,8},{10,11... | collective-permute-start | bytes 1572872 | tf_op jit(solution)/shard_map/ppermute | solution.py:432
  46.4 10.8 %collective-permute-start.9 = (f32[2,16,16,256]{3,2,1,0:T(8,128)S(1)}, f32[2,16,16,256]{3,2,1,0:T(8,128)S(1)}, u32[]{:S(2)}, u32[]{:S(2)}) collective-permute-start(f32[2,16,16,256]{3,2,1,0:T(8,128)S(1)} %collective-permute-done.8.refs_6_), channel_id=1, source_target_pairs={{0,1},{1,0},{2,3},{3,2},{4,5},{5,4},{6,7},{7,6},{8,9},{9,8},{10,11... | collective-permute-start | bytes 1572872 | tf_op jit(solution)/shard_map/ppermute | solution.py:432
  57.2 1.0 %copy-start.2 = (f32[18,16,256]{2,1,0:T(8,128)S(1)}, f32[18,16,256]{2,1,0:T(8,128)}, u32[]{:S(2)}) copy-start(f32[18,16,256]{2,1,0:T(8,128)} %copy-done.1) | copy-start | bytes 884740

commit v3 on v2

--- a/solution.py
+++ b/solution.py
@@ -16,6 +16,12 @@
 SMEM = pl.BlockSpec(memory_space=pltpu.SMEM)
 F32 = jnp.float32
 BF16 = jnp.bfloat16
+PARAMS = pltpu.CompilerParams(vmem_limit_bytes=12 * 1024 * 1024)
+FORECAST_FLOPS = 2 * 10**9
+
+
+def cost(flops, size):
+    return pl.CostEstimate(flops=flops, bytes_accessed=size, transcendentals=0)
 
 
 def diff_cols(field):
@@ -95,9 +101,9 @@
         v[t] = state[:, 2, t, :]
         flux[t + 1] = deep[t] * u[t]
     deltas = []
-    for (first_flux, _, _, _), _, sign, edge, _ in sides:
+    for (first_flux, _, _, _), _, sign, edge, inside in sides:
         deltas.append(sign * mass_rate * flux[edge + 1])
-        flux[outer(edge)] = first_flux
+        flux[outer(edge)] = first_flux * inside
 
     def new_heights():
         for t in range(rows):
@@ -123,7 +129,7 @@
     new_heights()
     for delta, ((_, first, east, _), deeps, sign, edge, inside) in zip(deltas, sides):
         h[outer(edge)] = (first + delta) * inside
-        flux[outer(edge)] = deeps[0] * (east + sign * wave_rate * h[edge + 1])
+        flux[outer(edge)] = inside * deeps[0] * (east + sign * wave_rate * h[edge + 1])
     new_winds(keep)
     rims = []
     for delta, ((_, _, _, twice), deeps, sign, edge, inside) in zip(deltas, sides):
@@ -158,7 +164,8 @@
             pltpu.VMEM((rows, members, cols), F32),
             pltpu.VMEM((rows + 2, members, cols), F32),
         ],
-        compiler_params=pltpu.CompilerParams(vmem_limit_bytes=32 * 1024 * 1024),
+        compiler_params=PARAMS,
+        cost_estimate=cost(FORECAST_FLOPS, 4 * state.size),
         name="forecast",
     )(state, depth, above, below, *held)
 
@@ -204,12 +211,38 @@
         put(b, result)
         return carry
 
-    lax.fori_loop(0, blocks, block, 0, unroll=2)
-
-
-def predict_kernel(count, *refs):
+    lax.fori_loop(0, blocks, block, 0, unroll=8)
+
+
+def collect(got, pieces, split):
+    _, members, _ = pieces[0].shape
+    rows = split.shape[0] // (len(pieces) * members)
+    slots = got.shape[1]
+    peers = got.shape[0] // len(pieces)
+    for k, piece in enumerate(pieces):
+        for j in range(peers):
+            at = j * slots
+            got[k * peers + j] = piece[rows + at // members, at % members : at % members + slots, :]
+
+
+def predict_kernel(count, owners, *refs):
     pieces = refs[:count]
-    cells, weights, out, split = refs[count:]
+    cells, weights, out, near, slots, split, used = refs[count:]
+    share = slots.shape[0]
+    collect(near, pieces, split)
+    begin = lax.axis_index("mem") * share
+    for owner in range(used.shape[0]):
+        used[owner] = 0
+
+    def skip(b, carry):
+        used[owners[b]] += 1
+        return carry
+
+    lax.fori_loop(0, begin, skip, 0)
+    for i in range(share):
+        owner = owners[begin + i]
+        slots[i] = used[owner]
+        used[owner] += 1
 
     def put(b, result):
         out[b] = result
@@ -217,72 +250,46 @@
     interpolate(pieces, cells, weights, split, put)
 
 
-def gram_kernel(scale, count, count_mem, owners, *refs):
-    pieces = refs[:count_mem]
-    early = refs[count_mem : count_mem + count_mem // count - 1]
-    cells, weights, out, split, got, seen, factor, lined, used = refs[-9:]
+def gram_kernel(scale, count, count_mem, owners, slots, *refs):
+    pieces = refs[:count]
+    cells, weights, near, early, out, split, lined, got = refs[count:]
     _, members, cols = pieces[0].shape
     total = members * count_mem
     part = members * count
-    rows = split.shape[0] // part
-    all_blocks = owners.shape[0]
-    blocks, width = all_blocks // count_mem, cells.shape[2]
-    slots = got.shape[1]
-    peers = got.shape[0] // count_mem
-    space, quarter = lax.axis_index("space"), lax.axis_index("mem")
-
-    for owner in range(got.shape[0]):
-        used[owner] = 0
-    for k, piece in enumerate(pieces):
-        who = lax.bitwise_xor(quarter, k)
-        for j in range(peers):
-            at = j * slots
-            got[who * peers + j] = piece[
-                rows + at // members, at % members : at % members + slots, :
-            ]
-
-    def dispatch(b, carry):
-        owner = owners[b]
-        slot = used[owner]
-        used[owner] = slot + 1
-        at = b - quarter * blocks
-
-        @pl.when((at >= 0) & (at < blocks))
-        def _():
-            line = got[lax.bitwise_xor(owner, space), pl.ds(slot, 1)]
-            seen[pl.ds(at, 1)] = line[:, 0:width]
-            factor[pl.ds(at, 1)] = line[:, width : 2 * width] * scale
-
-        return carry
-
-    lax.fori_loop(0, all_blocks, dispatch, 0)
+    blocks, width = slots.shape[0], cells.shape[2]
+    quarter = lax.axis_index("mem")
+    peers = near.shape[0] // count
+    got[0 : near.shape[0]] = near[...]
+    collect(got.at[near.shape[0] :], pieces, split)
 
     mine = quarter // count
-    groups = count_mem // count
-    for g in range(groups - 1):
-        base = pl.multiple_of(lax.bitwise_xor(mine, g) * part, part)
-        for b in range(blocks):
-            lined[pl.ds(base, part), b * width : (b + 1) * width] = early[g][b]
-    final = pl.multiple_of(lax.bitwise_xor(mine, groups - 1) * part, part)
+    base = pl.multiple_of(mine * part, part)
+    final = pl.multiple_of(lax.bitwise_xor(mine, 1) * part, part)
 
     def put(b, result):
         at = pl.ds(pl.multiple_of(b * width, width), width)
         lined[pl.ds(final, part), at] = result
-
-    interpolate(pieces[count_mem - count :], cells, weights, split, put)
+        lined[pl.ds(base, part), at] = early[b]
+
+    interpolate(pieces, cells, weights, split, put)
     lined[total : 2 * total] = jnp.zeros((total, blocks * width), F32)
     for b in range(blocks):
+        apart = lax.bitwise_xor(owners[quarter * blocks + b], lax.axis_index("space"))
+        line = got[lax.bitwise_xor(apart, quarter * peers), pl.ds(slots[b], 1)]
+        seen, much = line[:, 0:width], line[:, width : 2 * width] * scale
         at = pl.ds(b * width, width)
         values = lined[0:total, at]
-        much = factor[b : b + 1]
         middle = jnp.sum(values, axis=0, keepdims=True) * (1.0 / total)
         lined[0:total, at] = (values - middle) * much
-        lined[total : total + 1, at] = (seen[b : b + 1] - middle) * much
+        lined[total : total + 1, at] = (seen - middle) * much
 
     x = lined[...]
-    gram = lax.dot_general(
-        x, x, (((1,), (1,)), ((), ())), precision=lax.Precision.HIGHEST, preferred_element_type=F32
-    )
+    high = x.astype(BF16)
+    low = (x - high.astype(F32)).astype(BF16)
+    turned = (((1,), (1,)), ((), ()))
+    gram = lax.dot_general(high, high, turned, preferred_element_type=F32)
+    cross = lax.dot_general(high, low, turned, preferred_element_type=F32)
+    gram = gram + (cross + cross.T)
     packed = pack_gram(gram, total)
     spread = out.shape[1]
     for d in range(out.shape[0]):
@@ -336,7 +343,7 @@
     line = lax.broadcasted_iota(jnp.int32, (total, span), 0)
     work = jnp.where(lane < total, system, jnp.where(lane == line + total, 1.0, 0.0))
     tiles = [work[8 * g : 8 * g + 8] for g in range(total // 8)]
-    step = 4
+    step = 8
     below = lax.broadcasted_iota(jnp.int32, (8, span), 0)
 
     def lanes(x, k):
@@ -436,10 +443,6 @@
     return lax.optimization_barrier((x,) + others)[0]
 
 
-def cost(flops, size):
-    return pl.CostEstimate(flops=flops, bytes_accessed=size, transcendentals=0)
-
-
 def local(state, depth, obs_cells, obs_weights, owner_map, obs_values, obs_precision):
     members, fields, rows, cols = state.shape
     count = lax.axis_size("space")
@@ -447,13 +450,14 @@
     total = members * count_mem
     blocks, width = obs_cells.shape[1:]
     share = blocks // count_mem
+    scale = math.sqrt((total - 1) / (count * blocks * width))
+
     peers = count // count_mem
-    scale = math.sqrt((total - 1) / (count * blocks * width))
 
     to_above, to_below, *held = edges(peers, state, depth, obs_values, obs_precision)
     ends = count - 1
-    below = lax.ppermute(to_above, "space", [(i + 1, i) for i in range(ends)])
-    above = lax.ppermute(to_below, "space", [(i, i + 1) for i in range(ends)])
+    below = lax.ppermute(to_above, "space", [((i + 1) % count, i) for i in range(count)])
+    above = lax.ppermute(to_below, "space", [(i, (i + 1) % count) for i in range(count)])
     held = [
         lax.ppermute(
             piece,
@@ -468,65 +472,54 @@
     ]
     height, wind = forecast(ends, state, depth, above, below, held)
 
-    group = 2
-    early_shape = (share, group * members, width)
-    split = pltpu.VMEM((rows * group * members, 2 * cols), BF16)
-    params = pltpu.CompilerParams(vmem_limit_bytes=20 * 1024 * 1024)
-    flops = 4 * obs_cells.shape[0] * share * width * rows * members * group * cols
-
-    def predict(k):
-        return pl.pallas_call(
-            functools.partial(predict_kernel, group),
-            out_shape=jax.ShapeDtypeStruct(early_shape, F32),
-            in_specs=[VMEM] * (group + 2),
-            out_specs=VMEM,
-            scratch_shapes=[split],
-            compiler_params=params,
-            cost_estimate=cost(flops, 4 * height.size * group),
-            name="predict",
-        )(*[heights[i] for i in range(k, k + group)], obs_cells, obs_weights)
-
+    near, far = 1, count_mem // 2
+    early_shape = (share, far * members, width)
+    split = pltpu.VMEM((rows * far * members, 2 * cols), BF16)
+    flops = 4 * obs_cells.shape[0] * share * width * rows * members * far * cols
+    owners = owner_map[:, 0]
     heights = {0: height}
     winds = {0: wind}
-    far = [1 << i for i in range(1, count_mem.bit_length() - 1)]
-    for bit in far:
-        heights[bit] = swap(height, "mem", bit)
-    heights[1] = swap(height, "mem", 1)
-    early = [predict(0)]
-    for bit in far:
-        heights[bit] = after(heights[bit], early[0])
-        for k in range(1, bit):
-            heights[bit + k] = swap(heights[bit], "mem", k) if k == 1 else swap(heights[bit + 1], "mem", k - 1)
-    for bit in far:
-        winds[bit] = swap(after(wind, heights[bit]), "mem", bit)
-    winds[1] = swap(wind, "mem", 1)
-    for bit in far:
-        for k in range(1, bit):
-            winds[bit + k] = swap(winds[bit], "mem", k) if k == 1 else swap(winds[bit + 1], "mem", k - 1)
-    early += [predict(k) for k in range(group, count_mem - group, group)]
+    heights[far] = swap(height, "mem", far)
+    heights[near] = swap(height, "mem", near)
+    near_shape = (far * peers, obs_values.shape[2], cols)
+    early, first, slots = pl.pallas_call(
+        functools.partial(predict_kernel, far),
+        out_shape=(
+            jax.ShapeDtypeStruct(early_shape, F32),
+            jax.ShapeDtypeStruct(near_shape, F32),
+            jax.ShapeDtypeStruct((share,), jnp.int32),
+        ),
+        in_specs=[SMEM] + [VMEM] * (far + 2),
+        out_specs=(VMEM, VMEM, SMEM),
+        scratch_shapes=[split, pltpu.SMEM((count,), jnp.int32)],
+        compiler_params=PARAMS,
+        cost_estimate=cost(flops, 4 * height.size * far),
+        name="predict",
+    )(owners, heights[0], heights[near], obs_cells, obs_weights)
+    heights[far] = after(heights[far], early)
+    heights[far + near] = swap(heights[far], "mem", near)
+    winds[far] = swap(after(wind, heights[far]), "mem", far)
+    winds[near] = swap(wind, "mem", near)
+    winds[far + near] = swap(winds[far], "mem", near)
     heights = [heights[k] for k in range(count_mem)]
     winds = [winds[k] for k in range(count_mem)]
 
-    owners = owner_map[:, 0]
     spread = total // 4 + 1
     devices = count * count_mem
     sent = pl.pallas_call(
-        functools.partial(gram_kernel, scale, group, count_mem),
+        functools.partial(gram_kernel, scale, far, count_mem),
         out_shape=jax.ShapeDtypeStruct((devices, spread, 1, 2 * total), F32),
-        in_specs=[SMEM] + [VMEM] * (count_mem + len(early) + 2),
+        in_specs=[SMEM, SMEM] + [VMEM] * (far + 4),
         out_specs=VMEM,
         scratch_shapes=[
             split,
-            pltpu.VMEM((count, obs_values.shape[2], cols), F32),
-            pltpu.VMEM((share, width), F32),
-            pltpu.VMEM((share, width), F32),
             pltpu.VMEM((2 * total, share * width), F32),
-            pltpu.SMEM((count,), jnp.int32),
+            pltpu.VMEM((count,) + near_shape[1:], F32),
         ],
-        compiler_params=params,
+        compiler_params=PARAMS,
         cost_estimate=cost(flops, 4 * height.size * count_mem),
         name="gram",
-    )(owners, *heights, *early, obs_cells, obs_weights)
+    )(owners, slots, *heights[far:], obs_cells, obs_weights, first, early)
     sums = lax.all_to_all(sent, ("space", "mem"), split_axis=0, concat_axis=0, tiled=True)
 
     return pl.pallas_call(
@@ -535,7 +528,7 @@
         in_specs=[VMEM] * (1 + 2 * count_mem),
         out_specs=VMEM,
         scratch_shapes=[pltpu.VMEM((total, 2 * total), F32)],
-        compiler_params=params,
+        compiler_params=PARAMS,
         name="analysis",
     )(sums, *heights, *winds)
 

time: 63.6 us -> 56.7 us (0.89)
  starting transfers between devices: 23.6 us -> 18 us
  Pallas kernels: 24.3 us -> 19.9 us
  waiting for transfers between devices: 13.7 us -> 16.7 us
    pallas_call x2, Pallas kernels: 16.1 us -> 12.6 us  [the longest x1 6.97 us: local(): pl.pallas_call(functools.partial(gram_kernel, scale, far, count_mem), out...]
    ppermute x6, starting transfers between devices: 10.6 us -> 7.19 us  [swap(): return lax.ppermute(x, axis, [(i, i ^ bit) for i in range(count)])]
    ppermute x2, starting transfers between devices: 4.02 us -> 1.37 us  [local(): lax.ppermute(piece, ('space', 'mem'), [(s * count_mem + q, (s ^ peers * q...]
    ppermute x2, waiting for transfers between devices: 1.93 us -> 3.95 us  [local(): lax.ppermute(piece, ('space', 'mem'), [(s * count_mem + q, (s ^ peers * q...]
    ppermute x6, waiting for transfers between devices: 2.62 us -> 3.64 us  [swap(): return lax.ppermute(x, axis, [(i, i ^ bit) for i in range(count)])]
    pallas_call x1, Pallas kernels: 5.09 us -> 4.28 us  [local(): pl.pallas_call(functools.partial(analysis_kernel, count_mem), out_shape=j...]
  transfers between devices with their start and end apart: 11 -> 11, of which waited for: 4 -> 5; matrix products, arithmetic and copies ran while one was open for 0% -> 0% of each run, Pallas kernels for 25% -> 22%
where the time goes in v3:
time: 56.7 us; the launch traced here: 56.4 us
  Pallas kernels  19.9 us (35%)
  starting transfers between devices  18 us (32%)
  waiting for transfers between devices  16.7 us (29%)
  local copies, waits for them, and re-layouts  1.7 us (3%)
    all_to_all x1, waiting for transfers between devices, local(): lax.all_to_all(sent, ('space', 'mem'), split_axis=0, concat_axis=0, tiled...  9.12 us
    ppermute x6, starting transfers between devices, swap(): return lax.ppermute(x, axis, [(i, i ^ bit) for i in range(count)])  7.19 us
    pallas_call x1, Pallas kernels, local(): pl.pallas_call(functools.partial(gram_kernel, scale, far, count_mem), out...  6.97 us
    pallas_call x1, Pallas kernels, local(): pl.pallas_call(functools.partial(predict_kernel, far), out_shape=(jax.Sha...  5.59 us
    pallas_call x1, Pallas kernels, local(): pl.pallas_call(functools.partial(analysis_kernel, count_mem), out_shape=j...  4.28 us
    ppermute x2, waiting for transfers between devices, local(): lax.ppermute(piece, ('space', 'mem'), [(s * count_mem + q, (s ^ peers * q...  3.95 us
    ppermute x6, waiting for transfers between devices, swap(): return lax.ppermute(x, axis, [(i, i ^ bit) for i in range(count)])  3.64 us
    all_to_all x1, starting transfers between devices, local(): lax.all_to_all(sent, ('space', 'mem'), split_axis=0, concat_axis=0, tiled...  3.41 us
  transfers between devices with their start and end apart: 11, of which 5 were waited for; matrix products, arithmetic and copies ran while one was open for 0% of the time, Pallas kernels for 22%

profile of v3, /device:TPU:0, one launch (start us, length us, event | category | flops | bytes accessed | tf_op | source)
XLA Modules:
  0.0 56.4 jit_solution(7309624852175392054)
XLA Ops:
  0.0 0.0 copy-start.3
  0.0 0.0 copy-start
  0.0 2.2 %edges.1 = (f32[72,256]{1,0:T(8,128)}, f32[72,256]{1,0:T(8,128)}, f32[16,256]{1,0:T(8,128)}, f32[16,256]{1,0:T(8,128)}) custom-call(f32[16,3,16,256]{3,2,1,0:T(8,128)} %state.3, f32[16,256]{1,0:T(8,128)} %depth.3, f32[1,8,16,128]{3,2,1,0:T(8,128)} %values.1, f32[1,8,16,128]{3,2,1,0:T(8,128)} %precision.1), custom_call_target="tpu_custom_call" | custom-call | tf_op jit(solution)/shard_map/edges/pallas_call | solution.py:67
  2.2 2.9 %collective-permute-start = (f32[72,256]{1,0:T(8,128)}, f32[72,256]{1,0:T(8,128)S(1)}, u32[]{:S(2)}, u32[]{:S(2)}) collective-permute-start(f32[72,256]{1,0:T(8,128)} %get-tuple-element.16), channel_id=1, source_target_pairs={{0,4},{4,8},{8,12},{12,16},{16,20},{20,24},{24,28},{28,0},{1,5},{5... | collective-permute-start | bytes 221192 | tf_op jit(solution)/shard_map/ppermute | solution.py:460
  5.1 3.1 %collective-permute-start.1 = (f32[72,256]{1,0:T(8,128)}, f32[72,256]{1,0:T(8,128)S(1)}, u32[]{:S(2)}, u32[]{:S(2)}) collective-permute-start(f32[72,256]{1,0:T(8,128)} %get-tuple-element.17), channel_id=1, source_target_pairs={{4,0},{8,4},{12,8},{16,12},{20,16},{24,20},{28,24},{0,28},{5,1},{9... | collective-permute-start | bytes 221192 | tf_op jit(solution)/shard_map/ppermute | solution.py:459
  8.2 1.4 %collective-permute-start.2 = (f32[16,256]{1,0:T(8,128)}, f32[16,256]{1,0:T(8,128)S(1)}, u32[]{:S(2)}, u32[]{:S(2)}) collective-permute-start(f32[16,256]{1,0:T(8,128)} %get-tuple-element.18), channel_id=1, source_target_pairs={{0,0},{1,9},{2,18},{3,27},{4,4},{5,13},{6,22},{7,31},{8,8},{9,1},{... | collective-permute-start | bytes 49160 | tf_op jit(solution)/shard_map/ppermute | solution.py:462
  9.6 0.0 copy-start.4
  9.6 0.0 copy-start.5
  9.6 0.0 collective-permute-start.3
  9.6 0.0 collective-permute-done.2.refs_0_
  9.6 4.0 %collective-permute-done.3.refs_1_ = f32[16,256]{1,0:T(8,128)S(1)} collective-permute-done((f32[16,256]{1,0:T(8,128)}, f32[16,256]{1,0:T(8,128)S(1)}, u32[]{:S(2)}, u32[]{:S(2)}) %collective-permute-start.3) | collective-permute-done | bytes 16416 | tf_op jit(solution)/shard_map/ppermute | solution.py:462
  13.5 0.0 collective-permute-done.above
  13.5 0.0 collective-permute-done.1.below
  13.5 0.0 copy-done.3
  13.5 0.0 copy-done
  13.5 0.9 %forecast.1 = (f32[18,16,256]{2,1,0:T(8,128)S(1)}, f32[2,16,16,256]{3,2,1,0:T(8,128)S(1)}) custom-call(f32[16,3,16,256]{3,2,1,0:T(8,128)S(1)} %copy-done, f32[16,256]{1,0:T(8,128)S(1)} %copy-done.3, f32[72,256]{1,0:T(8,128)S(1)} %collective-permute-done.above, f32[72,256]{1,0:T(8,128)S(1)} %collective-permute-done.1.below, ...), custom_call_target="tpu_custom_call" | custom-call | flops 2000000000 | bytes 786432 | tf_op jit(solution)/shard_map/forecast/pallas_call | solution.py:153
  14.5 0.0 copy-start.6
  14.5 0.1 collective-permute-start.4
  14.6 5.0 %collective-permute-start.5 = (f32[18,16,256]{2,1,0:T(8,128)S(1)}, f32[18,16,256]{2,1,0:T(8,128)S(1)}, u32[]{:S(2)}, u32[]{:S(2)}) collective-permute-start(f32[18,16,256]{2,1,0:T(8,128)S(1)} %get-tuple-element.20.refs_0_), channel_id=1, source_target_pairs={{0,2},{1,3},{2,0},{3,1},{4,6},{5,7},{6,4},{7,5},{8,10},{9,11},{10,... | collective-permute-start | bytes 884744 | tf_op jit(solution)/shard_map/ppermute | solution.py:439
  19.6 0.0 collective-permute-done.4.refs_1_
  19.6 0.0 copy-done.4
  19.6 0.0 copy-done.5
  19.6 0.0 copy-done.6
  19.6 5.6 %predict.1 = (f32[16,32,128]{2,1,0:T(8,128)S(1)}, f32[4,16,256]{2,1,0:T(8,128)S(1)}, s32[16]{0:T(128)S(1)}) custom-call(s32[64]{0:T(128)S(1)} %bitcast.1, f32[18,16,256]{2,1,0:T(8,128)S(1)} %get-tuple-element.20.refs_0_, f32[18,16,256]{2,1,0:T(8,128)S(1)} %collective-permute-done.4.refs_1_, s32[4,64,128]{2,1,0:T(8,128)S(1)} %copy-done.4, ...), custom_call_target="tpu_custom_call" | custom-call | flops 4294967296 | bytes 589824 | tf_op jit(solution)/shard_map/predict/pallas_call | solution.py:485
  25.2 2.0 %collective-permute-done.5.refs_0_.refs_2_ = f32[18,16,256]{2,1,0:T(8,128)S(1)} collective-permute-done((f32[18,16,256]{2,1,0:T(8,128)S(1)}, f32[18,16,256]{2,1,0:T(8,128)S(1)}, u32[]{:S(2)}, u32[]{:S(2)}) %collective-permute-start.5) | collective-permute-done | bytes 294944 | tf_op jit(solution)/shard_map/ppermute | solution.py:439
  27.2 0.0 collective-permute-start.6
  27.2 1.8 %collective-permute-start.8 = (f32[2,16,16,256]{3,2,1,0:T(8,128)S(1)}, f32[2,16,16,256]{3,2,1,0:T(8,128)S(1)}, u32[]{:S(2)}, u32[]{:S(2)}) collective-permute-start(f32[2,16,16,256]{3,2,1,0:T(8,128)S(1)} %get-tuple-element.26.refs_4_), channel_id=1, source_target_pairs={{0,2},{1,3},{2,0},{3,1},{4,6},{5,7},{6,4},{7,5},{8,10},{9,11},{10,... | collective-permute-start | bytes 1572872 | tf_op jit(solution)/shard_map/ppermute | solution.py:439
  29.0 0.0 collective-permute-done.6.refs_1_.refs_3_
  29.0 7.0 %gram.1 = f32[32,17,1,128]{3,2,1,0:T(1,128)} custom-call(s32[64]{0:T(128)S(1)} %bitcast.2, s32[16]{0:T(128)S(1)} %get-tuple-element.21.slots, f32[18,16,256]{2,1,0:T(8,128)S(1)} %collective-permute-done.5.refs_0_.refs_2_, f32[18,16,256]{2,1,0:T(8,128)S(1)} %collective-permute-done.6.refs_1_.refs_3_, s32[4,64,128]{2,1,0:T(8,128)S(1)} %copy-done.4, ...), custom_call_target="tpu_custom_call" | custom-call | flops 4294967296 | bytes 1179648 | tf_op jit(solution)/shard_map/gram/pallas_call | solution.py:509
  35.9 0.0 copy-start.1
  35.9 0.7 %copy-done.1 = f32[18,16,256]{2,1,0:T(8,128)} copy-done((f32[18,16,256]{2,1,0:T(8,128)}, f32[18,16,256]{2,1,0:T(8,128)S(1)}, u32[]{:S(2)}) %copy-start.1) | copy-done | bytes 294936
  36.7 3.4 %all-to-all-start = ((f32[32,17,1,128]{3,2,1,0:T(1,128)}), f32[32,17,1,128]{3,2,1,0:T(1,128)S(1)}, u32[]{:S(2)}, u32[]{:S(2)}) async-start(f32[32,17,1,128]{3,2,1,0:T(1,128)} %gram.1), calls=%async_computation | async-start | bytes 557056 | tf_op jit(solution)/shard_map/all_to_all | solution.py:523
  40.1 0.3 collective-permute-start.7
  40.4 1.2 %collective-permute-done.8.refs_6_ = f32[2,16,16,256]{3,2,1,0:T(8,128)S(1)} collective-permute-done((f32[2,16,16,256]{3,2,1,0:T(8,128)S(1)}, f32[2,16,16,256]{3,2,1,0:T(8,128)S(1)}, u32[]{:S(2)}, u32[]{:S(2)}) %collective-permute-start.8) | collective-permute-done | bytes 524320 | tf_op jit(solution)/shard_map/ppermute | solution.py:439
  41.6 0.0 collective-permute-start.9
  41.6 0.5 collective-permute-done.7.refs_5_
  42.0 9.1 %all-to-all-done.sums = f32[32,17,1,128]{3,2,1,0:T(1,128)S(1)} async-done(((f32[32,17,1,128]{3,2,1,0:T(1,128)}), f32[32,17,1,128]{3,2,1,0:T(1,128)S(1)}, u32[]{:S(2)}, u32[]{:S(2)}) %all-to-all-start) | async-done | bytes 278560 | tf_op jit(solution)/shard_map/all_to_all | solution.py:523
  51.2 0.0 collective-permute-done.9.refs_7_
  51.2 0.0 copy-start.2
  51.2 1.0 %copy-done.2 = f32[18,16,256]{2,1,0:T(8,128)S(1)} copy-done((f32[18,16,256]{2,1,0:T(8,128)S(1)}, f32[18,16,256]{2,1,0:T(8,128)}, u32[]{:S(2)}) %copy-start.2) | copy-done | bytes 294936
  52.1 4.3 %analysis.1 = f32[16,3,16,256]{3,2,1,0:T(8,128)} custom-call(f32[32,17,1,128]{3,2,1,0:T(1,128)S(1)} %all-to-all-done.sums, f32[18,16,256]{2,1,0:T(8,128)S(1)} %get-tuple-element.20.refs_0_, f32[18,16,256]{2,1,0:T(8,128)S(1)} %collective-permute-done.4.refs_1_, f32[18,16,256]{2,1,0:T(8,128)S(1)} %collective-permute-done.5.refs_0_.refs_2_, ...), custom_call_target="tpu_custom_call" | custom-call | tf_op jit(solution)/shard_map/analysis/pallas_call | solution.py:525
Async XLA Ops:
  0.0 13.5 %copy-start.3 = (f32[16,256]{1,0:T(8,128)S(1)}, f32[16,256]{1,0:T(8,128)}, u32[]{:S(2)}) copy-start(f32[16,256]{1,0:T(8,128)} %depth.3) | copy-start | bytes 49156
  0.0 13.5 %copy-start = (f32[16,3,16,256]{3,2,1,0:T(8,128)S(1)}, f32[16,3,16,256]{3,2,1,0:T(8,128)}, u32[]{:S(2)}) copy-start(f32[16,3,16,256]{3,2,1,0:T(8,128)} %state.3) | copy-start | bytes 2359300
  2.2 11.4 %collective-permute-start = (f32[72,256]{1,0:T(8,128)}, f32[72,256]{1,0:T(8,128)S(1)}, u32[]{:S(2)}, u32[]{:S(2)}) collective-permute-start(f32[72,256]{1,0:T(8,128)} %get-tuple-element.16), channel_id=1, source_target_pairs={{0,4},{4,8},{8,12},{12,16},{16,20},{20,24},{24,28},{28,0},{1,5},{5... | collective-permute-start | bytes 221192 | tf_op jit(solution)/shard_map/ppermute | solution.py:460
  5.1 8.4 %collective-permute-start.1 = (f32[72,256]{1,0:T(8,128)}, f32[72,256]{1,0:T(8,128)S(1)}, u32[]{:S(2)}, u32[]{:S(2)}) collective-permute-start(f32[72,256]{1,0:T(8,128)} %get-tuple-element.17), channel_id=1, source_target_pairs={{4,0},{8,4},{12,8},{16,12},{20,16},{24,20},{28,24},{0,28},{5,1},{9... | collective-permute-start | bytes 221192 | tf_op jit(solution)/shard_map/ppermute | solution.py:459
  8.2 1.4 %collective-permute-start.2 = (f32[16,256]{1,0:T(8,128)}, f32[16,256]{1,0:T(8,128)S(1)}, u32[]{:S(2)}, u32[]{:S(2)}) collective-permute-start(f32[16,256]{1,0:T(8,128)} %get-tuple-element.18), channel_id=1, source_target_pairs={{0,0},{1,9},{2,18},{3,27},{4,4},{5,13},{6,22},{7,31},{8,8},{9,1},{... | collective-permute-start | bytes 49160 | tf_op jit(solution)/shard_map/ppermute | solution.py:462
  9.6 10.1 %copy-start.4 = (s32[4,64,128]{2,1,0:T(8,128)S(1)}, s32[4,64,128]{2,1,0:T(8,128)}, u32[]{:S(2)}) copy-start(s32[4,64,128]{2,1,0:T(8,128)} %refs_2_.3) | copy-start | bytes 393220
  9.6 10.1 %copy-start.5 = (f32[4,64,128]{2,1,0:T(8,128)S(1)}, f32[4,64,128]{2,1,0:T(8,128)}, u32[]{:S(2)}) copy-start(f32[4,64,128]{2,1,0:T(8,128)} %refs_3_.3) | copy-start | bytes 393220
  9.6 4.0 %collective-permute-start.3 = (f32[16,256]{1,0:T(8,128)}, f32[16,256]{1,0:T(8,128)S(1)}, u32[]{:S(2)}, u32[]{:S(2)}) collective-permute-start(f32[16,256]{1,0:T(8,128)} %get-tuple-element.19), channel_id=1, source_target_pairs={{0,4},{1,13},{2,22},{3,31},{4,0},{5,9},{6,18},{7,27},{8,12},{9,5},... | collective-permute-start | bytes 49160 | tf_op jit(solution)/shard_map/ppermute | solution.py:462
  14.5 5.1 %copy-start.6 = (s32[64,1]{0,1:T(1,128)S(1)}, s32[64,1]{0,1:T(1,128)}, u32[]{:S(2)}) copy-start(s32[64,1]{0,1:T(1,128)} %param.11) | copy-start | bytes 772
  14.5 5.1 %collective-permute-start.4 = (f32[18,16,256]{2,1,0:T(8,128)S(1)}, f32[18,16,256]{2,1,0:T(8,128)S(1)}, u32[]{:S(2)}, u32[]{:S(2)}) collective-permute-start(f32[18,16,256]{2,1,0:T(8,128)S(1)} %get-tuple-element.20.refs_0_), channel_id=1, source_target_pairs={{0,1},{1,0},{2,3},{3,2},{4,5},{5,4},{6,7},{7,6},{8,9},{9,8},{10,11... | collective-permute-start | bytes 884744 | tf_op jit(solution)/shard_map/ppermute | solution.py:439
  14.6 12.6 %collective-permute-start.5 = (f32[18,16,256]{2,1,0:T(8,128)S(1)}, f32[18,16,256]{2,1,0:T(8,128)S(1)}, u32[]{:S(2)}, u32[]{:S(2)}) collective-permute-start(f32[18,16,256]{2,1,0:T(8,128)S(1)} %get-tuple-element.20.refs_0_), channel_id=1, source_target_pairs={{0,2},{1,3},{2,0},{3,1},{4,6},{5,7},{6,4},{7,5},{8,10},{9,11},{10,... | collective-permute-start | bytes 884744 | tf_op jit(solution)/shard_map/ppermute | solution.py:439
  27.2 1.8 %collective-permute-start.6 = (f32[18,16,256]{2,1,0:T(8,128)S(1)}, f32[18,16,256]{2,1,0:T(8,128)S(1)}, u32[]{:S(2)}, u32[]{:S(2)}) collective-permute-start(f32[18,16,256]{2,1,0:T(8,128)S(1)} %collective-permute-done.5.refs_0_.refs_2_), channel_id=1, source_target_pairs={{0,1},{1,0},{2,3},{3,2},{4,5},{5,4},{6,7},{7,6},{8,9},{9,8},{10,11... | collective-permute-start | bytes 884744 | tf_op jit(solution)/shard_map/ppermute | solution.py:439
  27.2 14.4 %collective-permute-start.8 = (f32[2,16,16,256]{3,2,1,0:T(8,128)S(1)}, f32[2,16,16,256]{3,2,1,0:T(8,128)S(1)}, u32[]{:S(2)}, u32[]{:S(2)}) collective-permute-start(f32[2,16,16,256]{3,2,1,0:T(8,128)S(1)} %get-tuple-element.26.refs_4_), channel_id=1, source_target_pairs={{0,2},{1,3},{2,0},{3,1},{4,6},{5,7},{6,4},{7,5},{8,10},{9,11},{10,... | collective-permute-start | bytes 1572872 | tf_op jit(solution)/shard_map/ppermute | solution.py:439
  35.9 0.7 %copy-start.1 = (f32[18,16,256]{2,1,0:T(8,128)}, f32[18,16,256]{2,1,0:T(8,128)S(1)}, u32[]{:S(2)}) copy-start(f32[18,16,256]{2,1,0:T(8,128)S(1)} %collective-permute-done.6.refs_1_.refs_3_) | copy-start | bytes 884740
  36.7 14.5 %all-to-all-start = ((f32[32,17,1,128]{3,2,1,0:T(1,128)}), f32[32,17,1,128]{3,2,1,0:T(1,128)S(1)}, u32[]{:S(2)}, u32[]{:S(2)}) async-start(f32[32,17,1,128]{3,2,1,0:T(1,128)} %gram.1), calls=%async_computation | async-start | bytes 557056 | tf_op jit(solution)/shard_map/all_to_all | solution.py:523
  40.1 2.0 %collective-permute-start.7 = (f32[2,16,16,256]{3,2,1,0:T(8,128)S(1)}, f32[2,16,16,256]{3,2,1,0:T(8,128)S(1)}, u32[]{:S(2)}, u32[]{:S(2)}) collective-permute-start(f32[2,16,16,256]{3,2,1,0:T(8,128)S(1)} %get-tuple-element.26.refs_4_), channel_id=1, source_target_pairs={{0,1},{1,0},{2,3},{3,2},{4,5},{5,4},{6,7},{7,6},{8,9},{9,8},{10,11... | collective-permute-start | bytes 1572872 | tf_op jit(solution)/shard_map/ppermute | solution.py:439
  41.6 9.6 %collective-permute-start.9 = (f32[2,16,16,256]{3,2,1,0:T(8,128)S(1)}, f32[2,16,16,256]{3,2,1,0:T(8,128)S(1)}, u32[]{:S(2)}, u32[]{:S(2)}) collective-permute-start(f32[2,16,16,256]{3,2,1,0:T(8,128)S(1)} %collective-permute-done.8.refs_6_), channel_id=1, source_target_pairs={{0,1},{1,0},{2,3},{3,2},{4,5},{5,4},{6,7},{7,6},{8,9},{9,8},{10,11... | collective-permute-start | bytes 1572872 | tf_op jit(solution)/shard_map/ppermute | solution.py:439
  51.2 1.0 %copy-start.2 = (f32[18,16,256]{2,1,0:T(8,128)S(1)}, f32[18,16,256]{2,1,0:T(8,128)}, u32[]{:S(2)}) copy-start(f32[18,16,256]{2,1,0:T(8,128)} %copy-done.1) | copy-start | bytes 884740

commit v4 on v3

--- a/solution.py
+++ b/solution.py
@@ -13,6 +13,7 @@
 turn_rate = 0.1
 
 VMEM = pl.BlockSpec(memory_space=pltpu.VMEM)
+HBM = pl.BlockSpec(memory_space=pltpu.HBM)
 SMEM = pl.BlockSpec(memory_space=pltpu.SMEM)
 F32 = jnp.float32
 BF16 = jnp.bfloat16
@@ -29,9 +30,37 @@
     return pltpu.roll(field, width - 1, 1) - pltpu.roll(field, 1, 1)
 
 
-def edge_kernel(peers, state, depth, values, precision, above, below, *held):
+def far_shift(index):
+    half = 2 + index // 2
+    return half - 2 * half * (index % 2)
+
+
+def edge_kernel(state_in, depth_in, values, precision, above, below, own, *refs):
+    peers = len(refs) - 5
+    held = refs[:peers]
+    state, depth, seen, weight, sems = refs[peers:]
     members, _, rows, cols = state.shape
     width = values.shape[-1]
+    half = members // 2
+    copies = [
+        pltpu.make_async_copy(state_in.at[0:half], state.at[0:half], sems.at[0]),
+        pltpu.make_async_copy(state_in.at[half:members], state.at[half:members], sems.at[1]),
+        pltpu.make_async_copy(depth_in, depth, sems.at[2]),
+    ]
+    place, count = lax.axis_index("space"), values.shape[1]
+    peers_of = [place, lax.rem(place + count - 1, count), lax.rem(place + 1, count)]
+    for j in range(peers):
+        index = j * lax.axis_size("mem") + lax.axis_index("mem")
+        half = 2 + lax.div(index, 2)
+        shift = half - 2 * half * lax.rem(index, 2)
+        peers_of.append(lax.rem(place + 2 * count - shift, count))
+    for j, peer in enumerate(peers_of):
+        copies.append(pltpu.make_async_copy(values.at[0, peer], seen.at[j], sems.at[3 + 2 * j]))
+        copies.append(pltpu.make_async_copy(precision.at[0, peer], weight.at[j], sems.at[4 + 2 * j]))
+    for copy in copies:
+        copy.start()
+    for copy in copies:
+        copy.wait()
     for out, sign, at in ((above, 1.0, range(4)), (below, -1.0, range(rows - 1, rows - 5, -1))):
         deep = [jnp.broadcast_to(depth[t : t + 1], (members, cols)) for t in at]
         h = [state[:, 0, t, :] for t in at]
@@ -54,28 +83,39 @@
         out[4 * members : 4 * members + 8] = jnp.concatenate(
             [deep[0][0:1], deep[1][0:1], jnp.zeros((6, cols), F32)], axis=0
         )
-    for j, out in enumerate(held):
-        peer = lax.bitwise_xor(lax.axis_index("space"), peers * lax.axis_index("mem") + j)
-        out[:, 0:width] = values[0, peer]
-        out[:, width : 2 * width] = precision[0, peer]
+    rim = 4 * members + 8
+    slots = seen.shape[1]
+    places = [own, above.at[rim : rim + slots], below.at[rim : rim + slots]] + list(held)
+    for j, out in enumerate(places):
+        out[:, 0:width] = seen[j]
+        out[:, width : 2 * width] = weight[j]
 
 
 def edges(peers, state, depth, values, precision):
     members, _, _, cols = state.shape
-    rim = jax.ShapeDtypeStruct((4 * members + 8, cols), F32)
-    held = jax.ShapeDtypeStruct((values.shape[2], cols), F32)
+    slots = values.shape[2]
+    rim = jax.ShapeDtypeStruct((4 * members + 8 + slots, cols), F32)
+    held = jax.ShapeDtypeStruct((slots, cols), F32)
     return pl.pallas_call(
-        functools.partial(edge_kernel, peers),
-        out_shape=(rim, rim) + (held,) * peers,
-        in_specs=[VMEM] * 4,
-        out_specs=(VMEM,) * (2 + peers),
+        edge_kernel,
+        out_shape=(rim, rim, held) + (held,) * peers,
+        in_specs=[HBM] * 4,
+        out_specs=(VMEM,) * (3 + peers),
+        scratch_shapes=[
+            pltpu.VMEM(state.shape, F32),
+            pltpu.VMEM(depth.shape, F32),
+            pltpu.VMEM((3 + peers,) + values.shape[2:], F32),
+            pltpu.VMEM((3 + peers,) + values.shape[2:], F32),
+            pltpu.SemaphoreType.DMA((9 + 2 * peers,)),
+        ],
+        compiler_params=pltpu.CompilerParams(vmem_limit_bytes=56 * 1024 * 1024),
         name="edges",
     )(state, depth, values, precision)
 
 
 def forecast_kernel(last, state, depth, above, below, *refs):
-    held = refs[:-6]
-    height_out, wind_out, h, u, v, flux = refs[-6:]
+    held = refs[:-7]
+    height_out, east_out, north_out, h, u, v, flux = refs[-7:]
     members, _, rows, cols = state.shape
     slots = held[0].shape[0]
     deep = [jnp.broadcast_to(depth[t : t + 1], (members, cols)) for t in range(rows)]
@@ -123,8 +163,8 @@
         flux[t + 1] = deep[t] * east
 
     def emit(t, east, north):
-        wind_out[0, t] = east
-        wind_out[1, t] = north
+        east_out[t] = east
+        north_out[t] = north
 
     new_heights()
     for delta, ((_, first, east, _), deeps, sign, edge, inside) in zip(deltas, sides):
@@ -154,10 +194,11 @@
         functools.partial(forecast_kernel, last),
         out_shape=(
             jax.ShapeDtypeStruct((rows + extra, members, cols), F32),
-            jax.ShapeDtypeStruct((2, rows, members, cols), F32),
+            jax.ShapeDtypeStruct((rows, members, cols), F32),
+            jax.ShapeDtypeStruct((rows, members, cols), F32),
         ),
         in_specs=[VMEM] * (4 + len(held)),
-        out_specs=(VMEM, VMEM),
+        out_specs=(VMEM, VMEM, VMEM),
         scratch_shapes=[
             pltpu.VMEM((rows + 2, members, cols), F32),
             pltpu.VMEM((rows, members, cols), F32),
@@ -227,10 +268,17 @@
 
 def predict_kernel(count, owners, *refs):
     pieces = refs[:count]
-    cells, weights, out, near, slots, split, used = refs[count:]
+    cells, weights, own, above, below, out, near, slots, spots, split, used = refs[count:]
     share = slots.shape[0]
-    collect(near, pieces, split)
-    begin = lax.axis_index("mem") * share
+    near[0] = own[...]
+    rim = below.shape[0] - own.shape[0]
+    near[1] = below[rim:]
+    near[2] = above[rim:]
+    collect(near.at[3:], pieces, split)
+    peers = (near.shape[0] - 3) // count
+    space, quarter = lax.axis_index("space"), lax.axis_index("mem")
+    spaces, quarters = used.shape[0], lax.axis_size("mem")
+    begin = quarter * share
     for owner in range(used.shape[0]):
         used[owner] = 0
 
@@ -243,6 +291,12 @@
         owner = owners[begin + i]
         slots[i] = used[owner]
         used[owner] += 1
+        apart = lax.rem(owner + spaces - space, spaces)
+        index = jnp.where(apart <= spaces // 2, 2 * (apart - 2), 2 * (spaces - apart - 2) + 1)
+        who = lax.rem(index, quarters)
+        spot = 3 + lax.bitwise_xor(who, quarter) * peers + lax.div(index, quarters)
+        spot = jnp.where(apart <= 1, apart, spot)
+        spots[i] = jnp.where(apart == spaces - 1, 2, spot)
 
     def put(b, result):
         out[b] = result
@@ -250,15 +304,14 @@
     interpolate(pieces, cells, weights, split, put)
 
 
-def gram_kernel(scale, count, count_mem, owners, slots, *refs):
+def gram_kernel(scale, count, count_mem, spots, slots, *refs):
     pieces = refs[:count]
-    cells, weights, near, early, out, split, lined, got = refs[count:]
+    cells, weights, near, early, keep, give, split, lined, got = refs[count:]
     _, members, cols = pieces[0].shape
     total = members * count_mem
     part = members * count
     blocks, width = slots.shape[0], cells.shape[2]
     quarter = lax.axis_index("mem")
-    peers = near.shape[0] // count
     got[0 : near.shape[0]] = near[...]
     collect(got.at[near.shape[0] :], pieces, split)
 
@@ -274,8 +327,7 @@
     interpolate(pieces, cells, weights, split, put)
     lined[total : 2 * total] = jnp.zeros((total, blocks * width), F32)
     for b in range(blocks):
-        apart = lax.bitwise_xor(owners[quarter * blocks + b], lax.axis_index("space"))
-        line = got[lax.bitwise_xor(apart, quarter * peers), pl.ds(slots[b], 1)]
+        line = got[spots[b], pl.ds(slots[b], 1)]
         seen, much = line[:, 0:width], line[:, width : 2 * width] * scale
         at = pl.ds(b * width, width)
         values = lined[0:total, at]
@@ -291,10 +343,18 @@
     cross = lax.dot_general(high, low, turned, preferred_element_type=F32)
     gram = gram + (cross + cross.T)
     packed = pack_gram(gram, total)
-    spread = out.shape[1]
+    half = keep.shape[0]
+    odd = lax.rem(quarter, 2) == 1
+    for r in range(half):
+        low, high = packed[r : r + 1], packed[half + r : half + r + 1]
+        keep[r] = jnp.where(odd, high, low)
+        give[r] = jnp.where(odd, low, high)
+
+
+def spread_kernel(keep, given, out):
+    both = keep[...] + given[...]
     for d in range(out.shape[0]):
-        for r in range(spread):
-            out[d, r] = packed[r : r + 1]
+        out[d] = both
 
 
 def pack_gram(gram, total):
@@ -410,24 +470,22 @@
 
 
 def analysis_kernel(count_mem, sums, *refs):
-    heights = refs[:count_mem]
-    winds = refs[count_mem : 2 * count_mem]
-    out, lower = refs[2 * count_mem :]
-    _, members, cols = heights[0].shape
-    rows = winds[0].shape[1]
+    fields = [refs[f * count_mem : (f + 1) * count_mem] for f in range(3)]
+    out, lower = refs[3 * count_mem :]
+    rows, members, cols = fields[1][0].shape
     total = members * count_mem
 
-    packed = sums[0]
-    for d in range(1, sums.shape[0]):
-        packed = packed + sums[d]
-    packed = jnp.concatenate([packed[r] for r in range(packed.shape[0])], axis=0)
+    halves = [sums[0], sums[1]]
+    for d in range(2, sums.shape[0]):
+        halves[d % 2] = halves[d % 2] + sums[d]
+    packed = jnp.concatenate([half[r] for half in halves for r in range(half.shape[0])], axis=0)
     mixing = mixing_columns(packed, total, members, count_mem, lower)
     high = mixing.astype(BF16)
     low = (mixing - high.astype(F32)).astype(BF16)
     left = jnp.concatenate([high, high, low], axis=1)
     for field in range(3):
         for r in range(rows):
-            pieces = [heights[k][r] if field == 0 else winds[k][field - 1, r] for k in range(count_mem)]
+            pieces = [piece[r] for piece in fields[field]]
             upper = [x.astype(BF16) for x in pieces]
             rest = [(x - y.astype(F32)).astype(BF16) for x, y in zip(pieces, upper)]
             stack = jnp.concatenate(upper + rest + upper, axis=0)
@@ -452,9 +510,9 @@
     share = blocks // count_mem
     scale = math.sqrt((total - 1) / (count * blocks * width))
 
-    peers = count // count_mem
-
-    to_above, to_below, *held = edges(peers, state, depth, obs_values, obs_precision)
+    peers = -(-(count - 3) // count_mem)
+
+    to_above, to_below, own, *held = edges(peers, state, depth, obs_values, obs_precision)
     ends = count - 1
     below = lax.ppermute(to_above, "space", [((i + 1) % count, i) for i in range(count)])
     above = lax.ppermute(to_below, "space", [(i, (i + 1) % count) for i in range(count)])
@@ -463,14 +521,15 @@
             piece,
             ("space", "mem"),
             [
-                (s * count_mem + q, (s ^ (peers * q + j)) * count_mem + q)
+                (s * count_mem + q, (s - far_shift(j * count_mem + q)) % count * count_mem + q)
                 for s in range(count)
                 for q in range(count_mem)
+                if j * count_mem + q < count - 3
             ],
         )
         for j, piece in enumerate(held)
     ]
-    height, wind = forecast(ends, state, depth, above, below, held)
+    height, *parts = forecast(ends, state, depth, above, below, held)
 
     near, far = 1, count_mem // 2
     early_shape = (share, far * members, width)
@@ -478,54 +537,66 @@
     flops = 4 * obs_cells.shape[0] * share * width * rows * members * far * cols
     owners = owner_map[:, 0]
     heights = {0: height}
-    winds = {0: wind}
+    winds = [{0: part} for part in parts]
     heights[far] = swap(height, "mem", far)
     heights[near] = swap(height, "mem", near)
-    near_shape = (far * peers, obs_values.shape[2], cols)
-    early, first, slots = pl.pallas_call(
+    near_shape = (3 + far * peers, obs_values.shape[2], cols)
+    early, first, slots, spots = pl.pallas_call(
         functools.partial(predict_kernel, far),
         out_shape=(
             jax.ShapeDtypeStruct(early_shape, F32),
             jax.ShapeDtypeStruct(near_shape, F32),
             jax.ShapeDtypeStruct((share,), jnp.int32),
+            jax.ShapeDtypeStruct((share,), jnp.int32),
         ),
-        in_specs=[SMEM] + [VMEM] * (far + 2),
-        out_specs=(VMEM, VMEM, SMEM),
+        in_specs=[SMEM] + [VMEM] * (far + 5),
+        out_specs=(VMEM, VMEM, SMEM, SMEM),
         scratch_shapes=[split, pltpu.SMEM((count,), jnp.int32)],
         compiler_params=PARAMS,
         cost_estimate=cost(flops, 4 * height.size * far),
         name="predict",
-    )(owners, heights[0], heights[near], obs_cells, obs_weights)
+    )(owners, heights[0], heights[near], obs_cells, obs_weights, own, above, below)
     heights[far] = after(heights[far], early)
     heights[far + near] = swap(heights[far], "mem", near)
-    winds[far] = swap(after(wind, heights[far]), "mem", far)
-    winds[near] = swap(wind, "mem", near)
-    winds[far + near] = swap(winds[far], "mem", near)
+    for wind in winds:
+        wind[far] = swap(after(wind[0], heights[far]), "mem", far)
+        wind[near] = swap(wind[0], "mem", near)
+    for wind in winds:
+        wind[far + near] = swap(wind[far], "mem", near)
     heights = [heights[k] for k in range(count_mem)]
-    winds = [winds[k] for k in range(count_mem)]
-
-    spread = total // 4 + 1
+    winds = [wind[k] for wind in winds for k in range(count_mem)]
+
+    half = (total // 4 + 2) // 2
     devices = count * count_mem
-    sent = pl.pallas_call(
+    part = jax.ShapeDtypeStruct((half, 1, 2 * total), F32)
+    keep, give = pl.pallas_call(
         functools.partial(gram_kernel, scale, far, count_mem),
-        out_shape=jax.ShapeDtypeStruct((devices, spread, 1, 2 * total), F32),
+        out_shape=(part, part),
         in_specs=[SMEM, SMEM] + [VMEM] * (far + 4),
-        out_specs=VMEM,
+        out_specs=(VMEM, VMEM),
         scratch_shapes=[
             split,
             pltpu.VMEM((2 * total, share * width), F32),
-            pltpu.VMEM((count,) + near_shape[1:], F32),
+            pltpu.VMEM((3 + count_mem * peers,) + near_shape[1:], F32),
         ],
         compiler_params=PARAMS,
         cost_estimate=cost(flops, 4 * height.size * count_mem),
         name="gram",
-    )(owners, slots, *heights[far:], obs_cells, obs_weights, first, early)
+    )(spots, slots, *heights[far:], obs_cells, obs_weights, first, early)
+    sent = pl.pallas_call(
+        spread_kernel,
+        out_shape=jax.ShapeDtypeStruct((devices,) + part.shape, F32),
+        in_specs=[VMEM, VMEM],
+        out_specs=VMEM,
+        compiler_params=PARAMS,
+        name="spread",
+    )(keep, swap(give, "mem", near))
     sums = lax.all_to_all(sent, ("space", "mem"), split_axis=0, concat_axis=0, tiled=True)
 
     return pl.pallas_call(
         functools.partial(analysis_kernel, count_mem),
         out_shape=jax.ShapeDtypeStruct(state.shape, F32),
-        in_specs=[VMEM] * (1 + 2 * count_mem),
+        in_specs=[VMEM] * (1 + 3 * count_mem),
         out_specs=VMEM,
         scratch_shapes=[pltpu.VMEM((total, 2 * total), F32)],
         compiler_params=PARAMS,

time: 56.7 us -> 53.3 us (0.940)
  starting transfers between devices: 18 us -> 15.5 us
  local copies, waits for them, and re-layouts: 1.7 us -> 0.66 us
    ppermute x6 -> x10, starting transfers between devices: 7.19 us -> 2.9 us  [swap(): return lax.ppermute(x, axis, [(i, i ^ bit) for i in range(count)])]
    all_to_all x1, waiting for transfers between devices: 9.12 us -> 5.31 us  [local(): lax.all_to_all(sent, ('space', 'mem'), split_axis=0, concat_axis=0, tiled...]
    ppermute x6 -> x10, waiting for transfers between devices: 3.64 us -> 6.51 us  [swap(): return lax.ppermute(x, axis, [(i, i ^ bit) for i in range(count)])]
    ppermute x2, starting transfers between devices: 1.37 us -> 3.97 us  [local(): lax.ppermute(piece, ('space', 'mem'), [(s * count_mem + q, (s - far_shift...]
    unnamed x14 -> x12, local copies, waits for them, and re-layouts: 1.7 us -> 0.66 us
    ppermute x2, waiting for transfers between devices: 3.95 us -> 4.81 us  [local(): lax.ppermute(piece, ('space', 'mem'), [(s * count_mem + q, (s - far_shift...]
    pallas_call x1 -> x2, Pallas kernels: 2.15 us -> 3 us  [the longest x1 2.26 us: edges(): pl.pallas_call(edge_kernel, out_shape=(rim, rim, held) + (held,) * peers,...]
    all_to_all x1, starting transfers between devices: 3.41 us -> 2.58 us  [local(): lax.all_to_all(sent, ('space', 'mem'), split_axis=0, concat_axis=0, tiled...]
  transfers between devices with their start and end apart: 11 -> 15, of which waited for: 5 -> 9; matrix products, arithmetic and copies ran while one was open for 0% -> 0% of each run, Pallas kernels for 22% -> 24%
where the time goes in v4:
time: 53.3 us; the launch traced here: 53 us
  Pallas kernels  20.1 us (38%)
  waiting for transfers between devices  16.6 us (31%)
  starting transfers between devices  15.5 us (29%)
  local copies, waits for them, and re-layouts  0.66 us (1%)
    ppermute x10, waiting for transfers between devices, swap(): return lax.ppermute(x, axis, [(i, i ^ bit) for i in range(count)])  6.51 us
    pallas_call x1, Pallas kernels, local(): pl.pallas_call(functools.partial(gram_kernel, scale, far, count_mem), out...  6.21 us
    pallas_call x1, Pallas kernels, local(): pl.pallas_call(functools.partial(predict_kernel, far), out_shape=(jax.Sha...  5.73 us
    all_to_all x1, waiting for transfers between devices, local(): lax.all_to_all(sent, ('space', 'mem'), split_axis=0, concat_axis=0, tiled...  5.31 us
    ppermute x2, waiting for transfers between devices, local(): lax.ppermute(piece, ('space', 'mem'), [(s * count_mem + q, (s - far_shift...  4.81 us
    pallas_call x1, Pallas kernels, local(): pl.pallas_call(functools.partial(analysis_kernel, count_mem), out_shape=j...  4.22 us
    ppermute x2, starting transfers between devices, local(): lax.ppermute(piece, ('space', 'mem'), [(s * count_mem + q, (s - far_shift...  3.97 us
    ppermute x1, starting transfers between devices, local(): lax.ppermute(to_above, 'space', [((i + 1) % count, i) for i in range(coun...  3.1 us
  transfers between devices with their start and end apart: 15, of which 9 were waited for; matrix products, arithmetic and copies ran while one was open for 0% of the time, Pallas kernels for 24%

profile of v4, /device:TPU:0, one launch (start us, length us, event | category | flops | bytes accessed | tf_op | source)
XLA Modules:
  0.0 53.0 jit_solution(16951301170531298502)
XLA Ops:
  0.0 0.0 copy-start.1
  0.0 0.0 copy-start
  0.0 2.3 %edges.1 = (f32[88,256]{1,0:T(8,128)}, f32[88,256]{1,0:T(8,128)}, f32[16,256]{1,0:T(8,128)}, f32[16,256]{1,0:T(8,128)}, f32[16,256]{1,0:T(8,128)}) custom-call(f32[16,3,16,256]{3,2,1,0:T(8,128)} %state.1, f32[16,256]{1,0:T(8,128)} %depth.1, f32[1,8,16,128]{3,2,1,0:T(8,128)} %values.1, f32[1,8,16,128]{3,2,1,0:T(8,128)} %precision.1), custom_call_target="tpu_custom_call" | custom-call | tf_op jit(solution)/shard_map/edges/pallas_call | solution.py:99
  2.3 3.0 %collective-permute-start = (f32[88,256]{1,0:T(8,128)}, f32[88,256]{1,0:T(8,128)S(1)}, u32[]{:S(2)}, u32[]{:S(2)}) collective-permute-start(f32[88,256]{1,0:T(8,128)} %get-tuple-element.22), channel_id=1, source_target_pairs={{0,4},{4,8},{8,12},{12,16},{16,20},{20,24},{24,28},{28,0},{1,5},{5... | collective-permute-start | bytes 270344 | tf_op jit(solution)/shard_map/ppermute | solution.py:518
  5.3 3.1 %collective-permute-start.1 = (f32[88,256]{1,0:T(8,128)}, f32[88,256]{1,0:T(8,128)S(1)}, u32[]{:S(2)}, u32[]{:S(2)}) collective-permute-start(f32[88,256]{1,0:T(8,128)} %get-tuple-element.23), channel_id=1, source_target_pairs={{4,0},{8,4},{12,8},{16,12},{20,16},{24,20},{28,24},{0,28},{5,1},{9... | collective-permute-start | bytes 270344 | tf_op jit(solution)/shard_map/ppermute | solution.py:517
  8.4 1.9 %collective-permute-start.2 = (f32[16,256]{1,0:T(8,128)}, f32[16,256]{1,0:T(8,128)S(1)}, u32[]{:S(2)}, u32[]{:S(2)}) collective-permute-start(f32[16,256]{1,0:T(8,128)} %get-tuple-element.24), channel_id=1, source_target_pairs={{0,24},{1,9},{2,22},{3,15},{4,28},{5,13},{6,26},{7,19},{8,0},{9,17... | collective-permute-start | bytes 49160 | tf_op jit(solution)/shard_map/ppermute | solution.py:520
  10.3 0.0 copy-start.2
  10.3 0.0 copy-start.3
  10.3 0.0 copy-start.4
  10.3 2.0 %collective-permute-start.3 = (f32[16,256]{1,0:T(8,128)}, f32[16,256]{1,0:T(8,128)S(1)}, u32[]{:S(2)}, u32[]{:S(2)}) collective-permute-start(f32[16,256]{1,0:T(8,128)} %get-tuple-element.25), channel_id=1, source_target_pairs={{0,16},{4,20},{8,24},{12,28},{16,0},{20,4},{24,8},{28,12}} | collective-permute-start | bytes 49160 | tf_op jit(solution)/shard_map/ppermute | solution.py:520
  12.4 0.0 collective-permute-done.2.refs_0_
  12.4 4.8 %collective-permute-done.3.refs_1_ = f32[16,256]{1,0:T(8,128)S(1)} collective-permute-done((f32[16,256]{1,0:T(8,128)}, f32[16,256]{1,0:T(8,128)S(1)}, u32[]{:S(2)}, u32[]{:S(2)}) %collective-permute-start.3) | collective-permute-done | bytes 16416 | tf_op jit(solution)/shard_map/ppermute | solution.py:520
  17.2 0.0 collective-permute-done.above.refs_5_
  17.2 0.0 collective-permute-done.1.below.refs_6_
  17.2 0.0 copy-done.1
  17.2 0.0 copy-done
  17.2 0.9 %forecast.1 = (f32[18,16,256]{2,1,0:T(8,128)S(1)}, f32[16,16,256]{2,1,0:T(8,128)S(1)}, f32[16,16,256]{2,1,0:T(8,128)S(1)}) custom-call(f32[16,3,16,256]{3,2,1,0:T(8,128)S(1)} %copy-done, f32[16,256]{1,0:T(8,128)S(1)} %copy-done.1, f32[88,256]{1,0:T(8,128)S(1)} %collective-permute-done.above.refs_5_, f32[88,256]{1,0:T(8,128)S(1)} %collective-permute-done.1.below.refs_6_, ...), custom_call_target="tpu_custom_call" | custom-call | flops 2000000000 | bytes 786432 | tf_op jit(solution)/shard_map/forecast/pallas_call | solution.py:193
  18.1 0.1 collective-permute-start.4
  18.2 0.1 collective-permute-start.5
  18.3 1.5 %collective-permute-done.4.refs_1_ = f32[18,16,256]{2,1,0:T(8,128)S(1)} collective-permute-done((f32[18,16,256]{2,1,0:T(8,128)S(1)}, f32[18,16,256]{2,1,0:T(8,128)S(1)}, u32[]{:S(2)}, u32[]{:S(2)}) %collective-permute-start.4) | collective-permute-done | bytes 294944 | tf_op jit(solution)/shard_map/ppermute | solution.py:497
  19.8 0.0 copy-start.5
  19.8 0.0 copy-done.2
  19.8 0.0 copy-done.3
  19.8 0.0 copy-done.4
  19.8 0.6 %copy-done.5 = s32[64,1]{0,1:T(1,128)S(1)} copy-done((s32[64,1]{0,1:T(1,128)S(1)}, s32[64,1]{0,1:T(1,128)}, u32[]{:S(2)}) %copy-start.5) | copy-done | bytes 280
  20.4 5.7 %predict.1 = (f32[16,32,128]{2,1,0:T(8,128)S(1)}, f32[7,16,256]{2,1,0:T(8,128)S(1)}, s32[16]{0:T(128)S(1)}, s32[16]{0:T(128)S(1)}) custom-call(s32[64]{0:T(128)S(1)} %bitcast.1, f32[18,16,256]{2,1,0:T(8,128)S(1)} %get-tuple-element.26.refs_0_, f32[18,16,256]{2,1,0:T(8,128)S(1)} %collective-permute-done.4.refs_1_, s32[4,64,128]{2,1,0:T(8,128)S(1)} %copy-done.2, ...), custom_call_target="tpu_custom_call" | custom-call | flops 4294967296 | bytes 589824 | tf_op jit(solution)/shard_map/predict/pallas_call | solution.py:544
  26.2 1.5 %collective-permute-done.5.refs_0_.refs_2_ = f32[18,16,256]{2,1,0:T(8,128)S(1)} collective-permute-done((f32[18,16,256]{2,1,0:T(8,128)S(1)}, f32[18,16,256]{2,1,0:T(8,128)S(1)}, u32[]{:S(2)}, u32[]{:S(2)}) %collective-permute-start.5) | collective-permute-done | bytes 294944 | tf_op jit(solution)/shard_map/ppermute | solution.py:497
  27.6 0.0 collective-permute-start.6
  27.6 0.3 collective-permute-start.9
  27.9 1.8 %collective-permute-start.12 = (f32[16,16,256]{2,1,0:T(8,128)S(1)}, f32[16,16,256]{2,1,0:T(8,128)S(1)}, u32[]{:S(2)}, u32[]{:S(2)}) collective-permute-start(f32[16,16,256]{2,1,0:T(8,128)S(1)} %get-tuple-element.38.refs_8_), channel_id=1, source_target_pairs={{0,2},{1,3},{2,0},{3,1},{4,6},{5,7},{6,4},{7,5},{8,10},{9,11},{10,... | collective-permute-start | bytes 786440 | tf_op jit(solution)/shard_map/ppermute | solution.py:497
  29.7 0.0 collective-permute-done.6.refs_1_.refs_3_
  29.7 6.2 %gram.1 = (f32[9,1,128]{2,1,0:T(1,128)S(1)}, f32[9,1,128]{2,1,0:T(1,128)S(1)}) custom-call(s32[16]{0:T(128)S(1)} %get-tuple-element.28.spots, s32[16]{0:T(128)S(1)} %get-tuple-element.29.slots, f32[18,16,256]{2,1,0:T(8,128)S(1)} %collective-permute-done.5.refs_0_.refs_2_, f32[18,16,256]{2,1,0:T(8,128)S(1)} %collective-permute-done.6.refs_1_.refs_3_, ...), custom_call_target="tpu_custom_call" | custom-call | flops 4294967296 | bytes 1179648 | tf_op jit(solution)/shard_map/gram/pallas_call | solution.py:572
  35.9 0.0 collective-permute-start.7
  35.9 1.2 %collective-permute-done.7.given = f32[9,1,128]{2,1,0:T(1,128)S(1)} collective-permute-done((f32[9,1,128]{2,1,0:T(1,128)S(1)}, f32[9,1,128]{2,1,0:T(1,128)S(1)}, u32[]{:S(2)}, u32[]{:S(2)}) %collective-permute-start.7) | collective-permute-done | bytes 4640 | tf_op jit(solution)/shard_map/ppermute | solution.py:497
  37.1 0.7 %spread.1 = f32[32,9,1,128]{3,2,1,0:T(1,128)} custom-call(f32[9,1,128]{2,1,0:T(1,128)S(1)} %get-tuple-element.33.keep, f32[9,1,128]{2,1,0:T(1,128)S(1)} %collective-permute-done.7.given), custom_call_target="tpu_custom_call" | custom-call | tf_op jit(solution)/shard_map/spread/pallas_call | solution.py:586
  37.8 2.6 %all-to-all-start = ((f32[32,9,1,128]{3,2,1,0:T(1,128)}), f32[32,9,1,128]{3,2,1,0:T(1,128)S(1)}, u32[]{:S(2)}, u32[]{:S(2)}) async-start(f32[32,9,1,128]{3,2,1,0:T(1,128)} %spread.1), calls=%async_computation | async-start | bytes 294912 | tf_op jit(solution)/shard_map/all_to_all | solution.py:594
  40.4 0.2 collective-permute-start.8
  40.6 0.4 collective-permute-start.11
  41.0 0.0 collective-permute-done.9.refs_6_
  41.0 0.1 collective-permute-start.10
  41.1 0.9 %collective-permute-done.12.refs_10_ = f32[16,16,256]{2,1,0:T(8,128)S(1)} collective-permute-done((f32[16,16,256]{2,1,0:T(8,128)S(1)}, f32[16,16,256]{2,1,0:T(8,128)S(1)}, u32[]{:S(2)}, u32[]{:S(2)}) %collective-permute-start.12) | collective-permute-done | bytes 262176 | tf_op jit(solution)/shard_map/ppermute | solution.py:497
  42.0 0.0 collective-permute-start.13
  42.0 0.0 collective-permute-done.8.refs_5_
  42.0 0.4 collective-permute-done.11.refs_9_
  42.4 0.4 collective-permute-done.10.refs_7_
  42.7 0.8 %collective-permute-done.13.refs_11_ = f32[16,16,256]{2,1,0:T(8,128)S(1)} collective-permute-done((f32[16,16,256]{2,1,0:T(8,128)S(1)}, f32[16,16,256]{2,1,0:T(8,128)S(1)}, u32[]{:S(2)}, u32[]{:S(2)}) %collective-permute-start.13) | collective-permute-done | bytes 262176 | tf_op jit(solution)/shard_map/ppermute | solution.py:497
  43.5 5.3 %all-to-all-done.sums = f32[32,9,1,128]{3,2,1,0:T(1,128)S(1)} async-done(((f32[32,9,1,128]{3,2,1,0:T(1,128)}), f32[32,9,1,128]{3,2,1,0:T(1,128)S(1)}, u32[]{:S(2)}, u32[]{:S(2)}) %all-to-all-start) | async-done | bytes 147488 | tf_op jit(solution)/shard_map/all_to_all | solution.py:594
  48.8 4.2 %analysis.1 = f32[16,3,16,256]{3,2,1,0:T(8,128)} custom-call(f32[32,9,1,128]{3,2,1,0:T(1,128)S(1)} %all-to-all-done.sums, f32[18,16,256]{2,1,0:T(8,128)S(1)} %get-tuple-element.26.refs_0_, f32[18,16,256]{2,1,0:T(8,128)S(1)} %collective-permute-done.4.refs_1_, f32[18,16,256]{2,1,0:T(8,128)S(1)} %collective-permute-done.5.refs_0_.refs_2_, ...), custom_call_target="tpu_custom_call" | custom-call | tf_op jit(solution)/shard_map/analysis/pallas_call | solution.py:596
Async XLA Ops:
  0.0 17.2 %copy-start.1 = (f32[16,256]{1,0:T(8,128)S(1)}, f32[16,256]{1,0:T(8,128)}, u32[]{:S(2)}) copy-start(f32[16,256]{1,0:T(8,128)} %depth.1) | copy-start | bytes 49156
  0.0 17.2 %copy-start = (f32[16,3,16,256]{3,2,1,0:T(8,128)S(1)}, f32[16,3,16,256]{3,2,1,0:T(8,128)}, u32[]{:S(2)}) copy-start(f32[16,3,16,256]{3,2,1,0:T(8,128)} %state.1) | copy-start | bytes 2359300
  2.3 14.9 %collective-permute-start = (f32[88,256]{1,0:T(8,128)}, f32[88,256]{1,0:T(8,128)S(1)}, u32[]{:S(2)}, u32[]{:S(2)}) collective-permute-start(f32[88,256]{1,0:T(8,128)} %get-tuple-element.22), channel_id=1, source_target_pairs={{0,4},{4,8},{8,12},{12,16},{16,20},{20,24},{24,28},{28,0},{1,5},{5... | collective-permute-start | bytes 270344 | tf_op jit(solution)/shard_map/ppermute | solution.py:518
  5.3 11.9 %collective-permute-start.1 = (f32[88,256]{1,0:T(8,128)}, f32[88,256]{1,0:T(8,128)S(1)}, u32[]{:S(2)}, u32[]{:S(2)}) collective-permute-start(f32[88,256]{1,0:T(8,128)} %get-tuple-element.23), channel_id=1, source_target_pairs={{4,0},{8,4},{12,8},{16,12},{20,16},{24,20},{28,24},{0,28},{5,1},{9... | collective-permute-start | bytes 270344 | tf_op jit(solution)/shard_map/ppermute | solution.py:517
  8.4 4.0 %collective-permute-start.2 = (f32[16,256]{1,0:T(8,128)}, f32[16,256]{1,0:T(8,128)S(1)}, u32[]{:S(2)}, u32[]{:S(2)}) collective-permute-start(f32[16,256]{1,0:T(8,128)} %get-tuple-element.24), channel_id=1, source_target_pairs={{0,24},{1,9},{2,22},{3,15},{4,28},{5,13},{6,26},{7,19},{8,0},{9,17... | collective-permute-start | bytes 49160 | tf_op jit(solution)/shard_map/ppermute | solution.py:520
  10.3 9.5 %copy-start.2 = (s32[4,64,128]{2,1,0:T(8,128)S(1)}, s32[4,64,128]{2,1,0:T(8,128)}, u32[]{:S(2)}) copy-start(s32[4,64,128]{2,1,0:T(8,128)} %refs_2_.3) | copy-start | bytes 393220
  10.3 9.5 %copy-start.3 = (f32[4,64,128]{2,1,0:T(8,128)S(1)}, f32[4,64,128]{2,1,0:T(8,128)}, u32[]{:S(2)}) copy-start(f32[4,64,128]{2,1,0:T(8,128)} %refs_3_.3) | copy-start | bytes 393220
  10.3 9.5 %copy-start.4 = (f32[16,256]{1,0:T(8,128)S(1)}, f32[16,256]{1,0:T(8,128)}, u32[]{:S(2)}) copy-start(f32[16,256]{1,0:T(8,128)} %get-tuple-element.27.refs_4_) | copy-start | bytes 49156
  10.3 6.9 %collective-permute-start.3 = (f32[16,256]{1,0:T(8,128)}, f32[16,256]{1,0:T(8,128)S(1)}, u32[]{:S(2)}, u32[]{:S(2)}) collective-permute-start(f32[16,256]{1,0:T(8,128)} %get-tuple-element.25), channel_id=1, source_target_pairs={{0,16},{4,20},{8,24},{12,28},{16,0},{20,4},{24,8},{28,12}} | collective-permute-start | bytes 49160 | tf_op jit(solution)/shard_map/ppermute | solution.py:520
  18.1 1.6 %collective-permute-start.4 = (f32[18,16,256]{2,1,0:T(8,128)S(1)}, f32[18,16,256]{2,1,0:T(8,128)S(1)}, u32[]{:S(2)}, u32[]{:S(2)}) collective-permute-start(f32[18,16,256]{2,1,0:T(8,128)S(1)} %get-tuple-element.26.refs_0_), channel_id=1, source_target_pairs={{0,1},{1,0},{2,3},{3,2},{4,5},{5,4},{6,7},{7,6},{8,9},{9,8},{10,11... | collective-permute-start | bytes 884744 | tf_op jit(solution)/shard_map/ppermute | solution.py:497
  18.2 9.4 %collective-permute-start.5 = (f32[18,16,256]{2,1,0:T(8,128)S(1)}, f32[18,16,256]{2,1,0:T(8,128)S(1)}, u32[]{:S(2)}, u32[]{:S(2)}) collective-permute-start(f32[18,16,256]{2,1,0:T(8,128)S(1)} %get-tuple-element.26.refs_0_), channel_id=1, source_target_pairs={{0,2},{1,3},{2,0},{3,1},{4,6},{5,7},{6,4},{7,5},{8,10},{9,11},{10,... | collective-permute-start | bytes 884744 | tf_op jit(solution)/shard_map/ppermute | solution.py:497
  19.8 0.7 %copy-start.5 = (s32[64,1]{0,1:T(1,128)S(1)}, s32[64,1]{0,1:T(1,128)}, u32[]{:S(2)}) copy-start(s32[64,1]{0,1:T(1,128)} %param.11) | copy-start | bytes 772
  27.6 2.0 %collective-permute-start.6 = (f32[18,16,256]{2,1,0:T(8,128)S(1)}, f32[18,16,256]{2,1,0:T(8,128)S(1)}, u32[]{:S(2)}, u32[]{:S(2)}) collective-permute-start(f32[18,16,256]{2,1,0:T(8,128)S(1)} %collective-permute-done.5.refs_0_.refs_2_), channel_id=1, source_target_pairs={{0,1},{1,0},{2,3},{3,2},{4,5},{5,4},{6,7},{7,6},{8,9},{9,8},{10,11... | collective-permute-start | bytes 884744 | tf_op jit(solution)/shard_map/ppermute | solution.py:497
  27.6 13.3 %collective-permute-start.9 = (f32[16,16,256]{2,1,0:T(8,128)S(1)}, f32[16,16,256]{2,1,0:T(8,128)S(1)}, u32[]{:S(2)}, u32[]{:S(2)}) collective-permute-start(f32[16,16,256]{2,1,0:T(8,128)S(1)} %get-tuple-element.36.refs_4_), channel_id=1, source_target_pairs={{0,2},{1,3},{2,0},{3,1},{4,6},{5,7},{6,4},{7,5},{8,10},{9,11},{10,... | collective-permute-start | bytes 786440 | tf_op jit(solution)/shard_map/ppermute | solution.py:497
  27.9 14.1 %collective-permute-start.12 = (f32[16,16,256]{2,1,0:T(8,128)S(1)}, f32[16,16,256]{2,1,0:T(8,128)S(1)}, u32[]{:S(2)}, u32[]{:S(2)}) collective-permute-start(f32[16,16,256]{2,1,0:T(8,128)S(1)} %get-tuple-element.38.refs_8_), channel_id=1, source_target_pairs={{0,2},{1,3},{2,0},{3,1},{4,6},{5,7},{6,4},{7,5},{8,10},{9,11},{10,... | collective-permute-start | bytes 786440 | tf_op jit(solution)/shard_map/ppermute | solution.py:497
  35.9 1.2 %collective-permute-start.7 = (f32[9,1,128]{2,1,0:T(1,128)S(1)}, f32[9,1,128]{2,1,0:T(1,128)S(1)}, u32[]{:S(2)}, u32[]{:S(2)}) collective-permute-start(f32[9,1,128]{2,1,0:T(1,128)S(1)} %get-tuple-element.34), channel_id=1, source_target_pairs={{0,1},{1,0},{2,3},{3,2},{4,5},{5,4},{6,7},{7,6},{8,9},{9,8},{10,11... | collective-permute-start | bytes 13832 | tf_op jit(solution)/shard_map/ppermute | solution.py:497
  37.8 11.0 %all-to-all-start = ((f32[32,9,1,128]{3,2,1,0:T(1,128)}), f32[32,9,1,128]{3,2,1,0:T(1,128)S(1)}, u32[]{:S(2)}, u32[]{:S(2)}) async-start(f32[32,9,1,128]{3,2,1,0:T(1,128)} %spread.1), calls=%async_computation | async-start | bytes 294912 | tf_op jit(solution)/shard_map/all_to_all | solution.py:594
  40.4 1.6 %collective-permute-start.8 = (f32[16,16,256]{2,1,0:T(8,128)S(1)}, f32[16,16,256]{2,1,0:T(8,128)S(1)}, u32[]{:S(2)}, u32[]{:S(2)}) collective-permute-start(f32[16,16,256]{2,1,0:T(8,128)S(1)} %get-tuple-element.36.refs_4_), channel_id=1, source_target_pairs={{0,1},{1,0},{2,3},{3,2},{4,5},{5,4},{6,7},{7,6},{8,9},{9,8},{10,11... | collective-permute-start | bytes 786440 | tf_op jit(solution)/shard_map/ppermute | solution.py:497
  40.6 1.8 %collective-permute-start.11 = (f32[16,16,256]{2,1,0:T(8,128)S(1)}, f32[16,16,256]{2,1,0:T(8,128)S(1)}, u32[]{:S(2)}, u32[]{:S(2)}) collective-permute-start(f32[16,16,256]{2,1,0:T(8,128)S(1)} %get-tuple-element.38.refs_8_), channel_id=1, source_target_pairs={{0,1},{1,0},{2,3},{3,2},{4,5},{5,4},{6,7},{7,6},{8,9},{9,8},{10,11... | collective-permute-start | bytes 786440 | tf_op jit(solution)/shard_map/ppermute | solution.py:497
  41.0 1.8 %collective-permute-start.10 = (f32[16,16,256]{2,1,0:T(8,128)S(1)}, f32[16,16,256]{2,1,0:T(8,128)S(1)}, u32[]{:S(2)}, u32[]{:S(2)}) collective-permute-start(f32[16,16,256]{2,1,0:T(8,128)S(1)} %collective-permute-done.9.refs_6_), channel_id=1, source_target_pairs={{0,1},{1,0},{2,3},{3,2},{4,5},{5,4},{6,7},{7,6},{8,9},{9,8},{10,11... | collective-permute-start | bytes 786440 | tf_op jit(solution)/shard_map/ppermute | solution.py:497
  42.0 1.5 %collective-permute-start.13 = (f32[16,16,256]{2,1,0:T(8,128)S(1)}, f32[16,16,256]{2,1,0:T(8,128)S(1)}, u32[]{:S(2)}, u32[]{:S(2)}) collective-permute-start(f32[16,16,256]{2,1,0:T(8,128)S(1)} %collective-permute-done.12.refs_10_), channel_id=1, source_target_pairs={{0,1},{1,0},{2,3},{3,2},{4,5},{5,4},{6,7},{7,6},{8,9},{9,8},{10,11... | collective-permute-start | bytes 786440 | tf_op jit(solution)/shard_map/ppermute | solution.py:497

commit v5 on v4

--- a/solution.py
+++ b/solution.py
@@ -12,6 +12,7 @@
 wave_rate = 0.2
 turn_rate = 0.1
 
+ANY = pl.BlockSpec(memory_space=pl.ANY)
 VMEM = pl.BlockSpec(memory_space=pltpu.VMEM)
 HBM = pl.BlockSpec(memory_space=pltpu.HBM)
 SMEM = pl.BlockSpec(memory_space=pltpu.SMEM)
@@ -19,6 +20,20 @@
 BF16 = jnp.bfloat16
 PARAMS = pltpu.CompilerParams(vmem_limit_bytes=12 * 1024 * 1024)
 FORECAST_FLOPS = 2 * 10**9
+RIM = 3
+
+
+def hold(arrays, *others):
+    return pl.pallas_call(
+        lambda *refs: None,
+        out_shape=tuple(jax.ShapeDtypeStruct(x.shape, x.dtype) for x in arrays),
+        in_specs=[ANY] * (len(arrays) + len(others)),
+        out_specs=(ANY,) * len(arrays),
+        input_output_aliases={i: i for i in range(len(arrays))},
+        compiler_params=PARAMS,
+        cost_estimate=cost(1, 1),
+        name="hold",
+    )(*arrays, *others)
 
 
 def cost(flops, size):
@@ -35,10 +50,9 @@
     return half - 2 * half * (index % 2)
 
 
-def edge_kernel(state_in, depth_in, values, precision, above, below, own, *refs):
-    peers = len(refs) - 5
-    held = refs[:peers]
-    state, depth, seen, weight, sems = refs[peers:]
+def edge_kernel(peers, state_in, depth_in, values, precision, above, below, own, *refs):
+    held = refs[:-5]
+    state, depth, seen, weight, sems = refs[-5:]
     members, _, rows, cols = state.shape
     width = values.shape[-1]
     half = members // 2
@@ -49,11 +63,14 @@
     ]
     place, count = lax.axis_index("space"), values.shape[1]
     peers_of = [place, lax.rem(place + count - 1, count), lax.rem(place + 1, count)]
+    quarters = lax.axis_size("mem")
     for j in range(peers):
-        index = j * lax.axis_size("mem") + lax.axis_index("mem")
+        index = j * quarters + lax.axis_index("mem")
         half = 2 + lax.div(index, 2)
         shift = half - 2 * half * lax.rem(index, 2)
         peers_of.append(lax.rem(place + 2 * count - shift, count))
+    for index in range(peers * quarters, count - 3):
+        peers_of.append(lax.rem(place + 2 * count - far_shift(index), count))
     for j, peer in enumerate(peers_of):
         copies.append(pltpu.make_async_copy(values.at[0, peer], seen.at[j], sems.at[3 + 2 * j]))
         copies.append(pltpu.make_async_copy(precision.at[0, peer], weight.at[j], sems.at[4 + 2 * j]))
@@ -96,21 +113,59 @@
     slots = values.shape[2]
     rim = jax.ShapeDtypeStruct((4 * members + 8 + slots, cols), F32)
     held = jax.ShapeDtypeStruct((slots, cols), F32)
+    owners = peers + (values.shape[1] - 3) % lax.axis_size("mem")
     return pl.pallas_call(
-        edge_kernel,
-        out_shape=(rim, rim, held) + (held,) * peers,
+        functools.partial(edge_kernel, peers),
+        out_shape=(rim, rim, held) + (held,) * owners,
         in_specs=[HBM] * 4,
-        out_specs=(VMEM,) * (3 + peers),
+        out_specs=(VMEM,) * (3 + owners),
         scratch_shapes=[
             pltpu.VMEM(state.shape, F32),
             pltpu.VMEM(depth.shape, F32),
-            pltpu.VMEM((3 + peers,) + values.shape[2:], F32),
-            pltpu.VMEM((3 + peers,) + values.shape[2:], F32),
-            pltpu.SemaphoreType.DMA((9 + 2 * peers,)),
+            pltpu.VMEM((3 + owners,) + values.shape[2:], F32),
+            pltpu.VMEM((3 + owners,) + values.shape[2:], F32),
+            pltpu.SemaphoreType.DMA((9 + 2 * owners,)),
         ],
         compiler_params=pltpu.CompilerParams(vmem_limit_bytes=56 * 1024 * 1024),
         name="edges",
     )(state, depth, values, precision)
+
+
+def inner_kernel(state, depth, out):
+    members, _, rows, cols = state.shape
+    deep = [jnp.broadcast_to(depth[t : t + 1], (members, cols)) for t in range(rows)]
+    h = [state[:, 0, t, :] for t in range(rows)]
+    u = [state[:, 1, t, :] for t in range(rows)]
+    v = [state[:, 2, t, :] for t in range(rows)]
+    for step in range(2):
+        edge = 2 * step + 1
+        flux = [d * e if e is not None else None for d, e in zip(deep, u)]
+        new = [None] * rows
+        for t in range(edge, rows - edge):
+            new[t] = h[t] - mass_rate * (flux[t + 1] - flux[t - 1] + diff_cols(deep[t] * v[t]))
+        h = new
+        if step == 1:
+            break
+        east, north = [None] * rows, [None] * rows
+        for t in range(edge + 1, rows - edge - 1):
+            east[t] = u[t] - wave_rate * (h[t + 1] - h[t - 1]) + turn_rate * v[t]
+            north[t] = v[t] - wave_rate * diff_cols(h[t]) - turn_rate * u[t]
+        u, v = east, north
+    for t in range(RIM, rows - RIM):
+        out[t - RIM] = h[t]
+
+
+def inner_heights(state, depth):
+    members, _, rows, cols = state.shape
+    return pl.pallas_call(
+        inner_kernel,
+        out_shape=jax.ShapeDtypeStruct((rows - 2 * RIM, members, cols), F32),
+        in_specs=[VMEM] * 2,
+        out_specs=VMEM,
+        compiler_params=PARAMS,
+        cost_estimate=cost(FORECAST_FLOPS, 4 * state.size),
+        name="inner",
+    )(state, depth)
 
 
 def forecast_kernel(last, state, depth, above, below, *refs):
@@ -180,11 +235,12 @@
     for edge, rim in rims:
         h[outer(edge)] = rim
     new_winds(emit)
-    for t in range(rows):
-        height_out[t] = h[t + 1]
+    outer_rows = list(range(RIM)) + list(range(rows - RIM, rows))
+    for i, t in enumerate(outer_rows):
+        height_out[i] = h[t + 1]
     for j, piece in enumerate(held):
         at = j * slots
-        height_out[rows + at // members, at % members : at % members + slots, :] = piece[...]
+        height_out[2 * RIM + at // members, at % members : at % members + slots, :] = piece[...]
 
 
 def forecast(last, state, depth, above, below, held):
@@ -193,7 +249,7 @@
     return pl.pallas_call(
         functools.partial(forecast_kernel, last),
         out_shape=(
-            jax.ShapeDtypeStruct((rows + extra, members, cols), F32),
+            jax.ShapeDtypeStruct((2 * RIM + extra, members, cols), F32),
             jax.ShapeDtypeStruct((rows, members, cols), F32),
             jax.ShapeDtypeStruct((rows, members, cols), F32),
         ),
@@ -211,25 +267,27 @@
     )(state, depth, above, below, *held)
 
 
-def interpolate(pieces, cells, weights, split, put):
-    rows = split.shape[0] // (len(pieces) * pieces[0].shape[1])
-    _, members, cols = pieces[0].shape
-    total = members * len(pieces)
+def interpolate(groups, cells, weights, split, put):
+    _, members, cols = groups[0][0][0].shape
+    total = members * len(groups[0][0])
     points, blocks, width = cells.shape
     quarter = lax.axis_index("mem")
     blocks = blocks // lax.axis_size("mem")
-    for k, piece in enumerate(pieces):
-        who = lax.bitwise_xor(lax.rem(quarter, len(pieces)), k)
-        for r in range(rows):
-            x = piece[r]
-            high = x.astype(BF16)
-            low = (x - high.astype(F32)).astype(BF16)
-            at = pl.ds(pl.multiple_of(r * total + who * members, members), members)
-            split[at, 0:cols] = high
-            split[at, cols : 2 * cols] = low
+    first = 0
+    for pieces, lines_of in groups:
+        for k, piece in enumerate(pieces):
+            who = lax.bitwise_xor(lax.rem(quarter, len(pieces)), k)
+            for r in range(len(lines_of)):
+                x = piece[r]
+                high = x.astype(BF16)
+                low = (x - high.astype(F32)).astype(BF16)
+                at = pl.ds(pl.multiple_of((first + r) * total + who * members, members), members)
+                split[at, 0:cols] = high
+                split[at, cols : 2 * cols] = low
+        first += len(lines_of)
 
     def block(b, carry):
-        result = None
+        results = [None] * len(groups)
         line = pl.ds(quarter * blocks + b, 1)
         for half in range(points // 2):
             cell = jnp.concatenate(
@@ -245,19 +303,23 @@
             lines = jnp.dot(
                 split[...], jnp.concatenate([pick, pick], axis=0), preferred_element_type=F32
             )
-            for r in range(rows):
-                term = lines[r * total : (r + 1) * total] * jnp.where(row == r, share, 0.0)
-                term = term[:, :width] + term[:, width:]
-                result = term if result is None else result + term
-        put(b, result)
+            first = 0
+            for g, (_, lines_of) in enumerate(groups):
+                for r, at in enumerate(lines_of):
+                    term = lines[(first + r) * total : (first + r + 1) * total]
+                    term = term * jnp.where(row == at, share, 0.0)
+                    term = term[:, :width] + term[:, width:]
+                    results[g] = term if results[g] is None else results[g] + term
+                first += len(lines_of)
+        put(b, *results)
         return carry
 
     lax.fori_loop(0, blocks, block, 0, unroll=8)
 
 
-def collect(got, pieces, split):
-    _, members, _ = pieces[0].shape
-    rows = split.shape[0] // (len(pieces) * members)
+def collect(got, pieces):
+    members = pieces[0].shape[1]
+    rows = 2 * RIM
     slots = got.shape[1]
     peers = got.shape[0] // len(pieces)
     for k, piece in enumerate(pieces):
@@ -266,54 +328,69 @@
             got[k * peers + j] = piece[rows + at // members, at % members : at % members + slots, :]
 
 
-def predict_kernel(count, owners, *refs):
+def block_lines(owners, share, spaces, slots, peers):
+    space, quarter = lax.axis_index("space"), lax.axis_index("mem")
+    quarters = lax.axis_size("mem")
+    shift = quarters.bit_length() - 1
+    blocks = owners.shape[1]
+    lane = lax.broadcasted_iota(jnp.int32, (share, blocks), 1)
+    line = lax.broadcasted_iota(jnp.int32, (share, blocks), 0) + quarter * share
+    row = jnp.broadcast_to(owners[...], (share, blocks)).astype(F32)
+    mine = jnp.sum(jnp.where(lane == line, row, 0.0), axis=1, keepdims=True)
+    slot = jnp.sum(jnp.where((row == mine) & (lane < line), 1.0, 0.0), axis=1, keepdims=True)
+    apart = mine.astype(jnp.int32) - space
+    apart = jnp.where(apart < 0, apart + spaces, apart)
+    index = jnp.where(apart <= spaces // 2, 2 * (apart - 2), 2 * (spaces - apart - 2) + 1)
+    who = lax.bitwise_xor(lax.bitwise_and(index, quarters - 1), quarter)
+    spot = 3 + who * peers + lax.shift_right_arithmetic(index, shift)
+    spot = jnp.where(index >= peers * quarters, 3 + index, spot)
+    spot = jnp.where(apart <= 1, apart, spot)
+    spot = jnp.where(apart == spaces - 1, 2, spot)
+    return spot * slots + slot.astype(jnp.int32)
+
+
+def near_inner_kernel(lines_of, count, *refs):
     pieces = refs[:count]
-    cells, weights, own, above, below, out, near, slots, spots, split, used = refs[count:]
-    share = slots.shape[0]
-    near[0] = own[...]
-    rim = below.shape[0] - own.shape[0]
-    near[1] = below[rim:]
-    near[2] = above[rim:]
-    collect(near.at[3:], pieces, split)
-    peers = (near.shape[0] - 3) // count
-    space, quarter = lax.axis_index("space"), lax.axis_index("mem")
-    spaces, quarters = used.shape[0], lax.axis_size("mem")
-    begin = quarter * share
-    for owner in range(used.shape[0]):
-        used[owner] = 0
-
-    def skip(b, carry):
-        used[owners[b]] += 1
-        return carry
-
-    lax.fori_loop(0, begin, skip, 0)
-    for i in range(share):
-        owner = owners[begin + i]
-        slots[i] = used[owner]
-        used[owner] += 1
-        apart = lax.rem(owner + spaces - space, spaces)
-        index = jnp.where(apart <= spaces // 2, 2 * (apart - 2), 2 * (spaces - apart - 2) + 1)
-        who = lax.rem(index, quarters)
-        spot = 3 + lax.bitwise_xor(who, quarter) * peers + lax.div(index, quarters)
-        spot = jnp.where(apart <= 1, apart, spot)
-        spots[i] = jnp.where(apart == spaces - 1, 2, spot)
+    cells, weights, owners, out, owners_out, split = refs[count:]
+    owners_out[...] = owners[...]
 
     def put(b, result):
         out[b] = result
 
-    interpolate(pieces, cells, weights, split, put)
-
-
-def gram_kernel(scale, count, count_mem, spots, slots, *refs):
+    interpolate([(pieces, lines_of)], cells, weights, split, put)
+
+
+def middle_kernel(inner_rows, outer_rows, count, *refs):
+    far, near = refs[:count], refs[count : 2 * count]
+    cells, weights, early, own, above, below, out, out_far, got, split = refs[2 * count :]
+    got[0] = own[...]
+    rim = below.shape[0] - own.shape[0]
+    got[1] = below[rim:]
+    got[2] = above[rim:]
+    collect(got.at[3:], near)
+
+    def put(b, result_far, result):
+        out_far[b] = result_far
+        out[b] = result + early[b]
+
+    interpolate([(far, inner_rows), (near, outer_rows)], cells, weights, split, put)
+
+
+def gram_kernel(lines_of, scale, count, count_mem, peers, owners, *refs):
     pieces = refs[:count]
-    cells, weights, near, early, keep, give, split, lined, got = refs[count:]
+    cells, weights, near, early, early_far = refs[count : count + 5]
+    direct = refs[count + 5 : -5]
+    keep, give, split, lined, got = refs[-5:]
     _, members, cols = pieces[0].shape
     total = members * count_mem
     part = members * count
-    blocks, width = slots.shape[0], cells.shape[2]
+    blocks, width = cells.shape[1] // count_mem, cells.shape[2]
     quarter = lax.axis_index("mem")
     got[0 : near.shape[0]] = near[...]
-    collect(got.at[near.shape[0] :], pieces, split)
+    later = got.shape[0] - len(direct)
+    collect(got.at[near.shape[0] : later], pieces)
+    for i, piece in enumerate(direct):
+        got[later + i] = piece[...]
 
     mine = quarter // count
     base = pl.multiple_of(mine * part, part)
@@ -321,13 +398,22 @@
 
     def put(b, result):
         at = pl.ds(pl.multiple_of(b * width, width), width)
-        lined[pl.ds(final, part), at] = result
+        lined[pl.ds(final, part), at] = result + early_far[b]
         lined[pl.ds(base, part), at] = early[b]
 
-    interpolate(pieces, cells, weights, split, put)
+    interpolate([(pieces, lines_of)], cells, weights, split, put)
     lined[total : 2 * total] = jnp.zeros((total, blocks * width), F32)
+    spaces, slots, across = got.shape
+    picks = block_lines(owners, blocks, spaces, slots, peers)
+    lane = lax.broadcasted_iota(jnp.int32, (blocks, spaces * slots), 1)
+    taken = jnp.dot(
+        jnp.where(lane == picks, 1.0, 0.0),
+        got[...].reshape(spaces * slots, across),
+        precision=lax.Precision.HIGHEST,
+        preferred_element_type=F32,
+    )
     for b in range(blocks):
-        line = got[spots[b], pl.ds(slots[b], 1)]
+        line = taken[b : b + 1]
         seen, much = line[:, 0:width], line[:, width : 2 * width] * scale
         at = pl.ds(b * width, width)
         values = lined[0:total, at]
@@ -470,9 +556,9 @@
 
 
 def analysis_kernel(count_mem, sums, *refs):
-    fields = [refs[f * count_mem : (f + 1) * count_mem] for f in range(3)]
-    out, lower = refs[3 * count_mem :]
-    rows, members, cols = fields[1][0].shape
+    inner, outer, *winds = [refs[f * count_mem : (f + 1) * count_mem] for f in range(4)]
+    out, lower = refs[4 * count_mem :]
+    rows, members, cols = winds[0][0].shape
     total = members * count_mem
 
     halves = [sums[0], sums[1]]
@@ -485,7 +571,12 @@
     left = jnp.concatenate([high, high, low], axis=1)
     for field in range(3):
         for r in range(rows):
-            pieces = [piece[r] for piece in fields[field]]
+            if field > 0:
+                pieces = [piece[r] for piece in winds[field - 1]]
+            elif RIM <= r < rows - RIM:
+                pieces = [piece[r - RIM] for piece in inner]
+            else:
+                pieces = [piece[r if r < RIM else r - rows + 2 * RIM] for piece in outer]
             upper = [x.astype(BF16) for x in pieces]
             rest = [(x - y.astype(F32)).astype(BF16) for x, y in zip(pieces, upper)]
             stack = jnp.concatenate(upper + rest + upper, axis=0)
@@ -510,9 +601,9 @@
     share = blocks // count_mem
     scale = math.sqrt((total - 1) / (count * blocks * width))
 
-    peers = -(-(count - 3) // count_mem)
-
-    to_above, to_below, own, *held = edges(peers, state, depth, obs_values, obs_precision)
+    peers = (count - 3) // count_mem
+
+    to_above, to_below, own, *blocks_out = edges(peers, state, depth, obs_values, obs_precision)
     ends = count - 1
     below = lax.ppermute(to_above, "space", [((i + 1) % count, i) for i in range(count)])
     above = lax.ppermute(to_below, "space", [(i, (i + 1) % count) for i in range(count)])
@@ -524,65 +615,97 @@
                 (s * count_mem + q, (s - far_shift(j * count_mem + q)) % count * count_mem + q)
                 for s in range(count)
                 for q in range(count_mem)
-                if j * count_mem + q < count - 3
             ],
         )
-        for j, piece in enumerate(held)
+        for j, piece in enumerate(blocks_out[:peers])
     ]
+    near, far = 1, count_mem // 2
+    inner_rows = list(range(RIM, rows - RIM))
+    outer_rows = list(range(RIM)) + list(range(rows - RIM, rows))
+    early = jax.ShapeDtypeStruct((share, far * members, width), F32)
+    owners = owner_map.reshape(1, blocks)
+
+    def work(lines_of):
+        return dict(
+            compiler_params=PARAMS,
+            cost_estimate=cost(
+                4 * obs_cells.shape[0] * share * width * len(lines_of) * members * far * cols,
+                4 * len(lines_of) * members * cols * far,
+            ),
+        )
+
+    def split(lines_of):
+        return pltpu.VMEM((len(lines_of) * far * members, 2 * cols), BF16)
+
+    inner = {0: inner_heights(state, after(depth, to_above))}
+    inner[far] = swap(inner[0], "mem", far)
+    inner[near] = swap(inner[0], "mem", near)
+    inner[far + near] = swap(inner[0], "mem", far + near)
+    first, owners = pl.pallas_call(
+        functools.partial(near_inner_kernel, inner_rows, far),
+        out_shape=(early, jax.ShapeDtypeStruct(owners.shape, owners.dtype)),
+        in_specs=[VMEM] * (far + 3),
+        out_specs=(VMEM, VMEM),
+        scratch_shapes=[split(inner_rows)],
+        name="near_inner",
+        **work(inner_rows),
+    )(inner[0], inner[near], obs_cells, obs_weights, owners)
+
+    above, below = (after(x, first) for x in (above, below))
     height, *parts = forecast(ends, state, depth, above, below, held)
-
-    near, far = 1, count_mem // 2
-    early_shape = (share, far * members, width)
-    split = pltpu.VMEM((rows * far * members, 2 * cols), BF16)
-    flops = 4 * obs_cells.shape[0] * share * width * rows * members * far * cols
-    owners = owner_map[:, 0]
-    heights = {0: height}
+    outer = {0: height}
+    outer[far] = swap(height, "mem", far)
+    direct = []
+    for i, piece in enumerate(blocks_out[peers:]):
+        shift = far_shift(peers * count_mem + i)
+        ring = [(s, (s - shift) % count) for s in range(count)]
+        direct.append(lax.ppermute(after(piece, height), "space", ring))
+    outer[near] = swap(height, "mem", near)
+    outer[far + near] = swap(height, "mem", far + near)
+    near_shape = (3 + far * peers, obs_values.shape[2], cols)
+    first, second, near_blocks = pl.pallas_call(
+        functools.partial(middle_kernel, inner_rows, outer_rows, far),
+        out_shape=(early, early, jax.ShapeDtypeStruct(near_shape, F32)),
+        in_specs=[VMEM] * (2 * far + 6),
+        out_specs=(VMEM,) * 3,
+        scratch_shapes=[split(inner_rows + outer_rows)],
+        name="middle",
+        **work(inner_rows + outer_rows),
+    )(
+        *[inner[k] for k in range(far, 2 * far)],
+        *[outer[k] for k in range(far)],
+        obs_cells,
+        obs_weights,
+        first,
+        own,
+        above,
+        below,
+    )
+    parts = hold(parts, outer[far], outer[far + near], second, *direct)
     winds = [{0: part} for part in parts]
-    heights[far] = swap(height, "mem", far)
-    heights[near] = swap(height, "mem", near)
-    near_shape = (3 + far * peers, obs_values.shape[2], cols)
-    early, first, slots, spots = pl.pallas_call(
-        functools.partial(predict_kernel, far),
-        out_shape=(
-            jax.ShapeDtypeStruct(early_shape, F32),
-            jax.ShapeDtypeStruct(near_shape, F32),
-            jax.ShapeDtypeStruct((share,), jnp.int32),
-            jax.ShapeDtypeStruct((share,), jnp.int32),
-        ),
-        in_specs=[SMEM] + [VMEM] * (far + 5),
-        out_specs=(VMEM, VMEM, SMEM, SMEM),
-        scratch_shapes=[split, pltpu.SMEM((count,), jnp.int32)],
-        compiler_params=PARAMS,
-        cost_estimate=cost(flops, 4 * height.size * far),
-        name="predict",
-    )(owners, heights[0], heights[near], obs_cells, obs_weights, own, above, below)
-    heights[far] = after(heights[far], early)
-    heights[far + near] = swap(heights[far], "mem", near)
     for wind in winds:
-        wind[far] = swap(after(wind[0], heights[far]), "mem", far)
+        wind[far] = swap(wind[0], "mem", far)
         wind[near] = swap(wind[0], "mem", near)
-    for wind in winds:
         wind[far + near] = swap(wind[far], "mem", near)
-    heights = [heights[k] for k in range(count_mem)]
+    inner, outer = ([x[k] for k in range(count_mem)] for x in (inner, outer))
     winds = [wind[k] for wind in winds for k in range(count_mem)]
 
     half = (total // 4 + 2) // 2
     devices = count * count_mem
     part = jax.ShapeDtypeStruct((half, 1, 2 * total), F32)
     keep, give = pl.pallas_call(
-        functools.partial(gram_kernel, scale, far, count_mem),
+        functools.partial(gram_kernel, outer_rows, scale, far, count_mem, peers),
         out_shape=(part, part),
-        in_specs=[SMEM, SMEM] + [VMEM] * (far + 4),
+        in_specs=[VMEM] * (far + 6 + len(direct)),
         out_specs=(VMEM, VMEM),
         scratch_shapes=[
-            split,
+            split(outer_rows),
             pltpu.VMEM((2 * total, share * width), F32),
-            pltpu.VMEM((3 + count_mem * peers,) + near_shape[1:], F32),
+            pltpu.VMEM((count,) + near_shape[1:], F32),
         ],
-        compiler_params=PARAMS,
-        cost_estimate=cost(flops, 4 * height.size * count_mem),
         name="gram",
-    )(spots, slots, *heights[far:], obs_cells, obs_weights, first, early)
+        **work(outer_rows),
+    )(owners, *outer[far:], obs_cells, obs_weights, near_blocks, first, second, *direct)
     sent = pl.pallas_call(
         spread_kernel,
         out_shape=jax.ShapeDtypeStruct((devices,) + part.shape, F32),
@@ -596,12 +719,12 @@
     return pl.pallas_call(
         functools.partial(analysis_kernel, count_mem),
         out_shape=jax.ShapeDtypeStruct(state.shape, F32),
-        in_specs=[VMEM] * (1 + 3 * count_mem),
+        in_specs=[VMEM] * (1 + 4 * count_mem),
         out_specs=VMEM,
         scratch_shapes=[pltpu.VMEM((total, 2 * total), F32)],
         compiler_params=PARAMS,
         name="analysis",
-    )(sums, *heights, *winds)
+    )(sums, *inner, *outer, *winds)
 
 
 def solution(mesh):

time: 53.3 us -> 51.3 us (0.962)
  waiting for transfers between devices: 16.6 us -> 12.1 us
  starting transfers between devices: 15.5 us -> 17.5 us
  Pallas kernels: 20.1 us -> 21.4 us
  local copies, waits for them, and re-layouts: 0.66 us -> 0.05 us
    ppermute x2 -> x1, waiting for transfers between devices: 4.81 us -> 0.01 us  [local(): lax.ppermute(piece, ('space', 'mem'), [(s * count_mem + q, (s - far_shift...]
    ppermute x10 -> x13, starting transfers between devices: 2.9 us -> 7.11 us  [swap(): return lax.ppermute(x, axis, [(i, i ^ bit) for i in range(count)])]
    ppermute x2 -> x1, starting transfers between devices: 3.97 us -> 0.45 us  [local(): lax.ppermute(piece, ('space', 'mem'), [(s * count_mem + q, (s - far_shift...]
    ppermute x10 -> x13, waiting for transfers between devices: 6.51 us -> 3.54 us  [swap(): return lax.ppermute(x, axis, [(i, i ^ bit) for i in range(count)])]
    ppermute x1, starting transfers between devices: 3.1 us -> 5.71 us  [local(): lax.ppermute(to_above, 'space', [((i + 1) % count, i) for i in range(coun...]
    ppermute x1, waiting for transfers between devices: 0.01 us -> 2.54 us  [local(): lax.ppermute(to_below, 'space', [(i, (i + 1) % count) for i in range(coun...]
    ppermute x1, starting transfers between devices: 2.99 us -> 0.7 us  [local(): lax.ppermute(to_below, 'space', [(i, (i + 1) % count) for i in range(coun...]
    pallas_call x3 -> x6, Pallas kernels: 14.2 us -> 15.5 us  [the longest x1 4.99 us: local(): pl.pallas_call(functools.partial(middle_kernel, inner_rows, outer_rows, f...]
  transfers between devices with their start and end apart: 15 -> 18, of which waited for: 9 -> 5; matrix products, arithmetic and copies ran while one was open for 0% -> 0% of each run, Pallas kernels for 24% -> 28%
where the time goes in v5:
time: 51.3 us; the launch traced here: 51.1 us
  Pallas kernels  21.4 us (42%)
  starting transfers between devices  17.5 us (34%)
  waiting for transfers between devices  12.1 us (24%)
    ppermute x13, starting transfers between devices, swap(): return lax.ppermute(x, axis, [(i, i ^ bit) for i in range(count)])  7.11 us
    all_to_all x1, waiting for transfers between devices, local(): lax.all_to_all(sent, ('space', 'mem'), split_axis=0, concat_axis=0, tiled...  5.97 us
    ppermute x1, starting transfers between devices, local(): lax.ppermute(to_above, 'space', [((i + 1) % count, i) for i in range(coun...  5.71 us
    pallas_call x1, Pallas kernels, local(): pl.pallas_call(functools.partial(middle_kernel, inner_rows, outer_rows, f...  4.99 us
    pallas_call x1, Pallas kernels, local(): pl.pallas_call(functools.partial(analysis_kernel, count_mem), out_shape=j...  4.22 us
    pallas_call x1, Pallas kernels, local(): pl.pallas_call(functools.partial(near_inner_kernel, inner_rows, far), out...  3.99 us
    pallas_call x1, Pallas kernels, local(): pl.pallas_call(functools.partial(gram_kernel, outer_rows, scale, far, cou...  3.67 us
    ppermute x13, waiting for transfers between devices, swap(): return lax.ppermute(x, axis, [(i, i ^ bit) for i in range(count)])  3.54 us
  transfers between devices with their start and end apart: 18, of which 5 were waited for; matrix products, arithmetic and copies ran while one was open for 0% of the time, Pallas kernels for 28%

profile of v5, /device:TPU:0, one launch (start us, length us, event | category | flops | bytes accessed | tf_op | source)
XLA Modules:
  0.0 51.1 jit_solution(818235504605657251)
XLA Ops:
  0.0 0.0 copy-start.1
  0.0 0.0 copy-start
  0.0 2.3 %edges.1 = (f32[88,256]{1,0:T(8,128)}, f32[88,256]{1,0:T(8,128)}, f32[16,256]{1,0:T(8,128)}, f32[16,256]{1,0:T(8,128)}, f32[16,256]{1,0:T(8,128)}) custom-call(f32[16,3,16,256]{3,2,1,0:T(8,128)} %state.3, f32[16,256]{1,0:T(8,128)} %depth.2, f32[1,8,16,128]{3,2,1,0:T(8,128)} %values.1, f32[1,8,16,128]{3,2,1,0:T(8,128)} %precision.1), custom_call_target="tpu_custom_call" | custom-call | tf_op jit(solution)/shard_map/edges/pallas_call | solution.py:117
  2.3 0.0 copy-done.1
  2.3 0.0 copy-done
  2.3 0.0 copy-start.7
  2.3 0.0 copy-start.9
  2.3 0.0 copy-start.6
  2.3 0.0 copy-start.2
  2.3 0.0 copy-start.3
  2.4 0.6 %inner.1.refs_0_ = f32[10,16,256]{2,1,0:T(8,128)S(1)} custom-call(f32[16,3,16,256]{3,2,1,0:T(8,128)S(1)} %copy-done, f32[16,256]{1,0:T(8,128)S(1)} %copy-done.1), custom_call_target="tpu_custom_call" | custom-call | flops 2000000000 | bytes 786432 | tf_op jit(solution)/shard_map/inner/pallas_call | solution.py:160
  2.9 0.5 %collective-permute-start = (f32[10,16,256]{2,1,0:T(8,128)S(1)}, f32[10,16,256]{2,1,0:T(8,128)S(1)}, u32[]{:S(2)}, u32[]{:S(2)}) collective-permute-start(f32[10,16,256]{2,1,0:T(8,128)S(1)} %inner.1.refs_0_), channel_id=1, source_target_pairs={{0,1},{1,0},{2,3},{3,2},{4,5},{5,4},{6,7},{7,6},{8,9},{9,8},{10,11... | collective-permute-start | bytes 491528 | tf_op jit(solution)/shard_map/ppermute | solution.py:588
  3.5 0.0 copy-done.7
  3.5 5.7 %collective-permute-start.2 = (f32[88,256]{1,0:T(8,128)S(1)}, f32[88,256]{1,0:T(8,128)S(1)}, u32[]{:S(2)}, u32[]{:S(2)}) collective-permute-start(f32[88,256]{1,0:T(8,128)S(1)} %copy-done.7), channel_id=1, source_target_pairs={{4,0},{8,4},{12,8},{16,12},{20,16},{24,20},{28,24},{0,28},{5,1},{9... | collective-permute-start | bytes 270344 | tf_op jit(solution)/shard_map/ppermute | solution.py:608
  9.2 1.2 %collective-permute-start.7 = (f32[10,16,256]{2,1,0:T(8,128)S(1)}, f32[10,16,256]{2,1,0:T(8,128)S(1)}, u32[]{:S(2)}, u32[]{:S(2)}) collective-permute-start(f32[10,16,256]{2,1,0:T(8,128)S(1)} %inner.1.refs_0_), channel_id=1, source_target_pairs={{0,3},{1,2},{2,1},{3,0},{4,7},{5,6},{6,5},{7,4},{8,11},{9,10},{10,... | collective-permute-start | bytes 491528 | tf_op jit(solution)/shard_map/ppermute | solution.py:588
  10.3 0.5 collective-permute-start.6
  10.8 0.0 copy-done.9
  10.8 0.4 collective-permute-start.3
  11.3 0.0 collective-permute-done.refs_1_
  11.3 0.0 copy-done.6
  11.3 0.0 copy-start.5
  11.3 0.7 %collective-permute-start.1 = (f32[88,256]{1,0:T(8,128)S(1)}, f32[88,256]{1,0:T(8,128)S(1)}, u32[]{:S(2)}, u32[]{:S(2)}) collective-permute-start(f32[88,256]{1,0:T(8,128)S(1)} %copy-done.6), channel_id=1, source_target_pairs={{0,4},{4,8},{8,12},{12,16},{16,20},{20,24},{24,28},{28,0},{1,5},{5... | collective-permute-start | bytes 270344 | tf_op jit(solution)/shard_map/ppermute | solution.py:609
  12.0 0.0 copy-done.2
  12.0 0.0 copy-done.3
  12.0 0.0 copy-done.5
  12.0 4.0 %near_inner.1 = (f32[16,32,128]{2,1,0:T(8,128)S(1)}, s32[1,64]{1,0:T(1,128)S(1)}) custom-call(f32[10,16,256]{2,1,0:T(8,128)S(1)} %inner.1.refs_0_, f32[10,16,256]{2,1,0:T(8,128)S(1)} %collective-permute-done.refs_1_, s32[4,64,128]{2,1,0:T(8,128)S(1)} %copy-done.2, f32[4,64,128]{2,1,0:T(8,128)S(1)} %copy-done.3, s32[1,64]{1,0:T(1,128)S(1)} %bitcast.1), custom_call_target="tpu_custom_call" | custom-call | flops 2684354560 | bytes 327680 | tf_op jit(solution)/shard_map/near_inner/pallas_call | solution.py:644
  16.0 0.0 collective-permute-done.2.below.refs_9_
  16.0 0.0 copy-start.8
  16.0 0.0 copy-start.4
  16.0 2.5 %collective-permute-done.1.above.refs_8_ = f32[88,256]{1,0:T(8,128)S(1)} collective-permute-done((f32[88,256]{1,0:T(8,128)S(1)}, f32[88,256]{1,0:T(8,128)S(1)}, u32[]{:S(2)}, u32[]{:S(2)}) %collective-permute-start.1) | collective-permute-done | bytes 90144 | tf_op jit(solution)/shard_map/ppermute | solution.py:609
  18.6 0.0 collective-permute-done.3.refs_0_
  18.6 0.9 %forecast.1 = (f32[7,16,256]{2,1,0:T(8,128)S(1)}, f32[16,16,256]{2,1,0:T(8,128)S(1)}, f32[16,16,256]{2,1,0:T(8,128)S(1)}) custom-call(f32[16,3,16,256]{3,2,1,0:T(8,128)S(1)} %copy-done, f32[16,256]{1,0:T(8,128)S(1)} %copy-done.1, f32[88,256]{1,0:T(8,128)S(1)} %collective-permute-done.1.above.refs_8_, f32[88,256]{1,0:T(8,128)S(1)} %collective-permute-done.2.below.refs_9_, ...), custom_call_target="tpu_custom_call" | custom-call | flops 2000000000 | bytes 786432 | tf_op jit(solution)/shard_map/forecast/pallas_call | solution.py:249
  19.5 0.1 collective-permute-start.8
  19.6 1.4 %collective-permute-start.5 = (f32[7,16,256]{2,1,0:T(8,128)S(1)}, f32[7,16,256]{2,1,0:T(8,128)S(1)}, u32[]{:S(2)}, u32[]{:S(2)}) collective-permute-start(f32[7,16,256]{2,1,0:T(8,128)S(1)} %get-tuple-element.34.refs_2_.refs_4_), channel_id=1, source_target_pairs={{0,3},{1,2},{2,1},{3,0},{4,7},{5,6},{6,5},{7,4},{8,11},{9,10},{10,... | collective-permute-start | bytes 344072 | tf_op jit(solution)/shard_map/ppermute | solution.py:588
  21.0 0.7 %collective-permute-start.4 = (f32[7,16,256]{2,1,0:T(8,128)S(1)}, f32[7,16,256]{2,1,0:T(8,128)S(1)}, u32[]{:S(2)}, u32[]{:S(2)}) collective-permute-start(f32[7,16,256]{2,1,0:T(8,128)S(1)} %get-tuple-element.34.refs_2_.refs_4_), channel_id=1, source_target_pairs={{0,2},{1,3},{2,0},{3,1},{4,6},{5,7},{6,4},{7,5},{8,10},{9,11},{10,... | collective-permute-start | bytes 344072 | tf_op jit(solution)/shard_map/ppermute | solution.py:588
  21.7 0.0 collective-permute-done.7.refs_1_.refs_3_
  21.7 0.0 copy-done.8
  21.7 0.0 collective-permute-start.9
  21.7 0.0 collective-permute-done.6.refs_0_.refs_2_
  21.7 0.0 collective-permute-done.8.refs_3_.refs_5_
  21.8 0.0 copy-done.4
  21.8 5.0 %middle.1 = (f32[16,32,128]{2,1,0:T(8,128)S(1)}, f32[16,32,128]{2,1,0:T(8,128)S(1)}, f32[5,16,256]{2,1,0:T(8,128)S(1)}) custom-call(f32[10,16,256]{2,1,0:T(8,128)S(1)} %collective-permute-done.6.refs_0_.refs_2_, f32[10,16,256]{2,1,0:T(8,128)S(1)} %collective-permute-done.7.refs_1_.refs_3_, f32[7,16,256]{2,1,0:T(8,128)S(1)} %get-tuple-element.34.refs_2_.refs_4_, ...), custom_call_target="tpu_custom_call" | custom-call | flops 4294967296 | bytes 524288 | tf_op jit(solution)/shard_map/middle/pallas_call | solution.py:666
  26.8 0.0 collective-permute-done.9.refs_7_.refs_5_
  26.8 0.0 collective-permute-done.5.refs_1_.refs_3_.refs_7_
  26.8 0.8 %collective-permute-done.4.refs_0_.refs_2_.refs_6_ = f32[7,16,256]{2,1,0:T(8,128)S(1)} collective-permute-done((f32[7,16,256]{2,1,0:T(8,128)S(1)}, f32[7,16,256]{2,1,0:T(8,128)S(1)}, u32[]{:S(2)}, u32[]{:S(2)}) %collective-permute-start.4) | collective-permute-done | bytes 114720 | tf_op jit(solution)/shard_map/ppermute | solution.py:588
  27.5 1.3 %collective-permute-start.12 = (f32[16,16,256]{2,1,0:T(8,128)S(1)}, f32[16,16,256]{2,1,0:T(8,128)S(1)}, u32[]{:S(2)}, u32[]{:S(2)}) collective-permute-start(f32[16,16,256]{2,1,0:T(8,128)S(1)} %get-tuple-element.45.refs_8_), channel_id=1, source_target_pairs={{0,2},{1,3},{2,0},{3,1},{4,6},{5,7},{6,4},{7,5},{8,10},{9,11},{10,... | collective-permute-start | bytes 786440 | tf_op jit(solution)/shard_map/ppermute | solution.py:588
  28.8 0.7 %collective-permute-start.15 = (f32[16,16,256]{2,1,0:T(8,128)S(1)}, f32[16,16,256]{2,1,0:T(8,128)S(1)}, u32[]{:S(2)}, u32[]{:S(2)}) collective-permute-start(f32[16,16,256]{2,1,0:T(8,128)S(1)} %get-tuple-element.46.refs_12_), channel_id=1, source_target_pairs={{0,2},{1,3},{2,0},{3,1},{4,6},{5,7},{6,4},{7,5},{8,10},{9,11},{10,... | collective-permute-start | bytes 786440 | tf_op jit(solution)/shard_map/ppermute | solution.py:588
  29.6 3.7 %gram.1 = (f32[9,1,128]{2,1,0:T(1,128)S(1)}, f32[9,1,128]{2,1,0:T(1,128)S(1)}) custom-call(s32[1,64]{1,0:T(1,128)S(1)} %get-tuple-element.28.owners, f32[7,16,256]{2,1,0:T(8,128)S(1)} %collective-permute-done.4.refs_0_.refs_2_.refs_6_, f32[7,16,256]{2,1,0:T(8,128)S(1)} %collective-permute-done.5.refs_1_.refs_3_.refs_7_, s32[4,64,128]{2,1,0:T(8,128)S(1)} %copy-done.2, ...), custom_call_target="tpu_custom_call" | custom-call | flops 1610612736 | bytes 196608 | tf_op jit(solution)/shard_map/gram/pallas_call | solution.py:696
  33.2 0.0 collective-permute-start.10
  33.3 1.2 %collective-permute-done.10.given = f32[9,1,128]{2,1,0:T(1,128)S(1)} collective-permute-done((f32[9,1,128]{2,1,0:T(1,128)S(1)}, f32[9,1,128]{2,1,0:T(1,128)S(1)}, u32[]{:S(2)}, u32[]{:S(2)}) %collective-permute-start.10) | collective-permute-done | bytes 4640 | tf_op jit(solution)/shard_map/ppermute | solution.py:588
  34.4 0.7 %spread.1 = f32[32,9,1,128]{3,2,1,0:T(1,128)} custom-call(f32[9,1,128]{2,1,0:T(1,128)S(1)} %get-tuple-element.41.keep, f32[9,1,128]{2,1,0:T(1,128)S(1)} %collective-permute-done.10.given), custom_call_target="tpu_custom_call" | custom-call | tf_op jit(solution)/shard_map/spread/pallas_call | solution.py:709
  35.2 3.5 %all-to-all-start = ((f32[32,9,1,128]{3,2,1,0:T(1,128)}), f32[32,9,1,128]{3,2,1,0:T(1,128)S(1)}, u32[]{:S(2)}, u32[]{:S(2)}) async-start(f32[32,9,1,128]{3,2,1,0:T(1,128)} %spread.1), calls=%async_computation | async-start | bytes 294912 | tf_op jit(solution)/shard_map/all_to_all | solution.py:717
  38.7 0.1 collective-permute-start.11
  38.8 0.4 collective-permute-start.14
  39.2 0.0 collective-permute-done.12.refs_10_
  39.2 0.1 collective-permute-start.13
  39.3 1.6 %collective-permute-done.15.refs_14_ = f32[16,16,256]{2,1,0:T(8,128)S(1)} collective-permute-done((f32[16,16,256]{2,1,0:T(8,128)S(1)}, f32[16,16,256]{2,1,0:T(8,128)S(1)}, u32[]{:S(2)}, u32[]{:S(2)}) %collective-permute-start.15) | collective-permute-done | bytes 262176 | tf_op jit(solution)/shard_map/ppermute | solution.py:588
  40.9 0.0 collective-permute-start.16
  40.9 0.0 collective-permute-done.11.refs_9_
  40.9 0.0 collective-permute-done.14.refs_13_
  40.9 6.0 %all-to-all-done.sums = f32[32,9,1,128]{3,2,1,0:T(1,128)S(1)} async-done(((f32[32,9,1,128]{3,2,1,0:T(1,128)}), f32[32,9,1,128]{3,2,1,0:T(1,128)S(1)}, u32[]{:S(2)}, u32[]{:S(2)}) %all-to-all-start) | async-done | bytes 147488 | tf_op jit(solution)/shard_map/all_to_all | solution.py:717
  46.9 0.0 collective-permute-done.13.refs_11_
  46.9 0.0 collective-permute-done.16.refs_15_
  46.9 4.2 %analysis.1 = f32[16,3,16,256]{3,2,1,0:T(8,128)} custom-call(f32[32,9,1,128]{3,2,1,0:T(1,128)S(1)} %all-to-all-done.sums, f32[10,16,256]{2,1,0:T(8,128)S(1)} %inner.1.refs_0_, f32[10,16,256]{2,1,0:T(8,128)S(1)} %collective-permute-done.refs_1_, f32[10,16,256]{2,1,0:T(8,128)S(1)} %collective-permute-done.6.refs_0_.refs_2_, ...), custom_call_target="tpu_custom_call" | custom-call | tf_op jit(solution)/shard_map/analysis/pallas_call | solution.py:719
  (1 shorter events, 0.0 us)
Async XLA Ops:
  0.0 2.3 %copy-start.1 = (f32[16,256]{1,0:T(8,128)S(1)}, f32[16,256]{1,0:T(8,128)}, u32[]{:S(2)}) copy-start(f32[16,256]{1,0:T(8,128)} %depth.2) | copy-start | bytes 49156
  0.0 2.3 %copy-start = (f32[16,3,16,256]{3,2,1,0:T(8,128)S(1)}, f32[16,3,16,256]{3,2,1,0:T(8,128)}, u32[]{:S(2)}) copy-start(f32[16,3,16,256]{3,2,1,0:T(8,128)} %state.3) | copy-start | bytes 2359300
  2.3 1.2 %copy-start.7 = (f32[88,256]{1,0:T(8,128)S(1)}, f32[88,256]{1,0:T(8,128)}, u32[]{:S(2)}) copy-start(f32[88,256]{1,0:T(8,128)} %get-tuple-element.26) | copy-start | bytes 270340
  2.3 8.5 %copy-start.9 = (f32[16,256]{1,0:T(8,128)S(1)}, f32[16,256]{1,0:T(8,128)}, u32[]{:S(2)}) copy-start(f32[16,256]{1,0:T(8,128)} %get-tuple-element.33) | copy-start | bytes 49156
  2.3 9.0 %copy-start.6 = (f32[88,256]{1,0:T(8,128)S(1)}, f32[88,256]{1,0:T(8,128)}, u32[]{:S(2)}) copy-start(f32[88,256]{1,0:T(8,128)} %get-tuple-element.29) | copy-start | bytes 270340
  2.3 9.7 %copy-start.2 = (s32[4,64,128]{2,1,0:T(8,128)S(1)}, s32[4,64,128]{2,1,0:T(8,128)}, u32[]{:S(2)}) copy-start(s32[4,64,128]{2,1,0:T(8,128)} %refs_2_.3) | copy-start | bytes 393220
  2.3 9.7 %copy-start.3 = (f32[4,64,128]{2,1,0:T(8,128)S(1)}, f32[4,64,128]{2,1,0:T(8,128)}, u32[]{:S(2)}) copy-start(f32[4,64,128]{2,1,0:T(8,128)} %refs_3_.3) | copy-start | bytes 393220
  2.9 8.4 %collective-permute-start = (f32[10,16,256]{2,1,0:T(8,128)S(1)}, f32[10,16,256]{2,1,0:T(8,128)S(1)}, u32[]{:S(2)}, u32[]{:S(2)}) collective-permute-start(f32[10,16,256]{2,1,0:T(8,128)S(1)} %inner.1.refs_0_), channel_id=1, source_target_pairs={{0,1},{1,0},{2,3},{3,2},{4,5},{5,4},{6,7},{7,6},{8,9},{9,8},{10,11... | collective-permute-start | bytes 491528 | tf_op jit(solution)/shard_map/ppermute | solution.py:588
  3.5 12.5 %collective-permute-start.2 = (f32[88,256]{1,0:T(8,128)S(1)}, f32[88,256]{1,0:T(8,128)S(1)}, u32[]{:S(2)}, u32[]{:S(2)}) collective-permute-start(f32[88,256]{1,0:T(8,128)S(1)} %copy-done.7), channel_id=1, source_target_pairs={{4,0},{8,4},{12,8},{16,12},{20,16},{24,20},{28,24},{0,28},{5,1},{9... | collective-permute-start | bytes 270344 | tf_op jit(solution)/shard_map/ppermute | solution.py:608
  9.2 12.6 %collective-permute-start.7 = (f32[10,16,256]{2,1,0:T(8,128)S(1)}, f32[10,16,256]{2,1,0:T(8,128)S(1)}, u32[]{:S(2)}, u32[]{:S(2)}) collective-permute-start(f32[10,16,256]{2,1,0:T(8,128)S(1)} %inner.1.refs_0_), channel_id=1, source_target_pairs={{0,3},{1,2},{2,1},{3,0},{4,7},{5,6},{6,5},{7,4},{8,11},{9,10},{10,... | collective-permute-start | bytes 491528 | tf_op jit(solution)/shard_map/ppermute | solution.py:588
  10.3 11.4 %collective-permute-start.6 = (f32[10,16,256]{2,1,0:T(8,128)S(1)}, f32[10,16,256]{2,1,0:T(8,128)S(1)}, u32[]{:S(2)}, u32[]{:S(2)}) collective-permute-start(f32[10,16,256]{2,1,0:T(8,128)S(1)} %inner.1.refs_0_), channel_id=1, source_target_pairs={{0,2},{1,3},{2,0},{3,1},{4,6},{5,7},{6,4},{7,5},{8,10},{9,11},{10,... | collective-permute-start | bytes 491528 | tf_op jit(solution)/shard_map/ppermute | solution.py:588
  10.8 7.7 %collective-permute-start.3 = (f32[16,256]{1,0:T(8,128)S(1)}, f32[16,256]{1,0:T(8,128)S(1)}, u32[]{:S(2)}, u32[]{:S(2)}) collective-permute-start(f32[16,256]{1,0:T(8,128)S(1)} %copy-done.9), channel_id=1, source_target_pairs={{0,24},{1,9},{2,22},{3,15},{4,28},{5,13},{6,26},{7,19},{8,0},{9,17... | collective-permute-start | bytes 49160 | tf_op jit(solution)/shard_map/ppermute | solution.py:611
  11.3 0.7 %copy-start.5 = (s32[64,1]{0,1:T(1,128)S(1)}, s32[64,1]{0,1:T(1,128)}, u32[]{:S(2)}) copy-start(s32[64,1]{0,1:T(1,128)} %param.11) | copy-start | bytes 772
  11.3 7.3 %collective-permute-start.1 = (f32[88,256]{1,0:T(8,128)S(1)}, f32[88,256]{1,0:T(8,128)S(1)}, u32[]{:S(2)}, u32[]{:S(2)}) collective-permute-start(f32[88,256]{1,0:T(8,128)S(1)} %copy-done.6), channel_id=1, source_target_pairs={{0,4},{4,8},{8,12},{12,16},{16,20},{20,24},{24,28},{28,0},{1,5},{5... | collective-permute-start | bytes 270344 | tf_op jit(solution)/shard_map/ppermute | solution.py:609
  16.0 5.7 %copy-start.8 = (f32[16,256]{1,0:T(8,128)S(1)}, f32[16,256]{1,0:T(8,128)}, u32[]{:S(2)}) copy-start(f32[16,256]{1,0:T(8,128)} %get-tuple-element.40) | copy-start | bytes 49156
  16.0 5.7 %copy-start.4 = (f32[16,256]{1,0:T(8,128)S(1)}, f32[16,256]{1,0:T(8,128)}, u32[]{:S(2)}) copy-start(f32[16,256]{1,0:T(8,128)} %get-tuple-element.35.refs_7_) | copy-start | bytes 49156
  19.5 2.2 %collective-permute-start.8 = (f32[7,16,256]{2,1,0:T(8,128)S(1)}, f32[7,16,256]{2,1,0:T(8,128)S(1)}, u32[]{:S(2)}, u32[]{:S(2)}) collective-permute-start(f32[7,16,256]{2,1,0:T(8,128)S(1)} %get-tuple-element.34.refs_2_.refs_4_), channel_id=1, source_target_pairs={{0,1},{1,0},{2,3},{3,2},{4,5},{5,4},{6,7},{7,6},{8,9},{9,8},{10,11... | collective-permute-start | bytes 344072 | tf_op jit(solution)/shard_map/ppermute | solution.py:588
  19.6 7.2 %collective-permute-start.5 = (f32[7,16,256]{2,1,0:T(8,128)S(1)}, f32[7,16,256]{2,1,0:T(8,128)S(1)}, u32[]{:S(2)}, u32[]{:S(2)}) collective-permute-start(f32[7,16,256]{2,1,0:T(8,128)S(1)} %get-tuple-element.34.refs_2_.refs_4_), channel_id=1, source_target_pairs={{0,3},{1,2},{2,1},{3,0},{4,7},{5,6},{6,5},{7,4},{8,11},{9,10},{10,... | collective-permute-start | bytes 344072 | tf_op jit(solution)/shard_map/ppermute | solution.py:588
  21.0 6.6 %collective-permute-start.4 = (f32[7,16,256]{2,1,0:T(8,128)S(1)}, f32[7,16,256]{2,1,0:T(8,128)S(1)}, u32[]{:S(2)}, u32[]{:S(2)}) collective-permute-start(f32[7,16,256]{2,1,0:T(8,128)S(1)} %get-tuple-element.34.refs_2_.refs_4_), channel_id=1, source_target_pairs={{0,2},{1,3},{2,0},{3,1},{4,6},{5,7},{6,4},{7,5},{8,10},{9,11},{10,... | collective-permute-start | bytes 344072 | tf_op jit(solution)/shard_map/ppermute | solution.py:588
  21.7 5.0 %collective-permute-start.9 = (f32[16,256]{1,0:T(8,128)S(1)}, f32[16,256]{1,0:T(8,128)S(1)}, u32[]{:S(2)}, u32[]{:S(2)}) collective-permute-start(f32[16,256]{1,0:T(8,128)S(1)} %copy-done.8), channel_id=1, source_target_pairs={{0,16},{4,20},{8,24},{12,28},{16,0},{20,4},{24,8},{28,12},{1,17},{... | collective-permute-start | bytes 49160 | tf_op jit(solution)/shard_map/ppermute | solution.py:662
  27.5 11.7 %collective-permute-start.12 = (f32[16,16,256]{2,1,0:T(8,128)S(1)}, f32[16,16,256]{2,1,0:T(8,128)S(1)}, u32[]{:S(2)}, u32[]{:S(2)}) collective-permute-start(f32[16,16,256]{2,1,0:T(8,128)S(1)} %get-tuple-element.45.refs_8_), channel_id=1, source_target_pairs={{0,2},{1,3},{2,0},{3,1},{4,6},{5,7},{6,4},{7,5},{8,10},{9,11},{10,... | collective-permute-start | bytes 786440 | tf_op jit(solution)/shard_map/ppermute | solution.py:588
  28.8 12.1 %collective-permute-start.15 = (f32[16,16,256]{2,1,0:T(8,128)S(1)}, f32[16,16,256]{2,1,0:T(8,128)S(1)}, u32[]{:S(2)}, u32[]{:S(2)}) collective-permute-start(f32[16,16,256]{2,1,0:T(8,128)S(1)} %get-tuple-element.46.refs_12_), channel_id=1, source_target_pairs={{0,2},{1,3},{2,0},{3,1},{4,6},{5,7},{6,4},{7,5},{8,10},{9,11},{10,... | collective-permute-start | bytes 786440 | tf_op jit(solution)/shard_map/ppermute | solution.py:588
  33.2 1.2 %collective-permute-start.10 = (f32[9,1,128]{2,1,0:T(1,128)S(1)}, f32[9,1,128]{2,1,0:T(1,128)S(1)}, u32[]{:S(2)}, u32[]{:S(2)}) collective-permute-start(f32[9,1,128]{2,1,0:T(1,128)S(1)} %get-tuple-element.42), channel_id=1, source_target_pairs={{0,1},{1,0},{2,3},{3,2},{4,5},{5,4},{6,7},{7,6},{8,9},{9,8},{10,11... | collective-permute-start | bytes 13832 | tf_op jit(solution)/shard_map/ppermute | solution.py:588
  35.2 11.7 %all-to-all-start = ((f32[32,9,1,128]{3,2,1,0:T(1,128)}), f32[32,9,1,128]{3,2,1,0:T(1,128)S(1)}, u32[]{:S(2)}, u32[]{:S(2)}) async-start(f32[32,9,1,128]{3,2,1,0:T(1,128)} %spread.1), calls=%async_computation | async-start | bytes 294912 | tf_op jit(solution)/shard_map/all_to_all | solution.py:717
  38.7 2.3 %collective-permute-start.11 = (f32[16,16,256]{2,1,0:T(8,128)S(1)}, f32[16,16,256]{2,1,0:T(8,128)S(1)}, u32[]{:S(2)}, u32[]{:S(2)}) collective-permute-start(f32[16,16,256]{2,1,0:T(8,128)S(1)} %get-tuple-element.45.refs_8_), channel_id=1, source_target_pairs={{0,1},{1,0},{2,3},{3,2},{4,5},{5,4},{6,7},{7,6},{8,9},{9,8},{10,11... | collective-permute-start | bytes 786440 | tf_op jit(solution)/shard_map/ppermute | solution.py:588
  38.8 2.1 %collective-permute-start.14 = (f32[16,16,256]{2,1,0:T(8,128)S(1)}, f32[16,16,256]{2,1,0:T(8,128)S(1)}, u32[]{:S(2)}, u32[]{:S(2)}) collective-permute-start(f32[16,16,256]{2,1,0:T(8,128)S(1)} %get-tuple-element.46.refs_12_), channel_id=1, source_target_pairs={{0,1},{1,0},{2,3},{3,2},{4,5},{5,4},{6,7},{7,6},{8,9},{9,8},{10,11... | collective-permute-start | bytes 786440 | tf_op jit(solution)/shard_map/ppermute | solution.py:588
  39.2 7.7 %collective-permute-start.13 = (f32[16,16,256]{2,1,0:T(8,128)S(1)}, f32[16,16,256]{2,1,0:T(8,128)S(1)}, u32[]{:S(2)}, u32[]{:S(2)}) collective-permute-start(f32[16,16,256]{2,1,0:T(8,128)S(1)} %collective-permute-done.12.refs_10_), channel_id=1, source_target_pairs={{0,1},{1,0},{2,3},{3,2},{4,5},{5,4},{6,7},{7,6},{8,9},{9,8},{10,11... | collective-permute-start | bytes 786440 | tf_op jit(solution)/shard_map/ppermute | solution.py:588
  40.9 6.0 %collective-permute-start.16 = (f32[16,16,256]{2,1,0:T(8,128)S(1)}, f32[16,16,256]{2,1,0:T(8,128)S(1)}, u32[]{:S(2)}, u32[]{:S(2)}) collective-permute-start(f32[16,16,256]{2,1,0:T(8,128)S(1)} %collective-permute-done.15.refs_14_), channel_id=1, source_target_pairs={{0,1},{1,0},{2,3},{3,2},{4,5},{5,4},{6,7},{7,6},{8,9},{9,8},{10,11... | collective-permute-start | bytes 786440 | tf_op jit(solution)/shard_map/ppermute | solution.py:588

commit v6 on v5

--- a/solution.py
+++ b/solution.py
@@ -169,8 +169,8 @@
 
 
 def forecast_kernel(last, state, depth, above, below, *refs):
-    held = refs[:-7]
-    height_out, east_out, north_out, h, u, v, flux = refs[-7:]
+    held = refs[:-6]
+    height_out, wind_out, h, u, v, flux = refs[-6:]
     members, _, rows, cols = state.shape
     slots = held[0].shape[0]
     deep = [jnp.broadcast_to(depth[t : t + 1], (members, cols)) for t in range(rows)]
@@ -218,8 +218,8 @@
         flux[t + 1] = deep[t] * east
 
     def emit(t, east, north):
-        east_out[t] = east
-        north_out[t] = north
+        wind_out[t] = east
+        wind_out[rows + t] = north
 
     new_heights()
     for delta, ((_, first, east, _), deeps, sign, edge, inside) in zip(deltas, sides):
@@ -250,11 +250,10 @@
         functools.partial(forecast_kernel, last),
         out_shape=(
             jax.ShapeDtypeStruct((2 * RIM + extra, members, cols), F32),
-            jax.ShapeDtypeStruct((rows, members, cols), F32),
-            jax.ShapeDtypeStruct((rows, members, cols), F32),
+            jax.ShapeDtypeStruct((2 * rows, members, cols), F32),
         ),
         in_specs=[VMEM] * (4 + len(held)),
-        out_specs=(VMEM, VMEM, VMEM),
+        out_specs=(VMEM, VMEM),
         scratch_shapes=[
             pltpu.VMEM((rows + 2, members, cols), F32),
             pltpu.VMEM((rows, members, cols), F32),
@@ -314,7 +313,7 @@
         put(b, *results)
         return carry
 
-    lax.fori_loop(0, blocks, block, 0, unroll=8)
+    lax.fori_loop(0, blocks, block, 0, unroll=16)
 
 
 def collect(got, pieces):
@@ -638,8 +637,9 @@
         return pltpu.VMEM((len(lines_of) * far * members, 2 * cols), BF16)
 
     inner = {0: inner_heights(state, after(depth, to_above))}
+    inner[near] = swap(inner[0], "mem", near)
+    (inner[0],) = hold([inner[0]], inner[near])
     inner[far] = swap(inner[0], "mem", far)
-    inner[near] = swap(inner[0], "mem", near)
     inner[far + near] = swap(inner[0], "mem", far + near)
     first, owners = pl.pallas_call(
         functools.partial(near_inner_kernel, inner_rows, far),
@@ -682,9 +682,9 @@
         below,
     )
     parts = hold(parts, outer[far], outer[far + near], second, *direct)
-    winds = [{0: part} for part in parts]
+    both = {0: parts[0], far: swap(parts[0], "mem", far)}
+    winds = [{k: x[i * rows : (i + 1) * rows] for k, x in both.items()} for i in range(2)]
     for wind in winds:
-        wind[far] = swap(wind[0], "mem", far)
         wind[near] = swap(wind[0], "mem", near)
         wind[far + near] = swap(wind[far], "mem", near)
     inner, outer = ([x[k] for k in range(count_mem)] for x in (inner, outer))

time: 51.3 us -> 49.1 us (0.957)
  waiting for transfers between devices: 12.1 us -> 8.59 us
  starting transfers between devices: 17.5 us -> 19.2 us
  Pallas kernels: 21.4 us -> 20.8 us
    ppermute x1, waiting for transfers between devices: 2.54 us -> 0.29 us  [local(): lax.ppermute(to_below, 'space', [(i, (i + 1) % count) for i in range(coun...]
    all_to_all x1, waiting for transfers between devices: 5.97 us -> 4.2 us  [local(): lax.all_to_all(sent, ('space', 'mem'), split_axis=0, concat_axis=0, tiled...]
    ppermute x13 -> x12, starting transfers between devices: 7.11 us -> 8.39 us  [swap(): return lax.ppermute(x, axis, [(i, i ^ bit) for i in range(count)])]
    ppermute x1, starting transfers between devices: 0.01 us -> 1.26 us  [local(): direct.append(lax.ppermute(after(piece, height), 'space', ring))]
    all_to_all x1, starting transfers between devices: 3.49 us -> 2.73 us  [local(): lax.all_to_all(sent, ('space', 'mem'), split_axis=0, concat_axis=0, tiled...]
    ppermute x13 -> x12, waiting for transfers between devices: 3.54 us -> 4.09 us  [swap(): return lax.ppermute(x, axis, [(i, i ^ bit) for i in range(count)])]
  transfers between devices with their start and end apart: 18 -> 17, of which waited for: 5 -> 4; matrix products, arithmetic and copies ran while one was open for 0% -> 0% of each run, Pallas kernels for 28% -> 28%
where the time goes in v6:
time: 49.1 us; the launch traced here: 48.9 us
  Pallas kernels  20.8 us (42%)
  starting transfers between devices  19.2 us (39%)
  waiting for transfers between devices  8.59 us (17%)
    ppermute x12, starting transfers between devices, swap(): return lax.ppermute(x, axis, [(i, i ^ bit) for i in range(count)])  8.39 us
    ppermute x1, starting transfers between devices, local(): lax.ppermute(to_above, 'space', [((i + 1) % count, i) for i in range(coun...  5.74 us
    pallas_call x1, Pallas kernels, local(): pl.pallas_call(functools.partial(middle_kernel, inner_rows, outer_rows, f...  4.76 us
    pallas_call x1, Pallas kernels, local(): pl.pallas_call(functools.partial(analysis_kernel, count_mem), out_shape=j...  4.22 us
    all_to_all x1, waiting for transfers between devices, local(): lax.all_to_all(sent, ('space', 'mem'), split_axis=0, concat_axis=0, tiled...  4.2 us
    ppermute x12, waiting for transfers between devices, swap(): return lax.ppermute(x, axis, [(i, i ^ bit) for i in range(count)])  4.09 us
    pallas_call x1, Pallas kernels, local(): pl.pallas_call(functools.partial(near_inner_kernel, inner_rows, far), out...  3.82 us
    pallas_call x1, Pallas kernels, local(): pl.pallas_call(functools.partial(gram_kernel, outer_rows, scale, far, cou...  3.5 us
  transfers between devices with their start and end apart: 17, of which 4 were waited for; matrix products, arithmetic and copies ran while one was open for 0% of the time, Pallas kernels for 28%

profile of v6, /device:TPU:0, one launch (start us, length us, event | category | flops | bytes accessed | tf_op | source)
XLA Modules:
  0.0 48.9 jit_solution(1343290145372918749)
XLA Ops:
  0.0 0.0 copy-start.1
  0.0 0.0 copy-start
  0.0 2.3 %edges.1 = (f32[88,256]{1,0:T(8,128)}, f32[88,256]{1,0:T(8,128)}, f32[16,256]{1,0:T(8,128)}, f32[16,256]{1,0:T(8,128)}, f32[16,256]{1,0:T(8,128)}) custom-call(f32[16,3,16,256]{3,2,1,0:T(8,128)} %state.3, f32[16,256]{1,0:T(8,128)} %depth.2, f32[1,8,16,128]{3,2,1,0:T(8,128)} %values.1, f32[1,8,16,128]{3,2,1,0:T(8,128)} %precision.1), custom_call_target="tpu_custom_call" | custom-call | tf_op jit(solution)/shard_map/edges/pallas_call | solution.py:117
  2.3 0.0 copy-done.1
  2.3 0.0 copy-done
  2.3 0.0 copy-start.7
  2.3 0.0 copy-start.9
  2.3 0.0 copy-start.6
  2.3 0.6 %inner.1.refs_0_ = f32[10,16,256]{2,1,0:T(8,128)S(1)} custom-call(f32[16,3,16,256]{3,2,1,0:T(8,128)S(1)} %copy-done, f32[16,256]{1,0:T(8,128)S(1)} %copy-done.1), custom_call_target="tpu_custom_call" | custom-call | flops 2000000000 | bytes 786432 | tf_op jit(solution)/shard_map/inner/pallas_call | solution.py:160
  2.9 0.5 %collective-permute-start = (f32[10,16,256]{2,1,0:T(8,128)S(1)}, f32[10,16,256]{2,1,0:T(8,128)S(1)}, u32[]{:S(2)}, u32[]{:S(2)}) collective-permute-start(f32[10,16,256]{2,1,0:T(8,128)S(1)} %inner.1.refs_0_), channel_id=1, source_target_pairs={{0,1},{1,0},{2,3},{3,2},{4,5},{5,4},{6,7},{7,6},{8,9},{9,8},{10,11... | collective-permute-start | bytes 491528 | tf_op jit(solution)/shard_map/ppermute | solution.py:587
  3.4 0.0 copy-done.7
  3.4 5.7 %collective-permute-start.2 = (f32[88,256]{1,0:T(8,128)S(1)}, f32[88,256]{1,0:T(8,128)S(1)}, u32[]{:S(2)}, u32[]{:S(2)}) collective-permute-start(f32[88,256]{1,0:T(8,128)S(1)} %copy-done.7), channel_id=1, source_target_pairs={{4,0},{8,4},{12,8},{16,12},{20,16},{24,20},{28,24},{0,28},{5,1},{9... | collective-permute-start | bytes 270344 | tf_op jit(solution)/shard_map/ppermute | solution.py:607
  9.2 0.0 copy-done.9
  9.2 0.4 collective-permute-start.3
  9.6 0.0 copy-done.6
  9.6 0.0 copy-start.2
  9.6 0.0 copy-start.3
  9.6 0.6 %collective-permute-start.1 = (f32[88,256]{1,0:T(8,128)S(1)}, f32[88,256]{1,0:T(8,128)S(1)}, u32[]{:S(2)}, u32[]{:S(2)}) collective-permute-start(f32[88,256]{1,0:T(8,128)S(1)} %copy-done.6), channel_id=1, source_target_pairs={{0,4},{4,8},{8,12},{12,16},{16,20},{20,24},{24,28},{28,0},{1,5},{5... | collective-permute-start | bytes 270344 | tf_op jit(solution)/shard_map/ppermute | solution.py:608
  10.3 0.0 collective-permute-done.refs_1_
  10.3 0.0 copy-start.5
  10.3 0.4 collective-permute-start.7
  10.7 2.0 %collective-permute-start.6 = (f32[10,16,256]{2,1,0:T(8,128)S(1)}, f32[10,16,256]{2,1,0:T(8,128)S(1)}, u32[]{:S(2)}, u32[]{:S(2)}) collective-permute-start(f32[10,16,256]{2,1,0:T(8,128)S(1)} %hold.2.refs_0_), channel_id=1, source_target_pairs={{0,2},{1,3},{2,0},{3,1},{4,6},{5,7},{6,4},{7,5},{8,10},{9,11},{10,... | collective-permute-start | bytes 491528 | tf_op jit(solution)/shard_map/ppermute | solution.py:587
  12.7 0.0 copy-done.2
  12.7 0.0 copy-done.3
  12.7 0.0 copy-done.5
  12.7 3.8 %near_inner.1 = (f32[16,32,128]{2,1,0:T(8,128)S(1)}, s32[1,64]{1,0:T(1,128)S(1)}) custom-call(f32[10,16,256]{2,1,0:T(8,128)S(1)} %hold.2.refs_0_, f32[10,16,256]{2,1,0:T(8,128)S(1)} %collective-permute-done.refs_1_, s32[4,64,128]{2,1,0:T(8,128)S(1)} %copy-done.2, f32[4,64,128]{2,1,0:T(8,128)S(1)} %copy-done.3, s32[1,64]{1,0:T(1,128)S(1)} %bitcast.1), custom_call_target="tpu_custom_call" | custom-call | flops 2684354560 | bytes 327680 | tf_op jit(solution)/shard_map/near_inner/pallas_call | solution.py:644
  16.5 0.0 collective-permute-done.2.below.refs_9_
  16.5 0.0 copy-start.8
  16.6 0.0 copy-start.4
  16.6 0.3 collective-permute-done.1.above.refs_8_
  16.9 0.0 collective-permute-done.3.refs_0_
  16.9 0.9 %forecast.1 = (f32[7,16,256]{2,1,0:T(8,128)S(1)}, f32[32,16,256]{2,1,0:T(8,128)S(1)}) custom-call(f32[16,3,16,256]{3,2,1,0:T(8,128)S(1)} %copy-done, f32[16,256]{1,0:T(8,128)S(1)} %copy-done.1, f32[88,256]{1,0:T(8,128)S(1)} %collective-permute-done.1.above.refs_8_, f32[88,256]{1,0:T(8,128)S(1)} %collective-permute-done.2.below.refs_9_, ...), custom_call_target="tpu_custom_call" | custom-call | flops 2000000000 | bytes 786432 | tf_op jit(solution)/shard_map/forecast/pallas_call | solution.py:249
  17.8 0.1 collective-permute-start.8
  17.9 1.3 %collective-permute-start.5 = (f32[7,16,256]{2,1,0:T(8,128)S(1)}, f32[7,16,256]{2,1,0:T(8,128)S(1)}, u32[]{:S(2)}, u32[]{:S(2)}) collective-permute-start(f32[7,16,256]{2,1,0:T(8,128)S(1)} %get-tuple-element.31.refs_2_.refs_4_), channel_id=1, source_target_pairs={{0,3},{1,2},{2,1},{3,0},{4,7},{5,6},{6,5},{7,4},{8,11},{9,10},{10,... | collective-permute-start | bytes 344072 | tf_op jit(solution)/shard_map/ppermute | solution.py:587
  19.1 0.9 %collective-permute-start.4 = (f32[7,16,256]{2,1,0:T(8,128)S(1)}, f32[7,16,256]{2,1,0:T(8,128)S(1)}, u32[]{:S(2)}, u32[]{:S(2)}) collective-permute-start(f32[7,16,256]{2,1,0:T(8,128)S(1)} %get-tuple-element.31.refs_2_.refs_4_), channel_id=1, source_target_pairs={{0,2},{1,3},{2,0},{3,1},{4,6},{5,7},{6,4},{7,5},{8,10},{9,11},{10,... | collective-permute-start | bytes 344072 | tf_op jit(solution)/shard_map/ppermute | solution.py:587
  20.0 0.0 collective-permute-done.8.refs_3_.refs_5_
  20.0 0.0 copy-done.8
  20.0 1.3 %collective-permute-start.9 = (f32[16,256]{1,0:T(8,128)S(1)}, f32[16,256]{1,0:T(8,128)S(1)}, u32[]{:S(2)}, u32[]{:S(2)}) collective-permute-start(f32[16,256]{1,0:T(8,128)S(1)} %copy-done.8), channel_id=1, source_target_pairs={{0,16},{4,20},{8,24},{12,28},{16,0},{20,4},{24,8},{28,12},{1,17},{... | collective-permute-start | bytes 49160 | tf_op jit(solution)/shard_map/ppermute | solution.py:662
  21.3 0.0 collective-permute-done.7.refs_1_.refs_3_
  21.3 0.0 collective-permute-done.6.refs_0_.refs_2_
  21.3 0.0 copy-done.4
  21.3 4.8 %middle.1 = (f32[16,32,128]{2,1,0:T(8,128)S(1)}, f32[16,32,128]{2,1,0:T(8,128)S(1)}, f32[5,16,256]{2,1,0:T(8,128)S(1)}) custom-call(f32[10,16,256]{2,1,0:T(8,128)S(1)} %collective-permute-done.6.refs_0_.refs_2_, f32[10,16,256]{2,1,0:T(8,128)S(1)} %collective-permute-done.7.refs_1_.refs_3_, f32[7,16,256]{2,1,0:T(8,128)S(1)} %get-tuple-element.31.refs_2_.refs_4_, ...), custom_call_target="tpu_custom_call" | custom-call | flops 4294967296 | bytes 524288 | tf_op jit(solution)/shard_map/middle/pallas_call | solution.py:666
  26.0 0.0 collective-permute-done.9.refs_7_.refs_4_
  26.1 0.0 collective-permute-done.5.refs_1_.refs_2_.refs_7_
  26.1 0.0 collective-permute-done.4.refs_0_.refs_1_.refs_6_
  26.1 2.0 %collective-permute-start.12 = (f32[32,16,256]{2,1,0:T(8,128)S(1)}, f32[32,16,256]{2,1,0:T(8,128)S(1)}, u32[]{:S(2)}, u32[]{:S(2)}) collective-permute-start(f32[32,16,256]{2,1,0:T(8,128)S(1)} %hold.3), channel_id=1, source_target_pairs={{0,2},{1,3},{2,0},{3,1},{4,6},{5,7},{6,4},{7,5},{8,10},{9,11},{10,... | collective-permute-start | bytes 1572872 | tf_op jit(solution)/shard_map/ppermute | solution.py:587
  28.1 3.5 %gram.1 = (f32[9,1,128]{2,1,0:T(1,128)S(1)}, f32[9,1,128]{2,1,0:T(1,128)S(1)}) custom-call(s32[1,64]{1,0:T(1,128)S(1)} %get-tuple-element.25.owners, f32[7,16,256]{2,1,0:T(8,128)S(1)} %collective-permute-done.4.refs_0_.refs_1_.refs_6_, f32[7,16,256]{2,1,0:T(8,128)S(1)} %collective-permute-done.5.refs_1_.refs_2_.refs_7_, s32[4,64,128]{2,1,0:T(8,128)S(1)} %copy-done.2, ...), custom_call_target="tpu_custom_call" | custom-call | flops 1610612736 | bytes 196608 | tf_op jit(solution)/shard_map/gram/pallas_call | solution.py:696
  31.6 0.0 collective-permute-start.10
  31.7 0.6 %collective-permute-start.14 = (f32[16,16,256]{2,1,0:T(8,128)S(1)}, f32[16,16,256]{2,1,0:T(8,128)S(1)}, u32[]{:S(2)}, u32[]{:S(2)}) collective-permute-start(f32[16,16,256]{2,1,0:T(8,128)S(1)} %get-tuple-element.43.refs_12_), channel_id=1, source_target_pairs={{0,1},{1,0},{2,3},{3,2},{4,5},{5,4},{6,7},{7,6},{8,9},{9,8},{10,11... | collective-permute-start | bytes 786440 | tf_op jit(solution)/shard_map/ppermute | solution.py:587
  32.2 0.1 collective-permute-start.11
  32.3 0.5 collective-permute-done.10.given
  32.8 0.7 %spread.1 = f32[32,9,1,128]{3,2,1,0:T(1,128)} custom-call(f32[9,1,128]{2,1,0:T(1,128)S(1)} %get-tuple-element.38.keep, f32[9,1,128]{2,1,0:T(1,128)S(1)} %collective-permute-done.10.given), custom_call_target="tpu_custom_call" | custom-call | tf_op jit(solution)/shard_map/spread/pallas_call | solution.py:709
  33.5 2.7 %all-to-all-start = ((f32[32,9,1,128]{3,2,1,0:T(1,128)}), f32[32,9,1,128]{3,2,1,0:T(1,128)S(1)}, u32[]{:S(2)}, u32[]{:S(2)}) async-start(f32[32,9,1,128]{3,2,1,0:T(1,128)} %spread.1), calls=%async_computation | async-start | bytes 294912 | tf_op jit(solution)/shard_map/all_to_all | solution.py:717
  36.3 3.6 %collective-permute-done.12 = f32[32,16,256]{2,1,0:T(8,128)S(1)} collective-permute-done((f32[32,16,256]{2,1,0:T(8,128)S(1)}, f32[32,16,256]{2,1,0:T(8,128)S(1)}, u32[]{:S(2)}, u32[]{:S(2)}) %collective-permute-start.12) | collective-permute-done | bytes 524320 | tf_op jit(solution)/shard_map/ppermute | solution.py:587
  39.9 0.1 collective-permute-start.15
  40.0 0.5 %collective-permute-start.13 = (f32[16,16,256]{2,1,0:T(8,128)S(1)}, f32[16,16,256]{2,1,0:T(8,128)S(1)}, u32[]{:S(2)}, u32[]{:S(2)}) collective-permute-start(f32[16,16,256]{2,1,0:T(8,128)S(1)} %get-tuple-element.42.refs_10_), channel_id=1, source_target_pairs={{0,1},{1,0},{2,3},{3,2},{4,5},{5,4},{6,7},{7,6},{8,9},{9,8},{10,11... | collective-permute-start | bytes 786440 | tf_op jit(solution)/shard_map/ppermute | solution.py:587
  40.5 0.0 collective-permute-done.14.refs_13_
  40.5 0.0 collective-permute-done.11.refs_9_
  40.5 4.2 %all-to-all-done.sums = f32[32,9,1,128]{3,2,1,0:T(1,128)S(1)} async-done(((f32[32,9,1,128]{3,2,1,0:T(1,128)}), f32[32,9,1,128]{3,2,1,0:T(1,128)S(1)}, u32[]{:S(2)}, u32[]{:S(2)}) %all-to-all-start) | async-done | bytes 147488 | tf_op jit(solution)/shard_map/all_to_all | solution.py:717
  44.7 0.0 collective-permute-done.15.refs_15_
  44.7 0.0 collective-permute-done.13.refs_11_
  44.7 4.2 %analysis.1 = f32[16,3,16,256]{3,2,1,0:T(8,128)} custom-call(f32[32,9,1,128]{3,2,1,0:T(1,128)S(1)} %all-to-all-done.sums, f32[10,16,256]{2,1,0:T(8,128)S(1)} %hold.2.refs_0_, f32[10,16,256]{2,1,0:T(8,128)S(1)} %collective-permute-done.refs_1_, f32[10,16,256]{2,1,0:T(8,128)S(1)} %collective-permute-done.6.refs_0_.refs_2_, ...), custom_call_target="tpu_custom_call" | custom-call | tf_op jit(solution)/shard_map/analysis/pallas_call | solution.py:719
  (4 shorter events, 0.1 us)
Async XLA Ops:
  0.0 2.3 %copy-start.1 = (f32[16,256]{1,0:T(8,128)S(1)}, f32[16,256]{1,0:T(8,128)}, u32[]{:S(2)}) copy-start(f32[16,256]{1,0:T(8,128)} %depth.2) | copy-start | bytes 49156
  0.0 2.3 %copy-start = (f32[16,3,16,256]{3,2,1,0:T(8,128)S(1)}, f32[16,3,16,256]{3,2,1,0:T(8,128)}, u32[]{:S(2)}) copy-start(f32[16,3,16,256]{3,2,1,0:T(8,128)} %state.3) | copy-start | bytes 2359300
  2.3 1.1 %copy-start.7 = (f32[88,256]{1,0:T(8,128)S(1)}, f32[88,256]{1,0:T(8,128)}, u32[]{:S(2)}) copy-start(f32[88,256]{1,0:T(8,128)} %get-tuple-element.23) | copy-start | bytes 270340
  2.3 6.9 %copy-start.9 = (f32[16,256]{1,0:T(8,128)S(1)}, f32[16,256]{1,0:T(8,128)}, u32[]{:S(2)}) copy-start(f32[16,256]{1,0:T(8,128)} %get-tuple-element.30) | copy-start | bytes 49156
  2.3 7.3 %copy-start.6 = (f32[88,256]{1,0:T(8,128)S(1)}, f32[88,256]{1,0:T(8,128)}, u32[]{:S(2)}) copy-start(f32[88,256]{1,0:T(8,128)} %get-tuple-element.26) | copy-start | bytes 270340
  2.9 7.4 %collective-permute-start = (f32[10,16,256]{2,1,0:T(8,128)S(1)}, f32[10,16,256]{2,1,0:T(8,128)S(1)}, u32[]{:S(2)}, u32[]{:S(2)}) collective-permute-start(f32[10,16,256]{2,1,0:T(8,128)S(1)} %inner.1.refs_0_), channel_id=1, source_target_pairs={{0,1},{1,0},{2,3},{3,2},{4,5},{5,4},{6,7},{7,6},{8,9},{9,8},{10,11... | collective-permute-start | bytes 491528 | tf_op jit(solution)/shard_map/ppermute | solution.py:587
  3.4 13.1 %collective-permute-start.2 = (f32[88,256]{1,0:T(8,128)S(1)}, f32[88,256]{1,0:T(8,128)S(1)}, u32[]{:S(2)}, u32[]{:S(2)}) collective-permute-start(f32[88,256]{1,0:T(8,128)S(1)} %copy-done.7), channel_id=1, source_target_pairs={{4,0},{8,4},{12,8},{16,12},{20,16},{24,20},{28,24},{0,28},{5,1},{9... | collective-permute-start | bytes 270344 | tf_op jit(solution)/shard_map/ppermute | solution.py:607
  9.2 7.7 %collective-permute-start.3 = (f32[16,256]{1,0:T(8,128)S(1)}, f32[16,256]{1,0:T(8,128)S(1)}, u32[]{:S(2)}, u32[]{:S(2)}) collective-permute-start(f32[16,256]{1,0:T(8,128)S(1)} %copy-done.9), channel_id=1, source_target_pairs={{0,24},{1,9},{2,22},{3,15},{4,28},{5,13},{6,26},{7,19},{8,0},{9,17... | collective-permute-start | bytes 49160 | tf_op jit(solution)/shard_map/ppermute | solution.py:610
  9.6 3.1 %copy-start.2 = (s32[4,64,128]{2,1,0:T(8,128)S(1)}, s32[4,64,128]{2,1,0:T(8,128)}, u32[]{:S(2)}) copy-start(s32[4,64,128]{2,1,0:T(8,128)} %refs_2_.3) | copy-start | bytes 393220
  9.6 3.1 %copy-start.3 = (f32[4,64,128]{2,1,0:T(8,128)S(1)}, f32[4,64,128]{2,1,0:T(8,128)}, u32[]{:S(2)}) copy-start(f32[4,64,128]{2,1,0:T(8,128)} %refs_3_.3) | copy-start | bytes 393220
  9.6 7.2 %collective-permute-start.1 = (f32[88,256]{1,0:T(8,128)S(1)}, f32[88,256]{1,0:T(8,128)S(1)}, u32[]{:S(2)}, u32[]{:S(2)}) collective-permute-start(f32[88,256]{1,0:T(8,128)S(1)} %copy-done.6), channel_id=1, source_target_pairs={{0,4},{4,8},{8,12},{12,16},{16,20},{20,24},{24,28},{28,0},{1,5},{5... | collective-permute-start | bytes 270344 | tf_op jit(solution)/shard_map/ppermute | solution.py:608
  10.3 2.4 %copy-start.5 = (s32[64,1]{0,1:T(1,128)S(1)}, s32[64,1]{0,1:T(1,128)}, u32[]{:S(2)}) copy-start(s32[64,1]{0,1:T(1,128)} %param.11) | copy-start | bytes 772
  10.3 11.0 %collective-permute-start.7 = (f32[10,16,256]{2,1,0:T(8,128)S(1)}, f32[10,16,256]{2,1,0:T(8,128)S(1)}, u32[]{:S(2)}, u32[]{:S(2)}) collective-permute-start(f32[10,16,256]{2,1,0:T(8,128)S(1)} %hold.2.refs_0_), channel_id=1, source_target_pairs={{0,3},{1,2},{2,1},{3,0},{4,7},{5,6},{6,5},{7,4},{8,11},{9,10},{10,... | collective-permute-start | bytes 491528 | tf_op jit(solution)/shard_map/ppermute | solution.py:587
  10.7 10.6 %collective-permute-start.6 = (f32[10,16,256]{2,1,0:T(8,128)S(1)}, f32[10,16,256]{2,1,0:T(8,128)S(1)}, u32[]{:S(2)}, u32[]{:S(2)}) collective-permute-start(f32[10,16,256]{2,1,0:T(8,128)S(1)} %hold.2.refs_0_), channel_id=1, source_target_pairs={{0,2},{1,3},{2,0},{3,1},{4,6},{5,7},{6,4},{7,5},{8,10},{9,11},{10,... | collective-permute-start | bytes 491528 | tf_op jit(solution)/shard_map/ppermute | solution.py:587
  16.5 3.5 %copy-start.8 = (f32[16,256]{1,0:T(8,128)S(1)}, f32[16,256]{1,0:T(8,128)}, u32[]{:S(2)}) copy-start(f32[16,256]{1,0:T(8,128)} %get-tuple-element.37) | copy-start | bytes 49156
  16.6 4.7 %copy-start.4 = (f32[16,256]{1,0:T(8,128)S(1)}, f32[16,256]{1,0:T(8,128)}, u32[]{:S(2)}) copy-start(f32[16,256]{1,0:T(8,128)} %get-tuple-element.32.refs_7_) | copy-start | bytes 49156
  17.8 2.2 %collective-permute-start.8 = (f32[7,16,256]{2,1,0:T(8,128)S(1)}, f32[7,16,256]{2,1,0:T(8,128)S(1)}, u32[]{:S(2)}, u32[]{:S(2)}) collective-permute-start(f32[7,16,256]{2,1,0:T(8,128)S(1)} %get-tuple-element.31.refs_2_.refs_4_), channel_id=1, source_target_pairs={{0,1},{1,0},{2,3},{3,2},{4,5},{5,4},{6,7},{7,6},{8,9},{9,8},{10,11... | collective-permute-start | bytes 344072 | tf_op jit(solution)/shard_map/ppermute | solution.py:587
  17.9 8.2 %collective-permute-start.5 = (f32[7,16,256]{2,1,0:T(8,128)S(1)}, f32[7,16,256]{2,1,0:T(8,128)S(1)}, u32[]{:S(2)}, u32[]{:S(2)}) collective-permute-start(f32[7,16,256]{2,1,0:T(8,128)S(1)} %get-tuple-element.31.refs_2_.refs_4_), channel_id=1, source_target_pairs={{0,3},{1,2},{2,1},{3,0},{4,7},{5,6},{6,5},{7,4},{8,11},{9,10},{10,... | collective-permute-start | bytes 344072 | tf_op jit(solution)/shard_map/ppermute | solution.py:587
  19.1 6.9 %collective-permute-start.4 = (f32[7,16,256]{2,1,0:T(8,128)S(1)}, f32[7,16,256]{2,1,0:T(8,128)S(1)}, u32[]{:S(2)}, u32[]{:S(2)}) collective-permute-start(f32[7,16,256]{2,1,0:T(8,128)S(1)} %get-tuple-element.31.refs_2_.refs_4_), channel_id=1, source_target_pairs={{0,2},{1,3},{2,0},{3,1},{4,6},{5,7},{6,4},{7,5},{8,10},{9,11},{10,... | collective-permute-start | bytes 344072 | tf_op jit(solution)/shard_map/ppermute | solution.py:587
  20.0 6.0 %collective-permute-start.9 = (f32[16,256]{1,0:T(8,128)S(1)}, f32[16,256]{1,0:T(8,128)S(1)}, u32[]{:S(2)}, u32[]{:S(2)}) collective-permute-start(f32[16,256]{1,0:T(8,128)S(1)} %copy-done.8), channel_id=1, source_target_pairs={{0,16},{4,20},{8,24},{12,28},{16,0},{20,4},{24,8},{28,12},{1,17},{... | collective-permute-start | bytes 49160 | tf_op jit(solution)/shard_map/ppermute | solution.py:662
  26.1 13.8 %collective-permute-start.12 = (f32[32,16,256]{2,1,0:T(8,128)S(1)}, f32[32,16,256]{2,1,0:T(8,128)S(1)}, u32[]{:S(2)}, u32[]{:S(2)}) collective-permute-start(f32[32,16,256]{2,1,0:T(8,128)S(1)} %hold.3), channel_id=1, source_target_pairs={{0,2},{1,3},{2,0},{3,1},{4,6},{5,7},{6,4},{7,5},{8,10},{9,11},{10,... | collective-permute-start | bytes 1572872 | tf_op jit(solution)/shard_map/ppermute | solution.py:587
  31.6 1.2 %collective-permute-start.10 = (f32[9,1,128]{2,1,0:T(1,128)S(1)}, f32[9,1,128]{2,1,0:T(1,128)S(1)}, u32[]{:S(2)}, u32[]{:S(2)}) collective-permute-start(f32[9,1,128]{2,1,0:T(1,128)S(1)} %get-tuple-element.39), channel_id=1, source_target_pairs={{0,1},{1,0},{2,3},{3,2},{4,5},{5,4},{6,7},{7,6},{8,9},{9,8},{10,11... | collective-permute-start | bytes 13832 | tf_op jit(solution)/shard_map/ppermute | solution.py:587
  31.7 8.8 %collective-permute-start.14 = (f32[16,16,256]{2,1,0:T(8,128)S(1)}, f32[16,16,256]{2,1,0:T(8,128)S(1)}, u32[]{:S(2)}, u32[]{:S(2)}) collective-permute-start(f32[16,16,256]{2,1,0:T(8,128)S(1)} %get-tuple-element.43.refs_12_), channel_id=1, source_target_pairs={{0,1},{1,0},{2,3},{3,2},{4,5},{5,4},{6,7},{7,6},{8,9},{9,8},{10,11... | collective-permute-start | bytes 786440 | tf_op jit(solution)/shard_map/ppermute | solution.py:587
  32.2 8.2 %collective-permute-start.11 = (f32[16,16,256]{2,1,0:T(8,128)S(1)}, f32[16,16,256]{2,1,0:T(8,128)S(1)}, u32[]{:S(2)}, u32[]{:S(2)}) collective-permute-start(f32[16,16,256]{2,1,0:T(8,128)S(1)} %get-tuple-element.44.refs_8_), channel_id=1, source_target_pairs={{0,1},{1,0},{2,3},{3,2},{4,5},{5,4},{6,7},{7,6},{8,9},{9,8},{10,11... | collective-permute-start | bytes 786440 | tf_op jit(solution)/shard_map/ppermute | solution.py:587
  33.5 11.2 %all-to-all-start = ((f32[32,9,1,128]{3,2,1,0:T(1,128)}), f32[32,9,1,128]{3,2,1,0:T(1,128)S(1)}, u32[]{:S(2)}, u32[]{:S(2)}) async-start(f32[32,9,1,128]{3,2,1,0:T(1,128)} %spread.1), calls=%async_computation | async-start | bytes 294912 | tf_op jit(solution)/shard_map/all_to_all | solution.py:717
  39.9 4.8 %collective-permute-start.15 = (f32[16,16,256]{2,1,0:T(8,128)S(1)}, f32[16,16,256]{2,1,0:T(8,128)S(1)}, u32[]{:S(2)}, u32[]{:S(2)}) collective-permute-start(f32[16,16,256]{2,1,0:T(8,128)S(1)} %get-tuple-element.41.refs_14_), channel_id=1, source_target_pairs={{0,1},{1,0},{2,3},{3,2},{4,5},{5,4},{6,7},{7,6},{8,9},{9,8},{10,11... | collective-permute-start | bytes 786440 | tf_op jit(solution)/shard_map/ppermute | solution.py:587
  40.0 4.7 %collective-permute-start.13 = (f32[16,16,256]{2,1,0:T(8,128)S(1)}, f32[16,16,256]{2,1,0:T(8,128)S(1)}, u32[]{:S(2)}, u32[]{:S(2)}) collective-permute-start(f32[16,16,256]{2,1,0:T(8,128)S(1)} %get-tuple-element.42.refs_10_), channel_id=1, source_target_pairs={{0,1},{1,0},{2,3},{3,2},{4,5},{5,4},{6,7},{7,6},{8,9},{9,8},{10,11... | collective-permute-start | bytes 786440 | tf_op jit(solution)/shard_map/ppermute | solution.py:587

commit v7 on v6

--- a/solution.py
+++ b/solution.py
@@ -640,7 +640,6 @@
     inner[near] = swap(inner[0], "mem", near)
     (inner[0],) = hold([inner[0]], inner[near])
     inner[far] = swap(inner[0], "mem", far)
-    inner[far + near] = swap(inner[0], "mem", far + near)
     first, owners = pl.pallas_call(
         functools.partial(near_inner_kernel, inner_rows, far),
         out_shape=(early, jax.ShapeDtypeStruct(owners.shape, owners.dtype)),
@@ -653,6 +652,8 @@
 
     above, below = (after(x, first) for x in (above, below))
     height, *parts = forecast(ends, state, depth, above, below, held)
+    (inner[far],) = hold([inner[far]], height)
+    inner[far + near] = swap(inner[far], "mem", near)
     outer = {0: height}
     outer[far] = swap(height, "mem", far)
     direct = []
@@ -681,7 +682,6 @@
         above,
         below,
     )
-    parts = hold(parts, outer[far], outer[far + near], second, *direct)
     both = {0: parts[0], far: swap(parts[0], "mem", far)}
     winds = [{k: x[i * rows : (i + 1) * rows] for k, x in both.items()} for i in range(2)]
     for wind in winds:
@@ -704,16 +704,10 @@
             pltpu.VMEM((count,) + near_shape[1:], F32),
         ],
         name="gram",
-        **work(outer_rows),
+        compiler_params=PARAMS,
+        cost_estimate=cost(1000, 1000),
     )(owners, *outer[far:], obs_cells, obs_weights, near_blocks, first, second, *direct)
-    sent = pl.pallas_call(
-        spread_kernel,
-        out_shape=jax.ShapeDtypeStruct((devices,) + part.shape, F32),
-        in_specs=[VMEM, VMEM],
-        out_specs=VMEM,
-        compiler_params=PARAMS,
-        name="spread",
-    )(keep, swap(give, "mem", near))
+    sent = jnp.broadcast_to(keep + swap(give, "mem", near), (devices,) + part.shape)
     sums = lax.all_to_all(sent, ("space", "mem"), split_axis=0, concat_axis=0, tiled=True)
 
     return pl.pallas_call(

time: 49.1 us -> 48.6 us (0.990)
  local copies, waits for them, and re-layouts: 0.11 us -> 1.89 us
  waiting for transfers between devices: 8.59 us -> 7.66 us
  Pallas kernels: 20.8 us -> 20.1 us
  starting transfers between devices: 19.2 us -> 18.6 us
    ppermute x12, waiting for transfers between devices: 4.09 us -> 2.38 us  [swap(): return lax.ppermute(x, axis, [(i, i ^ bit) for i in range(count)])]
    ppermute x12, starting transfers between devices: 8.39 us -> 7.28 us  [swap(): return lax.ppermute(x, axis, [(i, i ^ bit) for i in range(count)])]
    slice x2, local copies, waits for them, and re-layouts: 0.07 us -> 1.1 us  [local(): x[i * rows:(i + 1) * rows]]
    broadcast_in_dim x0 -> x1, local copies, waits for them, and re-layouts: none -> 0.74 us  [local(): jnp.broadcast_to(keep + swap(give, 'mem', near), (devices,) + part.shape)]
    pallas_call x1 -> x0, Pallas kernels: 0.74 us -> none  [local(): pl.pallas_call(spread_kernel, out_shape=jax.ShapeDtypeStruct((devices,) +...]
    all_to_all x1, waiting for transfers between devices: 4.2 us -> 4.88 us  [local(): lax.all_to_all(sent, ('space', 'mem'), split_axis=0, concat_axis=0, tiled...]
    all_to_all x1, starting transfers between devices: 2.73 us -> 3.24 us  [local(): lax.all_to_all(sent, ('space', 'mem'), split_axis=0, concat_axis=0, tiled...]
  transfers between devices with their start and end apart: 17 -> 17, of which waited for: 4 -> 4; matrix products, arithmetic and copies ran while one was open for 0% -> 4% of each run, Pallas kernels for 28% -> 27%
where the time goes in v7:
time: 48.6 us; the launch traced here: 48.4 us
  Pallas kernels  20.1 us (41%)
  starting transfers between devices  18.6 us (38%)
  waiting for transfers between devices  7.66 us (16%)
  local copies, waits for them, and re-layouts  1.89 us (4%)
    ppermute x12, starting transfers between devices, swap(): return lax.ppermute(x, axis, [(i, i ^ bit) for i in range(count)])  7.28 us
    ppermute x1, starting transfers between devices, local(): lax.ppermute(to_above, 'space', [((i + 1) % count, i) for i in range(coun...  5.74 us
    all_to_all x1, waiting for transfers between devices, local(): lax.all_to_all(sent, ('space', 'mem'), split_axis=0, concat_axis=0, tiled...  4.88 us
    pallas_call x1, Pallas kernels, local(): pl.pallas_call(functools.partial(middle_kernel, inner_rows, outer_rows, f...  4.77 us
    pallas_call x1, Pallas kernels, local(): pl.pallas_call(functools.partial(analysis_kernel, count_mem), out_shape=j...  4.22 us
    pallas_call x1, Pallas kernels, local(): pl.pallas_call(functools.partial(near_inner_kernel, inner_rows, far), out...  3.83 us
    pallas_call x1, Pallas kernels, local(): pl.pallas_call(functools.partial(gram_kernel, outer_rows, scale, far, cou...  3.49 us
    all_to_all x1, starting transfers between devices, local(): lax.all_to_all(sent, ('space', 'mem'), split_axis=0, concat_axis=0, tiled...  3.24 us
  transfers between devices with their start and end apart: 17, of which 4 were waited for; matrix products, arithmetic and copies ran while one was open for 4% of the time, Pallas kernels for 27%

profile of v7, /device:TPU:0, one launch (start us, length us, event | category | flops | bytes accessed | tf_op | source)
XLA Modules:
  0.0 48.4 jit_solution(3915212742685196972)
XLA Ops:
  0.0 0.0 copy-start.3
  0.0 0.0 copy-start
  0.0 2.3 %edges.1 = (f32[88,256]{1,0:T(8,128)}, f32[88,256]{1,0:T(8,128)}, f32[16,256]{1,0:T(8,128)}, f32[16,256]{1,0:T(8,128)}, f32[16,256]{1,0:T(8,128)}) custom-call(f32[16,3,16,256]{3,2,1,0:T(8,128)} %state.3, f32[16,256]{1,0:T(8,128)} %depth.2, f32[1,8,16,128]{3,2,1,0:T(8,128)} %values.1, f32[1,8,16,128]{3,2,1,0:T(8,128)} %precision.1), custom_call_target="tpu_custom_call" | custom-call | tf_op jit(solution)/shard_map/edges/pallas_call | solution.py:117
  2.3 0.0 copy-done.3
  2.3 0.0 copy-done
  2.3 0.0 copy-start.7
  2.3 0.0 copy-start.9
  2.3 0.0 copy-start.6
  2.3 0.6 %inner.1.refs_0_ = f32[10,16,256]{2,1,0:T(8,128)S(1)} custom-call(f32[16,3,16,256]{3,2,1,0:T(8,128)S(1)} %copy-done, f32[16,256]{1,0:T(8,128)S(1)} %copy-done.3), custom_call_target="tpu_custom_call" | custom-call | flops 2000000000 | bytes 786432 | tf_op jit(solution)/shard_map/inner/pallas_call | solution.py:160
  2.9 0.5 %collective-permute-start = (f32[10,16,256]{2,1,0:T(8,128)S(1)}, f32[10,16,256]{2,1,0:T(8,128)S(1)}, u32[]{:S(2)}, u32[]{:S(2)}) collective-permute-start(f32[10,16,256]{2,1,0:T(8,128)S(1)} %inner.1.refs_0_), channel_id=1, source_target_pairs={{0,1},{1,0},{2,3},{3,2},{4,5},{5,4},{6,7},{7,6},{8,9},{9,8},{10,11... | collective-permute-start | bytes 491528 | tf_op jit(solution)/shard_map/ppermute | solution.py:587
  3.4 0.0 copy-done.7
  3.4 5.7 %collective-permute-start.2 = (f32[88,256]{1,0:T(8,128)S(1)}, f32[88,256]{1,0:T(8,128)S(1)}, u32[]{:S(2)}, u32[]{:S(2)}) collective-permute-start(f32[88,256]{1,0:T(8,128)S(1)} %copy-done.7), channel_id=1, source_target_pairs={{4,0},{8,4},{12,8},{16,12},{20,16},{24,20},{28,24},{0,28},{5,1},{9... | collective-permute-start | bytes 270344 | tf_op jit(solution)/shard_map/ppermute | solution.py:607
  9.2 0.0 copy-done.9
  9.2 0.4 collective-permute-start.3
  9.6 0.0 copy-done.6
  9.6 0.0 copy-start.1
  9.6 0.0 copy-start.2
  9.6 0.6 %collective-permute-start.1 = (f32[88,256]{1,0:T(8,128)S(1)}, f32[88,256]{1,0:T(8,128)S(1)}, u32[]{:S(2)}, u32[]{:S(2)}) collective-permute-start(f32[88,256]{1,0:T(8,128)S(1)} %copy-done.6), channel_id=1, source_target_pairs={{0,4},{4,8},{8,12},{12,16},{16,20},{20,24},{24,28},{28,0},{1,5},{5... | collective-permute-start | bytes 270344 | tf_op jit(solution)/shard_map/ppermute | solution.py:608
  10.3 0.0 collective-permute-done.refs_1_
  10.3 0.0 copy-start.5
  10.3 2.3 %collective-permute-start.6 = (f32[10,16,256]{2,1,0:T(8,128)S(1)}, f32[10,16,256]{2,1,0:T(8,128)S(1)}, u32[]{:S(2)}, u32[]{:S(2)}) collective-permute-start(f32[10,16,256]{2,1,0:T(8,128)S(1)} %hold.2.refs_0_), channel_id=1, source_target_pairs={{0,2},{1,3},{2,0},{3,1},{4,6},{5,7},{6,4},{7,5},{8,10},{9,11},{10,... | collective-permute-start | bytes 491528 | tf_op jit(solution)/shard_map/ppermute | solution.py:587
  12.6 0.0 copy-done.1
  12.6 0.0 copy-done.2
  12.6 0.0 copy-done.5
  12.6 3.8 %near_inner.1 = (f32[16,32,128]{2,1,0:T(8,128)S(1)}, s32[1,64]{1,0:T(1,128)S(1)}) custom-call(f32[10,16,256]{2,1,0:T(8,128)S(1)} %hold.2.refs_0_, f32[10,16,256]{2,1,0:T(8,128)S(1)} %collective-permute-done.refs_1_, s32[4,64,128]{2,1,0:T(8,128)S(1)} %copy-done.1, f32[4,64,128]{2,1,0:T(8,128)S(1)} %copy-done.2, s32[1,64]{1,0:T(1,128)S(1)} %bitcast.4), custom_call_target="tpu_custom_call" | custom-call | flops 2684354560 | bytes 327680 | tf_op jit(solution)/shard_map/near_inner/pallas_call | solution.py:643
  16.5 0.0 collective-permute-done.2.below.refs_9_
  16.5 0.4 collective-permute-done.1.above.refs_8_
  16.9 0.0 collective-permute-done.3.refs_0_
  16.9 0.9 %forecast.1 = (f32[7,16,256]{2,1,0:T(8,128)S(1)}, f32[32,16,256]{2,1,0:T(8,128)S(1)}) custom-call(f32[16,3,16,256]{3,2,1,0:T(8,128)S(1)} %copy-done, f32[16,256]{1,0:T(8,128)S(1)} %copy-done.3, f32[88,256]{1,0:T(8,128)S(1)} %collective-permute-done.1.above.refs_8_, f32[88,256]{1,0:T(8,128)S(1)} %collective-permute-done.2.below.refs_9_, ...), custom_call_target="tpu_custom_call" | custom-call | flops 2000000000 | bytes 786432 | tf_op jit(solution)/shard_map/forecast/pallas_call | solution.py:249
  17.8 0.0 collective-permute-done.6.refs_0_
  17.8 0.0 copy-start.8
  17.8 0.0 copy-start.4
  17.8 0.1 collective-permute-start.7
  17.9 0.5 %collective-permute-start.8 = (f32[7,16,256]{2,1,0:T(8,128)S(1)}, f32[7,16,256]{2,1,0:T(8,128)S(1)}, u32[]{:S(2)}, u32[]{:S(2)}) collective-permute-start(f32[7,16,256]{2,1,0:T(8,128)S(1)} %get-tuple-element.31.refs_1_.refs_2_.refs_4_), channel_id=1, source_target_pairs={{0,1},{1,0},{2,3},{3,2},{4,5},{5,4},{6,7},{7,6},{8,9},{9,8},{10,11... | collective-permute-start | bytes 344072 | tf_op jit(solution)/shard_map/ppermute | solution.py:587
  18.4 0.8 %collective-permute-start.5 = (f32[7,16,256]{2,1,0:T(8,128)S(1)}, f32[7,16,256]{2,1,0:T(8,128)S(1)}, u32[]{:S(2)}, u32[]{:S(2)}) collective-permute-start(f32[7,16,256]{2,1,0:T(8,128)S(1)} %get-tuple-element.31.refs_1_.refs_2_.refs_4_), channel_id=1, source_target_pairs={{0,3},{1,2},{2,1},{3,0},{4,7},{5,6},{6,5},{7,4},{8,11},{9,10},{10,... | collective-permute-start | bytes 344072 | tf_op jit(solution)/shard_map/ppermute | solution.py:587
  19.2 0.9 %collective-permute-start.4 = (f32[7,16,256]{2,1,0:T(8,128)S(1)}, f32[7,16,256]{2,1,0:T(8,128)S(1)}, u32[]{:S(2)}, u32[]{:S(2)}) collective-permute-start(f32[7,16,256]{2,1,0:T(8,128)S(1)} %get-tuple-element.31.refs_1_.refs_2_.refs_4_), channel_id=1, source_target_pairs={{0,2},{1,3},{2,0},{3,1},{4,6},{5,7},{6,4},{7,5},{8,10},{9,11},{10,... | collective-permute-start | bytes 344072 | tf_op jit(solution)/shard_map/ppermute | solution.py:587
  20.1 0.0 copy-done.8
  20.1 1.2 %collective-permute-start.9 = (f32[16,256]{1,0:T(8,128)S(1)}, f32[16,256]{1,0:T(8,128)S(1)}, u32[]{:S(2)}, u32[]{:S(2)}) collective-permute-start(f32[16,256]{1,0:T(8,128)S(1)} %copy-done.8), channel_id=1, source_target_pairs={{0,16},{4,20},{8,24},{12,28},{16,0},{20,4},{24,8},{28,12},{1,17},{... | collective-permute-start | bytes 49160 | tf_op jit(solution)/shard_map/ppermute | solution.py:663
  21.3 0.0 collective-permute-done.8.refs_3_.refs_5_
  21.3 0.9 %collective-permute-start.12 = (f32[32,16,256]{2,1,0:T(8,128)S(1)}, f32[32,16,256]{2,1,0:T(8,128)}, u32[]{:S(2)}, u32[]{:S(2)}) collective-permute-start(f32[32,16,256]{2,1,0:T(8,128)S(1)} %get-tuple-element.40), channel_id=1, source_target_pairs={{0,2},{1,3},{2,0},{3,1},{4,6},{5,7},{6,4},{7,5},{8,10},{9,11},{10,... | collective-permute-start | bytes 1572872 | tf_op jit(solution)/shard_map/ppermute | solution.py:587
  22.3 0.0 collective-permute-done.7.refs_1_.refs_3_
  22.3 0.0 copy-done.4
  22.3 4.8 %middle.1 = (f32[16,32,128]{2,1,0:T(8,128)S(1)}, f32[16,32,128]{2,1,0:T(8,128)S(1)}, f32[5,16,256]{2,1,0:T(8,128)S(1)}) custom-call(f32[10,16,256]{2,1,0:T(8,128)S(1)} %hold.3.refs_0_.refs_2_, f32[10,16,256]{2,1,0:T(8,128)S(1)} %collective-permute-done.7.refs_1_.refs_3_, f32[7,16,256]{2,1,0:T(8,128)S(1)} %get-tuple-element.31.refs_1_.refs_2_.refs_4_, ...), custom_call_target="tpu_custom_call" | custom-call | flops 4294967296 | bytes 524288 | tf_op jit(solution)/shard_map/middle/pallas_call | solution.py:667
  27.0 0.0 collective-permute-done.9.refs_7_
  27.1 0.0 collective-permute-done.5.refs_1_.refs_7_
  27.1 0.0 collective-permute-done.4.refs_0_.refs_6_
  27.1 3.5 %gram.1 = (f32[9,1,128]{2,1,0:T(1,128)S(1)}, f32[9,1,128]{2,1,0:T(1,128)S(1)}) custom-call(s32[1,64]{1,0:T(1,128)S(1)} %get-tuple-element.25.owners, f32[7,16,256]{2,1,0:T(8,128)S(1)} %collective-permute-done.4.refs_0_.refs_6_, f32[7,16,256]{2,1,0:T(8,128)S(1)} %collective-permute-done.5.refs_1_.refs_7_, s32[4,64,128]{2,1,0:T(8,128)S(1)} %copy-done.1, ...), custom_call_target="tpu_custom_call" | custom-call | flops 1000 | bytes 1000 | tf_op jit(solution)/shard_map/gram/pallas_call | solution.py:696
  30.6 0.0 collective-permute-start.10
  30.6 0.6 %collective-permute-start.14 = (f32[16,16,256]{2,1,0:T(8,128)S(1)}, f32[16,16,256]{2,1,0:T(8,128)S(1)}, u32[]{:S(2)}, u32[]{:S(2)}) collective-permute-start(f32[16,16,256]{2,1,0:T(8,128)S(1)} %get-tuple-element.43.refs_12_), channel_id=1, source_target_pairs={{0,1},{1,0},{2,3},{3,2},{4,5},{5,4},{6,7},{7,6},{8,9},{9,8},{10,11... | collective-permute-start | bytes 786440 | tf_op jit(solution)/shard_map/ppermute | solution.py:587
  31.2 0.1 collective-permute-start.11
  31.3 0.5 collective-permute-done.10
  31.8 0.7 %broadcast_in_dim.3 = f32[32,9,1,128]{3,2,1,0:T(1,128)} broadcast(f32[9,128]{1,0:T(8,128)S(1)} %bitcast.5), dimensions={1,3} | broadcast | bytes 152064 | tf_op jit(solution)/shard_map/broadcast_in_dim | solution.py:710
  32.5 3.2 %all-to-all-start = ((f32[32,9,1,128]{3,2,1,0:T(1,128)}), f32[32,9,1,128]{3,2,1,0:T(1,128)S(1)}, u32[]{:S(2)}, u32[]{:S(2)}) async-start(f32[32,9,1,128]{3,2,1,0:T(1,128)} %broadcast_in_dim.3), calls=%async_computation | async-start | bytes 294912 | tf_op jit(solution)/shard_map/all_to_all | solution.py:711
  35.8 1.9 %collective-permute-done.12 = f32[32,16,256]{2,1,0:T(8,128)} collective-permute-done((f32[32,16,256]{2,1,0:T(8,128)S(1)}, f32[32,16,256]{2,1,0:T(8,128)}, u32[]{:S(2)}, u32[]{:S(2)}) %collective-permute-start.12) | collective-permute-done | bytes 524320 | tf_op jit(solution)/shard_map/ppermute | solution.py:587
  37.6 1.1 %fusion = (f32[16,16,256]{2,1,0:T(8,128)S(1)}, f32[16,16,256]{2,1,0:T(8,128)S(1)}) fusion(f32[32,16,256]{2,1,0:T(8,128)} %collective-permute-done.12), kind=kLoop, calls=%fused_computation.1 | loop fusion | bytes 1048576 | tf_op jit(solution)/shard_map/slice | solution.py:686
  38.7 0.1 collective-permute-start.15
  38.8 0.5 %collective-permute-start.13 = (f32[16,16,256]{2,1,0:T(8,128)S(1)}, f32[16,16,256]{2,1,0:T(8,128)S(1)}, u32[]{:S(2)}, u32[]{:S(2)}) collective-permute-start(f32[16,16,256]{2,1,0:T(8,128)S(1)} %get-tuple-element.42.refs_10_), channel_id=1, source_target_pairs={{0,1},{1,0},{2,3},{3,2},{4,5},{5,4},{6,7},{7,6},{8,9},{9,8},{10,11... | collective-permute-start | bytes 786440 | tf_op jit(solution)/shard_map/ppermute | solution.py:587
  39.3 0.0 collective-permute-done.14.refs_13_
  39.3 0.0 collective-permute-done.11.refs_9_
  39.3 4.9 %all-to-all-done.sums = f32[32,9,1,128]{3,2,1,0:T(1,128)S(1)} async-done(((f32[32,9,1,128]{3,2,1,0:T(1,128)}), f32[32,9,1,128]{3,2,1,0:T(1,128)S(1)}, u32[]{:S(2)}, u32[]{:S(2)}) %all-to-all-start) | async-done | bytes 147488 | tf_op jit(solution)/shard_map/all_to_all | solution.py:711
  44.2 0.0 collective-permute-done.15.refs_15_
  44.2 0.0 collective-permute-done.13.refs_11_
  44.2 4.2 %analysis.1 = f32[16,3,16,256]{3,2,1,0:T(8,128)} custom-call(f32[32,9,1,128]{3,2,1,0:T(1,128)S(1)} %all-to-all-done.sums, f32[10,16,256]{2,1,0:T(8,128)S(1)} %hold.2.refs_0_, f32[10,16,256]{2,1,0:T(8,128)S(1)} %collective-permute-done.refs_1_, f32[10,16,256]{2,1,0:T(8,128)S(1)} %hold.3.refs_0_.refs_2_, ...), custom_call_target="tpu_custom_call" | custom-call | tf_op jit(solution)/shard_map/analysis/pallas_call | solution.py:713
  (5 shorter events, 0.1 us)
Async XLA Ops:
  0.0 2.3 %copy-start.3 = (f32[16,256]{1,0:T(8,128)S(1)}, f32[16,256]{1,0:T(8,128)}, u32[]{:S(2)}) copy-start(f32[16,256]{1,0:T(8,128)} %depth.2) | copy-start | bytes 49156
  0.0 2.3 %copy-start = (f32[16,3,16,256]{3,2,1,0:T(8,128)S(1)}, f32[16,3,16,256]{3,2,1,0:T(8,128)}, u32[]{:S(2)}) copy-start(f32[16,3,16,256]{3,2,1,0:T(8,128)} %state.3) | copy-start | bytes 2359300
  2.3 1.1 %copy-start.7 = (f32[88,256]{1,0:T(8,128)S(1)}, f32[88,256]{1,0:T(8,128)}, u32[]{:S(2)}) copy-start(f32[88,256]{1,0:T(8,128)} %get-tuple-element.23) | copy-start | bytes 270340
  2.3 6.9 %copy-start.9 = (f32[16,256]{1,0:T(8,128)S(1)}, f32[16,256]{1,0:T(8,128)}, u32[]{:S(2)}) copy-start(f32[16,256]{1,0:T(8,128)} %get-tuple-element.30) | copy-start | bytes 49156
  2.3 7.3 %copy-start.6 = (f32[88,256]{1,0:T(8,128)S(1)}, f32[88,256]{1,0:T(8,128)}, u32[]{:S(2)}) copy-start(f32[88,256]{1,0:T(8,128)} %get-tuple-element.26) | copy-start | bytes 270340
  2.9 7.4 %collective-permute-start = (f32[10,16,256]{2,1,0:T(8,128)S(1)}, f32[10,16,256]{2,1,0:T(8,128)S(1)}, u32[]{:S(2)}, u32[]{:S(2)}) collective-permute-start(f32[10,16,256]{2,1,0:T(8,128)S(1)} %inner.1.refs_0_), channel_id=1, source_target_pairs={{0,1},{1,0},{2,3},{3,2},{4,5},{5,4},{6,7},{7,6},{8,9},{9,8},{10,11... | collective-permute-start | bytes 491528 | tf_op jit(solution)/shard_map/ppermute | solution.py:587
  3.4 13.0 %collective-permute-start.2 = (f32[88,256]{1,0:T(8,128)S(1)}, f32[88,256]{1,0:T(8,128)S(1)}, u32[]{:S(2)}, u32[]{:S(2)}) collective-permute-start(f32[88,256]{1,0:T(8,128)S(1)} %copy-done.7), channel_id=1, source_target_pairs={{4,0},{8,4},{12,8},{16,12},{20,16},{24,20},{28,24},{0,28},{5,1},{9... | collective-permute-start | bytes 270344 | tf_op jit(solution)/shard_map/ppermute | solution.py:607
  9.2 7.7 %collective-permute-start.3 = (f32[16,256]{1,0:T(8,128)S(1)}, f32[16,256]{1,0:T(8,128)S(1)}, u32[]{:S(2)}, u32[]{:S(2)}) collective-permute-start(f32[16,256]{1,0:T(8,128)S(1)} %copy-done.9), channel_id=1, source_target_pairs={{0,24},{1,9},{2,22},{3,15},{4,28},{5,13},{6,26},{7,19},{8,0},{9,17... | collective-permute-start | bytes 49160 | tf_op jit(solution)/shard_map/ppermute | solution.py:610
  9.6 3.0 %copy-start.1 = (s32[4,64,128]{2,1,0:T(8,128)S(1)}, s32[4,64,128]{2,1,0:T(8,128)}, u32[]{:S(2)}) copy-start(s32[4,64,128]{2,1,0:T(8,128)} %refs_2_.3) | copy-start | bytes 393220
  9.6 3.0 %copy-start.2 = (f32[4,64,128]{2,1,0:T(8,128)S(1)}, f32[4,64,128]{2,1,0:T(8,128)}, u32[]{:S(2)}) copy-start(f32[4,64,128]{2,1,0:T(8,128)} %refs_3_.3) | copy-start | bytes 393220
  9.6 7.2 %collective-permute-start.1 = (f32[88,256]{1,0:T(8,128)S(1)}, f32[88,256]{1,0:T(8,128)S(1)}, u32[]{:S(2)}, u32[]{:S(2)}) collective-permute-start(f32[88,256]{1,0:T(8,128)S(1)} %copy-done.6), channel_id=1, source_target_pairs={{0,4},{4,8},{8,12},{12,16},{16,20},{20,24},{24,28},{28,0},{1,5},{5... | collective-permute-start | bytes 270344 | tf_op jit(solution)/shard_map/ppermute | solution.py:608
  10.3 2.3 %copy-start.5 = (s32[64,1]{0,1:T(1,128)S(1)}, s32[64,1]{0,1:T(1,128)}, u32[]{:S(2)}) copy-start(s32[64,1]{0,1:T(1,128)} %param.11) | copy-start | bytes 772
  10.3 7.5 %collective-permute-start.6 = (f32[10,16,256]{2,1,0:T(8,128)S(1)}, f32[10,16,256]{2,1,0:T(8,128)S(1)}, u32[]{:S(2)}, u32[]{:S(2)}) collective-permute-start(f32[10,16,256]{2,1,0:T(8,128)S(1)} %hold.2.refs_0_), channel_id=1, source_target_pairs={{0,2},{1,3},{2,0},{3,1},{4,6},{5,7},{6,4},{7,5},{8,10},{9,11},{10,... | collective-permute-start | bytes 491528 | tf_op jit(solution)/shard_map/ppermute | solution.py:587
  17.8 2.3 %copy-start.8 = (f32[16,256]{1,0:T(8,128)S(1)}, f32[16,256]{1,0:T(8,128)}, u32[]{:S(2)}) copy-start(f32[16,256]{1,0:T(8,128)} %get-tuple-element.37) | copy-start | bytes 49156
  17.8 4.5 %copy-start.4 = (f32[16,256]{1,0:T(8,128)S(1)}, f32[16,256]{1,0:T(8,128)}, u32[]{:S(2)}) copy-start(f32[16,256]{1,0:T(8,128)} %get-tuple-element.32.refs_7_) | copy-start | bytes 49156
  17.8 4.4 %collective-permute-start.7 = (f32[10,16,256]{2,1,0:T(8,128)S(1)}, f32[10,16,256]{2,1,0:T(8,128)S(1)}, u32[]{:S(2)}, u32[]{:S(2)}) collective-permute-start(f32[10,16,256]{2,1,0:T(8,128)S(1)} %hold.3.refs_0_.refs_2_), channel_id=1, source_target_pairs={{0,1},{1,0},{2,3},{3,2},{4,5},{5,4},{6,7},{7,6},{8,9},{9,8},{10,11... | collective-permute-start | bytes 491528 | tf_op jit(solution)/shard_map/ppermute | solution.py:587
  17.9 3.4 %collective-permute-start.8 = (f32[7,16,256]{2,1,0:T(8,128)S(1)}, f32[7,16,256]{2,1,0:T(8,128)S(1)}, u32[]{:S(2)}, u32[]{:S(2)}) collective-permute-start(f32[7,16,256]{2,1,0:T(8,128)S(1)} %get-tuple-element.31.refs_1_.refs_2_.refs_4_), channel_id=1, source_target_pairs={{0,1},{1,0},{2,3},{3,2},{4,5},{5,4},{6,7},{7,6},{8,9},{9,8},{10,11... | collective-permute-start | bytes 344072 | tf_op jit(solution)/shard_map/ppermute | solution.py:587
  18.4 8.7 %collective-permute-start.5 = (f32[7,16,256]{2,1,0:T(8,128)S(1)}, f32[7,16,256]{2,1,0:T(8,128)S(1)}, u32[]{:S(2)}, u32[]{:S(2)}) collective-permute-start(f32[7,16,256]{2,1,0:T(8,128)S(1)} %get-tuple-element.31.refs_1_.refs_2_.refs_4_), channel_id=1, source_target_pairs={{0,3},{1,2},{2,1},{3,0},{4,7},{5,6},{6,5},{7,4},{8,11},{9,10},{10,... | collective-permute-start | bytes 344072 | tf_op jit(solution)/shard_map/ppermute | solution.py:587
  19.2 7.8 %collective-permute-start.4 = (f32[7,16,256]{2,1,0:T(8,128)S(1)}, f32[7,16,256]{2,1,0:T(8,128)S(1)}, u32[]{:S(2)}, u32[]{:S(2)}) collective-permute-start(f32[7,16,256]{2,1,0:T(8,128)S(1)} %get-tuple-element.31.refs_1_.refs_2_.refs_4_), channel_id=1, source_target_pairs={{0,2},{1,3},{2,0},{3,1},{4,6},{5,7},{6,4},{7,5},{8,10},{9,11},{10,... | collective-permute-start | bytes 344072 | tf_op jit(solution)/shard_map/ppermute | solution.py:587
  20.1 6.9 %collective-permute-start.9 = (f32[16,256]{1,0:T(8,128)S(1)}, f32[16,256]{1,0:T(8,128)S(1)}, u32[]{:S(2)}, u32[]{:S(2)}) collective-permute-start(f32[16,256]{1,0:T(8,128)S(1)} %copy-done.8), channel_id=1, source_target_pairs={{0,16},{4,20},{8,24},{12,28},{16,0},{20,4},{24,8},{28,12},{1,17},{... | collective-permute-start | bytes 49160 | tf_op jit(solution)/shard_map/ppermute | solution.py:663
  21.3 16.3 %collective-permute-start.12 = (f32[32,16,256]{2,1,0:T(8,128)S(1)}, f32[32,16,256]{2,1,0:T(8,128)}, u32[]{:S(2)}, u32[]{:S(2)}) collective-permute-start(f32[32,16,256]{2,1,0:T(8,128)S(1)} %get-tuple-element.40), channel_id=1, source_target_pairs={{0,2},{1,3},{2,0},{3,1},{4,6},{5,7},{6,4},{7,5},{8,10},{9,11},{10,... | collective-permute-start | bytes 1572872 | tf_op jit(solution)/shard_map/ppermute | solution.py:587
  30.6 1.2 %collective-permute-start.10 = (f32[9,1,128]{2,1,0:T(1,128)S(1)}, f32[9,1,128]{2,1,0:T(1,128)S(1)}, u32[]{:S(2)}, u32[]{:S(2)}) collective-permute-start(f32[9,1,128]{2,1,0:T(1,128)S(1)} %get-tuple-element.39), channel_id=1, source_target_pairs={{0,1},{1,0},{2,3},{3,2},{4,5},{5,4},{6,7},{7,6},{8,9},{9,8},{10,11... | collective-permute-start | bytes 13832 | tf_op jit(solution)/shard_map/ppermute | solution.py:587
  30.6 8.6 %collective-permute-start.14 = (f32[16,16,256]{2,1,0:T(8,128)S(1)}, f32[16,16,256]{2,1,0:T(8,128)S(1)}, u32[]{:S(2)}, u32[]{:S(2)}) collective-permute-start(f32[16,16,256]{2,1,0:T(8,128)S(1)} %get-tuple-element.43.refs_12_), channel_id=1, source_target_pairs={{0,1},{1,0},{2,3},{3,2},{4,5},{5,4},{6,7},{7,6},{8,9},{9,8},{10,11... | collective-permute-start | bytes 786440 | tf_op jit(solution)/shard_map/ppermute | solution.py:587
  31.2 8.1 %collective-permute-start.11 = (f32[16,16,256]{2,1,0:T(8,128)S(1)}, f32[16,16,256]{2,1,0:T(8,128)S(1)}, u32[]{:S(2)}, u32[]{:S(2)}) collective-permute-start(f32[16,16,256]{2,1,0:T(8,128)S(1)} %get-tuple-element.44.refs_8_), channel_id=1, source_target_pairs={{0,1},{1,0},{2,3},{3,2},{4,5},{5,4},{6,7},{7,6},{8,9},{9,8},{10,11... | collective-permute-start | bytes 786440 | tf_op jit(solution)/shard_map/ppermute | solution.py:587
  32.5 11.7 %all-to-all-start = ((f32[32,9,1,128]{3,2,1,0:T(1,128)}), f32[32,9,1,128]{3,2,1,0:T(1,128)S(1)}, u32[]{:S(2)}, u32[]{:S(2)}) async-start(f32[32,9,1,128]{3,2,1,0:T(1,128)} %broadcast_in_dim.3), calls=%async_computation | async-start | bytes 294912 | tf_op jit(solution)/shard_map/all_to_all | solution.py:711
  38.7 5.5 %collective-permute-start.15 = (f32[16,16,256]{2,1,0:T(8,128)S(1)}, f32[16,16,256]{2,1,0:T(8,128)S(1)}, u32[]{:S(2)}, u32[]{:S(2)}) collective-permute-start(f32[16,16,256]{2,1,0:T(8,128)S(1)} %get-tuple-element.41.refs_14_), channel_id=1, source_target_pairs={{0,1},{1,0},{2,3},{3,2},{4,5},{5,4},{6,7},{7,6},{8,9},{9,8},{10,11... | collective-permute-start | bytes 786440 | tf_op jit(solution)/shard_map/ppermute | solution.py:587
  38.8 5.4 %collective-permute-start.13 = (f32[16,16,256]{2,1,0:T(8,128)S(1)}, f32[16,16,256]{2,1,0:T(8,128)S(1)}, u32[]{:S(2)}, u32[]{:S(2)}) collective-permute-start(f32[16,16,256]{2,1,0:T(8,128)S(1)} %get-tuple-element.42.refs_10_), channel_id=1, source_target_pairs={{0,1},{1,0},{2,3},{3,2},{4,5},{5,4},{6,7},{7,6},{8,9},{9,8},{10,11... | collective-permute-start | bytes 786440 | tf_op jit(solution)/shard_map/ppermute | solution.py:587

commit v8 on v7

--- a/solution.py
+++ b/solution.py
@@ -555,9 +555,9 @@
 
 
 def analysis_kernel(count_mem, sums, *refs):
-    inner, outer, *winds = [refs[f * count_mem : (f + 1) * count_mem] for f in range(4)]
-    out, lower = refs[4 * count_mem :]
-    rows, members, cols = winds[0][0].shape
+    inner, outer = refs[:count_mem], refs[count_mem : 2 * count_mem]
+    *both, east, north, out, lower = refs[2 * count_mem :]
+    rows, members, cols = east.shape
     total = members * count_mem
 
     halves = [sums[0], sums[1]]
@@ -571,7 +571,8 @@
     for field in range(3):
         for r in range(rows):
             if field > 0:
-                pieces = [piece[r] for piece in winds[field - 1]]
+                last = east if field == 1 else north
+                pieces = [piece[(field - 1) * rows + r] for piece in both] + [last[r]]
             elif RIM <= r < rows - RIM:
                 pieces = [piece[r - RIM] for piece in inner]
             else:
@@ -682,13 +683,9 @@
         above,
         below,
     )
-    both = {0: parts[0], far: swap(parts[0], "mem", far)}
-    winds = [{k: x[i * rows : (i + 1) * rows] for k, x in both.items()} for i in range(2)]
-    for wind in winds:
-        wind[near] = swap(wind[0], "mem", near)
-        wind[far + near] = swap(wind[far], "mem", near)
+    both = [parts[0], swap(parts[0], "mem", near), swap(parts[0], "mem", far)]
+    winds = both + [swap(both[2][i * rows : (i + 1) * rows], "mem", near) for i in range(2)]
     inner, outer = ([x[k] for k in range(count_mem)] for x in (inner, outer))
-    winds = [wind[k] for wind in winds for k in range(count_mem)]
 
     half = (total // 4 + 2) // 2
     devices = count * count_mem
@@ -713,7 +710,7 @@
     return pl.pallas_call(
         functools.partial(analysis_kernel, count_mem),
         out_shape=jax.ShapeDtypeStruct(state.shape, F32),
-        in_specs=[VMEM] * (1 + 4 * count_mem),
+        in_specs=[VMEM] * (1 + 2 * count_mem + len(winds)),
         out_specs=VMEM,
         scratch_shapes=[pltpu.VMEM((total, 2 * total), F32)],
         compiler_params=PARAMS,

time: 48.6 us -> 58.7 us (1.21)
  waiting for transfers between devices: 7.66 us -> 18.7 us
  starting transfers between devices: 18.6 us -> 17.9 us
    ppermute x12 -> x11, waiting for transfers between devices: 2.38 us -> 11.2 us  [swap(): return lax.ppermute(x, axis, [(i, i ^ bit) for i in range(count)])]
    all_to_all x1, waiting for transfers between devices: 4.88 us -> 7.07 us  [local(): lax.all_to_all(sent, ('space', 'mem'), split_axis=0, concat_axis=0, tiled...]
    ppermute x12 -> x11, starting transfers between devices: 7.28 us -> 6.83 us  [swap(): return lax.ppermute(x, axis, [(i, i ^ bit) for i in range(count)])]
  transfers between devices with their start and end apart: 17 -> 16, of which waited for: 4 -> 5; matrix products, arithmetic and copies ran while one was open for 4% -> 3% of each run, Pallas kernels for 27% -> 22%
where the time goes in v8:
time: 58.7 us; the launch traced here: 58.5 us
  Pallas kernels  20 us (34%)
  waiting for transfers between devices  18.7 us (32%)
  starting transfers between devices  17.9 us (30%)
  local copies, waits for them, and re-layouts  1.61 us (3%)
    ppermute x11, waiting for transfers between devices, swap(): return lax.ppermute(x, axis, [(i, i ^ bit) for i in range(count)])  11.2 us
    all_to_all x1, waiting for transfers between devices, local(): lax.all_to_all(sent, ('space', 'mem'), split_axis=0, concat_axis=0, tiled...  7.07 us
    ppermute x11, starting transfers between devices, swap(): return lax.ppermute(x, axis, [(i, i ^ bit) for i in range(count)])  6.83 us
    ppermute x1, starting transfers between devices, local(): lax.ppermute(to_above, 'space', [((i + 1) % count, i) for i in range(coun...  5.74 us
    pallas_call x1, Pallas kernels, local(): pl.pallas_call(functools.partial(middle_kernel, inner_rows, outer_rows, f...  4.76 us
    pallas_call x1, Pallas kernels, local(): pl.pallas_call(functools.partial(analysis_kernel, count_mem), out_shape=j...  4.23 us
    pallas_call x1, Pallas kernels, local(): pl.pallas_call(functools.partial(near_inner_kernel, inner_rows, far), out...  3.83 us
    pallas_call x1, Pallas kernels, local(): pl.pallas_call(functools.partial(gram_kernel, outer_rows, scale, far, cou...  3.48 us
  transfers between devices with their start and end apart: 16, of which 5 were waited for; matrix products, arithmetic and copies ran while one was open for 3% of the time, Pallas kernels for 22%

profile of v8, /device:TPU:0, one launch (start us, length us, event | category | flops | bytes accessed | tf_op | source)
XLA Modules:
  0.0 58.5 jit_solution(3248634193307986191)
XLA Ops:
  0.0 0.0 copy-start.3
  0.0 0.0 copy-start
  0.0 2.3 %edges.1 = (f32[88,256]{1,0:T(8,128)}, f32[88,256]{1,0:T(8,128)}, f32[16,256]{1,0:T(8,128)}, f32[16,256]{1,0:T(8,128)}, f32[16,256]{1,0:T(8,128)}) custom-call(f32[16,3,16,256]{3,2,1,0:T(8,128)} %state.3, f32[16,256]{1,0:T(8,128)} %depth.2, f32[1,8,16,128]{3,2,1,0:T(8,128)} %values.1, f32[1,8,16,128]{3,2,1,0:T(8,128)} %precision.1), custom_call_target="tpu_custom_call" | custom-call | tf_op jit(solution)/shard_map/edges/pallas_call | solution.py:117
  2.3 0.0 copy-done.3
  2.3 0.0 copy-done
  2.3 0.0 copy-start.7
  2.3 0.0 copy-start.9
  2.3 0.0 copy-start.6
  2.3 0.6 inner.1.refs_0_
  2.9 0.5 collective-permute-start
  3.4 0.0 copy-done.7
  3.4 5.7 %collective-permute-start.2 = (f32[88,256]{1,0:T(8,128)S(1)}, f32[88,256]{1,0:T(8,128)S(1)}, u32[]{:S(2)}, u32[]{:S(2)}) collective-permute-start(f32[88,256]{1,0:T(8,128)S(1)} %copy-done.7), channel_id=1, source_target_pairs={{4,0},{8,4},{12,8},{16,12},{20,16},{24,20},{28,24},{0,28},{5,1},{9... | collective-permute-start | bytes 270344 | tf_op jit(solution)/shard_map/ppermute | solution.py:608
  9.2 0.0 copy-done.9
  9.2 0.4 collective-permute-start.3
  9.6 0.0 copy-done.6
  9.6 0.0 copy-start.1
  9.6 0.0 copy-start.2
  9.6 0.6 %collective-permute-start.1 = (f32[88,256]{1,0:T(8,128)S(1)}, f32[88,256]{1,0:T(8,128)S(1)}, u32[]{:S(2)}, u32[]{:S(2)}) collective-permute-start(f32[88,256]{1,0:T(8,128)S(1)} %copy-done.6), channel_id=1, source_target_pairs={{0,4},{4,8},{8,12},{12,16},{16,20},{20,24},{24,28},{28,0},{1,5},{5... | collective-permute-start | bytes 270344 | tf_op jit(solution)/shard_map/ppermute | solution.py:609
  10.3 0.0 collective-permute-done.refs_1_
  10.3 0.0 copy-start.5
  10.3 2.3 %collective-permute-start.6 = (f32[10,16,256]{2,1,0:T(8,128)S(1)}, f32[10,16,256]{2,1,0:T(8,128)S(1)}, u32[]{:S(2)}, u32[]{:S(2)}) collective-permute-start(f32[10,16,256]{2,1,0:T(8,128)S(1)} %hold.2.refs_0_), channel_id=1, source_target_pairs={{0,2},{1,3},{2,0},{3,1},{4,6},{5,7},{6,4},{7,5},{8,10},{9,11},{10,... | collective-permute-start | bytes 491528 | tf_op jit(solution)/shard_map/ppermute | solution.py:588
  12.6 0.0 copy-done.1
  12.6 0.0 copy-done.2
  12.6 0.0 copy-done.5
  12.6 3.8 %near_inner.1 = (f32[16,32,128]{2,1,0:T(8,128)S(1)}, s32[1,64]{1,0:T(1,128)S(1)}) custom-call(f32[10,16,256]{2,1,0:T(8,128)S(1)} %hold.2.refs_0_, f32[10,16,256]{2,1,0:T(8,128)S(1)} %collective-permute-done.refs_1_, s32[4,64,128]{2,1,0:T(8,128)S(1)} %copy-done.1, f32[4,64,128]{2,1,0:T(8,128)S(1)} %copy-done.2, s32[1,64]{1,0:T(1,128)S(1)} %bitcast.4), custom_call_target="tpu_custom_call" | custom-call | flops 2684354560 | bytes 327680 | tf_op jit(solution)/shard_map/near_inner/pallas_call | solution.py:644
  16.5 0.0 collective-permute-done.2.below.refs_9_
  16.5 0.4 collective-permute-done.1.above.refs_8_
  16.9 0.0 collective-permute-done.3.refs_0_
  16.9 0.9 %forecast.1 = (f32[7,16,256]{2,1,0:T(8,128)S(1)}, f32[32,16,256]{2,1,0:T(8,128)S(1)}) custom-call(f32[16,3,16,256]{3,2,1,0:T(8,128)S(1)} %copy-done, f32[16,256]{1,0:T(8,128)S(1)} %copy-done.3, f32[88,256]{1,0:T(8,128)S(1)} %collective-permute-done.1.above.refs_8_, f32[88,256]{1,0:T(8,128)S(1)} %collective-permute-done.2.below.refs_9_, ...), custom_call_target="tpu_custom_call" | custom-call | flops 2000000000 | bytes 786432 | tf_op jit(solution)/shard_map/forecast/pallas_call | solution.py:249
  17.8 0.0 collective-permute-done.6.refs_0_
  17.8 0.0 copy-start.8
  17.8 0.0 copy-start.4
  17.8 0.1 collective-permute-start.7
  17.9 1.2 %collective-permute-start.12 = (f32[32,16,256]{2,1,0:T(8,128)S(1)}, f32[32,16,256]{2,1,0:T(8,128)S(1)}, u32[]{:S(2)}, u32[]{:S(2)}) collective-permute-start(f32[32,16,256]{2,1,0:T(8,128)S(1)} %get-tuple-element.40.refs_8_), channel_id=1, source_target_pairs={{0,2},{1,3},{2,0},{3,1},{4,6},{5,7},{6,4},{7,5},{8,10},{9,11},{10,... | collective-permute-start | bytes 1572872 | tf_op jit(solution)/shard_map/ppermute | solution.py:588
  19.1 0.2 collective-permute-start.8
  19.3 0.8 %collective-permute-start.5 = (f32[7,16,256]{2,1,0:T(8,128)S(1)}, f32[7,16,256]{2,1,0:T(8,128)S(1)}, u32[]{:S(2)}, u32[]{:S(2)}) collective-permute-start(f32[7,16,256]{2,1,0:T(8,128)S(1)} %get-tuple-element.31.refs_1_.refs_2_.refs_4_), channel_id=1, source_target_pairs={{0,3},{1,2},{2,1},{3,0},{4,7},{5,6},{6,5},{7,4},{8,11},{9,10},{10,... | collective-permute-start | bytes 344072 | tf_op jit(solution)/shard_map/ppermute | solution.py:588
  20.1 1.2 %collective-permute-start.4 = (f32[7,16,256]{2,1,0:T(8,128)S(1)}, f32[7,16,256]{2,1,0:T(8,128)S(1)}, u32[]{:S(2)}, u32[]{:S(2)}) collective-permute-start(f32[7,16,256]{2,1,0:T(8,128)S(1)} %get-tuple-element.31.refs_1_.refs_2_.refs_4_), channel_id=1, source_target_pairs={{0,2},{1,3},{2,0},{3,1},{4,6},{5,7},{6,4},{7,5},{8,10},{9,11},{10,... | collective-permute-start | bytes 344072 | tf_op jit(solution)/shard_map/ppermute | solution.py:588
  21.3 0.0 collective-permute-done.8.refs_3_.refs_5_
  21.3 0.0 collective-permute-start.11
  21.3 0.0 collective-permute-done.7.refs_1_.refs_3_
  21.3 0.0 copy-done.8
  21.3 1.0 %collective-permute-start.9 = (f32[16,256]{1,0:T(8,128)S(1)}, f32[16,256]{1,0:T(8,128)S(1)}, u32[]{:S(2)}, u32[]{:S(2)}) collective-permute-start(f32[16,256]{1,0:T(8,128)S(1)} %copy-done.8), channel_id=1, source_target_pairs={{0,16},{4,20},{8,24},{12,28},{16,0},{20,4},{24,8},{28,12},{1,17},{... | collective-permute-start | bytes 49160 | tf_op jit(solution)/shard_map/ppermute | solution.py:664
  22.3 0.0 copy-done.4
  22.3 4.8 %middle.1 = (f32[16,32,128]{2,1,0:T(8,128)S(1)}, f32[16,32,128]{2,1,0:T(8,128)S(1)}, f32[5,16,256]{2,1,0:T(8,128)S(1)}) custom-call(f32[10,16,256]{2,1,0:T(8,128)S(1)} %hold.3.refs_0_.refs_2_, f32[10,16,256]{2,1,0:T(8,128)S(1)} %collective-permute-done.7.refs_1_.refs_3_, f32[7,16,256]{2,1,0:T(8,128)S(1)} %get-tuple-element.31.refs_1_.refs_2_.refs_4_, ...), custom_call_target="tpu_custom_call" | custom-call | flops 4294967296 | bytes 524288 | tf_op jit(solution)/shard_map/middle/pallas_call | solution.py:668
  27.1 0.0 collective-permute-done.9.refs_7_
  27.1 7.1 %collective-permute-done.5.refs_1_.refs_7_ = f32[7,16,256]{2,1,0:T(8,128)S(1)} collective-permute-done((f32[7,16,256]{2,1,0:T(8,128)S(1)}, f32[7,16,256]{2,1,0:T(8,128)S(1)}, u32[]{:S(2)}, u32[]{:S(2)}) %collective-permute-start.5) | collective-permute-done | bytes 114720 | tf_op jit(solution)/shard_map/ppermute | solution.py:588
  34.2 2.9 %collective-permute-done.4.refs_0_.refs_6_ = f32[7,16,256]{2,1,0:T(8,128)S(1)} collective-permute-done((f32[7,16,256]{2,1,0:T(8,128)S(1)}, f32[7,16,256]{2,1,0:T(8,128)S(1)}, u32[]{:S(2)}, u32[]{:S(2)}) %collective-permute-start.4) | collective-permute-done | bytes 114720 | tf_op jit(solution)/shard_map/ppermute | solution.py:588
  37.2 3.5 %gram.1 = (f32[9,1,128]{2,1,0:T(1,128)S(1)}, f32[9,1,128]{2,1,0:T(1,128)S(1)}) custom-call(s32[1,64]{1,0:T(1,128)S(1)} %get-tuple-element.25.owners, f32[7,16,256]{2,1,0:T(8,128)S(1)} %collective-permute-done.4.refs_0_.refs_6_, f32[7,16,256]{2,1,0:T(8,128)S(1)} %collective-permute-done.5.refs_1_.refs_7_, s32[4,64,128]{2,1,0:T(8,128)S(1)} %copy-done.1, ...), custom_call_target="tpu_custom_call" | custom-call | flops 1000 | bytes 1000 | tf_op jit(solution)/shard_map/gram/pallas_call | solution.py:693
  40.6 0.0 collective-permute-start.10
  40.7 1.2 %collective-permute-done.10 = f32[9,1,128]{2,1,0:T(1,128)S(1)} collective-permute-done((f32[9,1,128]{2,1,0:T(1,128)S(1)}, f32[9,1,128]{2,1,0:T(1,128)S(1)}, u32[]{:S(2)}, u32[]{:S(2)}) %collective-permute-start.10) | collective-permute-done | bytes 4640 | tf_op jit(solution)/shard_map/ppermute | solution.py:588
  41.8 0.7 %broadcast_in_dim.3 = f32[32,9,1,128]{3,2,1,0:T(1,128)} broadcast(f32[9,128]{1,0:T(8,128)S(1)} %bitcast.5), dimensions={1,3} | broadcast | bytes 152064 | tf_op jit(solution)/shard_map/broadcast_in_dim | solution.py:707
  42.6 3.2 %all-to-all-start = ((f32[32,9,1,128]{3,2,1,0:T(1,128)}), f32[32,9,1,128]{3,2,1,0:T(1,128)S(1)}, u32[]{:S(2)}, u32[]{:S(2)}) async-start(f32[32,9,1,128]{3,2,1,0:T(1,128)} %broadcast_in_dim.3), calls=%async_computation | async-start | bytes 294912 | tf_op jit(solution)/shard_map/all_to_all | solution.py:708
  45.8 0.0 collective-permute-done.12.refs_10_
  45.8 0.8 %fusion = (f32[16,16,256]{2,1,0:T(8,128)}, f32[16,16,256]{2,1,0:T(8,128)}) fusion(f32[32,16,256]{2,1,0:T(8,128)S(1)} %collective-permute-done.12.refs_10_), kind=kLoop, calls=%fused_computation.1 | loop fusion | bytes 1048576 | tf_op jit(solution)/shard_map/slice | solution.py:687
  46.7 0.3 collective-permute-start.14
  46.9 0.3 collective-permute-start.13
  47.2 0.0 collective-permute-done.11.refs_9_
  47.2 7.1 %all-to-all-done.sums = f32[32,9,1,128]{3,2,1,0:T(1,128)S(1)} async-done(((f32[32,9,1,128]{3,2,1,0:T(1,128)}), f32[32,9,1,128]{3,2,1,0:T(1,128)S(1)}, u32[]{:S(2)}, u32[]{:S(2)}) %all-to-all-start) | async-done | bytes 147488 | tf_op jit(solution)/shard_map/all_to_all | solution.py:708
  54.2 0.0 collective-permute-done.14.refs_12_
  54.2 0.0 collective-permute-done.13.refs_11_
  54.3 4.2 %analysis.1 = f32[16,3,16,256]{3,2,1,0:T(8,128)} custom-call(f32[32,9,1,128]{3,2,1,0:T(1,128)S(1)} %all-to-all-done.sums, f32[10,16,256]{2,1,0:T(8,128)S(1)} %hold.2.refs_0_, f32[10,16,256]{2,1,0:T(8,128)S(1)} %collective-permute-done.refs_1_, f32[10,16,256]{2,1,0:T(8,128)S(1)} %hold.3.refs_0_.refs_2_, ...), custom_call_target="tpu_custom_call" | custom-call | tf_op jit(solution)/shard_map/analysis/pallas_call | solution.py:710
  (4 shorter events, 0.0 us)
Async XLA Ops:
  0.0 2.3 %copy-start.3 = (f32[16,256]{1,0:T(8,128)S(1)}, f32[16,256]{1,0:T(8,128)}, u32[]{:S(2)}) copy-start(f32[16,256]{1,0:T(8,128)} %depth.2) | copy-start | bytes 49156
  0.0 2.3 %copy-start = (f32[16,3,16,256]{3,2,1,0:T(8,128)S(1)}, f32[16,3,16,256]{3,2,1,0:T(8,128)}, u32[]{:S(2)}) copy-start(f32[16,3,16,256]{3,2,1,0:T(8,128)} %state.3) | copy-start | bytes 2359300
  2.3 1.1 %copy-start.7 = (f32[88,256]{1,0:T(8,128)S(1)}, f32[88,256]{1,0:T(8,128)}, u32[]{:S(2)}) copy-start(f32[88,256]{1,0:T(8,128)} %get-tuple-element.23) | copy-start | bytes 270340
  2.3 6.9 %copy-start.9 = (f32[16,256]{1,0:T(8,128)S(1)}, f32[16,256]{1,0:T(8,128)}, u32[]{:S(2)}) copy-start(f32[16,256]{1,0:T(8,128)} %get-tuple-element.30) | copy-start | bytes 49156
  2.3 7.3 %copy-start.6 = (f32[88,256]{1,0:T(8,128)S(1)}, f32[88,256]{1,0:T(8,128)}, u32[]{:S(2)}) copy-start(f32[88,256]{1,0:T(8,128)} %get-tuple-element.26) | copy-start | bytes 270340
  2.9 7.4 %collective-permute-start = (f32[10,16,256]{2,1,0:T(8,128)S(1)}, f32[10,16,256]{2,1,0:T(8,128)S(1)}, u32[]{:S(2)}, u32[]{:S(2)}) collective-permute-start(f32[10,16,256]{2,1,0:T(8,128)S(1)} %inner.1.refs_0_), channel_id=1, source_target_pairs={{0,1},{1,0},{2,3},{3,2},{4,5},{5,4},{6,7},{7,6},{8,9},{9,8},{10,11... | collective-permute-start | bytes 491528 | tf_op jit(solution)/shard_map/ppermute | solution.py:588
  3.4 13.0 %collective-permute-start.2 = (f32[88,256]{1,0:T(8,128)S(1)}, f32[88,256]{1,0:T(8,128)S(1)}, u32[]{:S(2)}, u32[]{:S(2)}) collective-permute-start(f32[88,256]{1,0:T(8,128)S(1)} %copy-done.7), channel_id=1, source_target_pairs={{4,0},{8,4},{12,8},{16,12},{20,16},{24,20},{28,24},{0,28},{5,1},{9... | collective-permute-start | bytes 270344 | tf_op jit(solution)/shard_map/ppermute | solution.py:608
  9.2 7.7 %collective-permute-start.3 = (f32[16,256]{1,0:T(8,128)S(1)}, f32[16,256]{1,0:T(8,128)S(1)}, u32[]{:S(2)}, u32[]{:S(2)}) collective-permute-start(f32[16,256]{1,0:T(8,128)S(1)} %copy-done.9), channel_id=1, source_target_pairs={{0,24},{1,9},{2,22},{3,15},{4,28},{5,13},{6,26},{7,19},{8,0},{9,17... | collective-permute-start | bytes 49160 | tf_op jit(solution)/shard_map/ppermute | solution.py:611
  9.6 3.0 %copy-start.1 = (s32[4,64,128]{2,1,0:T(8,128)S(1)}, s32[4,64,128]{2,1,0:T(8,128)}, u32[]{:S(2)}) copy-start(s32[4,64,128]{2,1,0:T(8,128)} %refs_2_.3) | copy-start | bytes 393220
  9.6 3.0 %copy-start.2 = (f32[4,64,128]{2,1,0:T(8,128)S(1)}, f32[4,64,128]{2,1,0:T(8,128)}, u32[]{:S(2)}) copy-start(f32[4,64,128]{2,1,0:T(8,128)} %refs_3_.3) | copy-start | bytes 393220
  9.6 7.2 %collective-permute-start.1 = (f32[88,256]{1,0:T(8,128)S(1)}, f32[88,256]{1,0:T(8,128)S(1)}, u32[]{:S(2)}, u32[]{:S(2)}) collective-permute-start(f32[88,256]{1,0:T(8,128)S(1)} %copy-done.6), channel_id=1, source_target_pairs={{0,4},{4,8},{8,12},{12,16},{16,20},{20,24},{24,28},{28,0},{1,5},{5... | collective-permute-start | bytes 270344 | tf_op jit(solution)/shard_map/ppermute | solution.py:609
  10.3 2.3 %copy-start.5 = (s32[64,1]{0,1:T(1,128)S(1)}, s32[64,1]{0,1:T(1,128)}, u32[]{:S(2)}) copy-start(s32[64,1]{0,1:T(1,128)} %param.11) | copy-start | bytes 772
  10.3 7.5 %collective-permute-start.6 = (f32[10,16,256]{2,1,0:T(8,128)S(1)}, f32[10,16,256]{2,1,0:T(8,128)S(1)}, u32[]{:S(2)}, u32[]{:S(2)}) collective-permute-start(f32[10,16,256]{2,1,0:T(8,128)S(1)} %hold.2.refs_0_), channel_id=1, source_target_pairs={{0,2},{1,3},{2,0},{3,1},{4,6},{5,7},{6,4},{7,5},{8,10},{9,11},{10,... | collective-permute-start | bytes 491528 | tf_op jit(solution)/shard_map/ppermute | solution.py:588
  17.8 3.5 %copy-start.8 = (f32[16,256]{1,0:T(8,128)S(1)}, f32[16,256]{1,0:T(8,128)}, u32[]{:S(2)}) copy-start(f32[16,256]{1,0:T(8,128)} %get-tuple-element.37) | copy-start | bytes 49156
  17.8 4.5 %copy-start.4 = (f32[16,256]{1,0:T(8,128)S(1)}, f32[16,256]{1,0:T(8,128)}, u32[]{:S(2)}) copy-start(f32[16,256]{1,0:T(8,128)} %get-tuple-element.32.refs_7_) | copy-start | bytes 49156
  17.8 3.5 %collective-permute-start.7 = (f32[10,16,256]{2,1,0:T(8,128)S(1)}, f32[10,16,256]{2,1,0:T(8,128)S(1)}, u32[]{:S(2)}, u32[]{:S(2)}) collective-permute-start(f32[10,16,256]{2,1,0:T(8,128)S(1)} %hold.3.refs_0_.refs_2_), channel_id=1, source_target_pairs={{0,1},{1,0},{2,3},{3,2},{4,5},{5,4},{6,7},{7,6},{8,9},{9,8},{10,11... | collective-permute-start | bytes 491528 | tf_op jit(solution)/shard_map/ppermute | solution.py:588
  17.9 27.9 %collective-permute-start.12 = (f32[32,16,256]{2,1,0:T(8,128)S(1)}, f32[32,16,256]{2,1,0:T(8,128)S(1)}, u32[]{:S(2)}, u32[]{:S(2)}) collective-permute-start(f32[32,16,256]{2,1,0:T(8,128)S(1)} %get-tuple-element.40.refs_8_), channel_id=1, source_target_pairs={{0,2},{1,3},{2,0},{3,1},{4,6},{5,7},{6,4},{7,5},{8,10},{9,11},{10,... | collective-permute-start | bytes 1572872 | tf_op jit(solution)/shard_map/ppermute | solution.py:588
  19.1 2.1 %collective-permute-start.8 = (f32[7,16,256]{2,1,0:T(8,128)S(1)}, f32[7,16,256]{2,1,0:T(8,128)S(1)}, u32[]{:S(2)}, u32[]{:S(2)}) collective-permute-start(f32[7,16,256]{2,1,0:T(8,128)S(1)} %get-tuple-element.31.refs_1_.refs_2_.refs_4_), channel_id=1, source_target_pairs={{0,1},{1,0},{2,3},{3,2},{4,5},{5,4},{6,7},{7,6},{8,9},{9,8},{10,11... | collective-permute-start | bytes 344072 | tf_op jit(solution)/shard_map/ppermute | solution.py:588
  19.3 14.9 %collective-permute-start.5 = (f32[7,16,256]{2,1,0:T(8,128)S(1)}, f32[7,16,256]{2,1,0:T(8,128)S(1)}, u32[]{:S(2)}, u32[]{:S(2)}) collective-permute-start(f32[7,16,256]{2,1,0:T(8,128)S(1)} %get-tuple-element.31.refs_1_.refs_2_.refs_4_), channel_id=1, source_target_pairs={{0,3},{1,2},{2,1},{3,0},{4,7},{5,6},{6,5},{7,4},{8,11},{9,10},{10,... | collective-permute-start | bytes 344072 | tf_op jit(solution)/shard_map/ppermute | solution.py:588
  20.1 17.0 %collective-permute-start.4 = (f32[7,16,256]{2,1,0:T(8,128)S(1)}, f32[7,16,256]{2,1,0:T(8,128)S(1)}, u32[]{:S(2)}, u32[]{:S(2)}) collective-permute-start(f32[7,16,256]{2,1,0:T(8,128)S(1)} %get-tuple-element.31.refs_1_.refs_2_.refs_4_), channel_id=1, source_target_pairs={{0,2},{1,3},{2,0},{3,1},{4,6},{5,7},{6,4},{7,5},{8,10},{9,11},{10,... | collective-permute-start | bytes 344072 | tf_op jit(solution)/shard_map/ppermute | solution.py:588
  21.3 25.9 %collective-permute-start.11 = (f32[32,16,256]{2,1,0:T(8,128)S(1)}, f32[32,16,256]{2,1,0:T(8,128)S(1)}, u32[]{:S(2)}, u32[]{:S(2)}) collective-permute-start(f32[32,16,256]{2,1,0:T(8,128)S(1)} %get-tuple-element.40.refs_8_), channel_id=1, source_target_pairs={{0,1},{1,0},{2,3},{3,2},{4,5},{5,4},{6,7},{7,6},{8,9},{9,8},{10,11... | collective-permute-start | bytes 1572872 | tf_op jit(solution)/shard_map/ppermute | solution.py:588
  21.3 5.8 %collective-permute-start.9 = (f32[16,256]{1,0:T(8,128)S(1)}, f32[16,256]{1,0:T(8,128)S(1)}, u32[]{:S(2)}, u32[]{:S(2)}) collective-permute-start(f32[16,256]{1,0:T(8,128)S(1)} %copy-done.8), channel_id=1, source_target_pairs={{0,16},{4,20},{8,24},{12,28},{16,0},{20,4},{24,8},{28,12},{1,17},{... | collective-permute-start | bytes 49160 | tf_op jit(solution)/shard_map/ppermute | solution.py:664
  40.6 1.2 %collective-permute-start.10 = (f32[9,1,128]{2,1,0:T(1,128)S(1)}, f32[9,1,128]{2,1,0:T(1,128)S(1)}, u32[]{:S(2)}, u32[]{:S(2)}) collective-permute-start(f32[9,1,128]{2,1,0:T(1,128)S(1)} %get-tuple-element.39), channel_id=1, source_target_pairs={{0,1},{1,0},{2,3},{3,2},{4,5},{5,4},{6,7},{7,6},{8,9},{9,8},{10,11... | collective-permute-start | bytes 13832 | tf_op jit(solution)/shard_map/ppermute | solution.py:588
  42.6 11.7 %all-to-all-start = ((f32[32,9,1,128]{3,2,1,0:T(1,128)}), f32[32,9,1,128]{3,2,1,0:T(1,128)S(1)}, u32[]{:S(2)}, u32[]{:S(2)}) async-start(f32[32,9,1,128]{3,2,1,0:T(1,128)} %broadcast_in_dim.3), calls=%async_computation | async-start | bytes 294912 | tf_op jit(solution)/shard_map/all_to_all | solution.py:708
  46.7 7.6 %collective-permute-start.14 = (f32[16,16,256]{2,1,0:T(8,128)}, f32[16,16,256]{2,1,0:T(8,128)S(1)}, u32[]{:S(2)}, u32[]{:S(2)}) collective-permute-start(f32[16,16,256]{2,1,0:T(8,128)} %get-tuple-element.41), channel_id=1, source_target_pairs={{0,1},{1,0},{2,3},{3,2},{4,5},{5,4},{6,7},{7,6},{8,9},{9,8},{10,11... | collective-permute-start | bytes 786440 | tf_op jit(solution)/shard_map/ppermute | solution.py:588
  46.9 7.3 %collective-permute-start.13 = (f32[16,16,256]{2,1,0:T(8,128)}, f32[16,16,256]{2,1,0:T(8,128)S(1)}, u32[]{:S(2)}, u32[]{:S(2)}) collective-permute-start(f32[16,16,256]{2,1,0:T(8,128)} %get-tuple-element.42), channel_id=1, source_target_pairs={{0,1},{1,0},{2,3},{3,2},{4,5},{5,4},{6,7},{7,6},{8,9},{9,8},{10,11... | collective-permute-start | bytes 786440 | tf_op jit(solution)/shard_map/ppermute | solution.py:588

commit v9 on v7

--- a/solution.py
+++ b/solution.py
@@ -76,7 +76,7 @@
         copies.append(pltpu.make_async_copy(precision.at[0, peer], weight.at[j], sems.at[4 + 2 * j]))
     for copy in copies:
         copy.start()
-    for copy in copies:
+    for copy in copies[:3]:
         copy.wait()
     for out, sign, at in ((above, 1.0, range(4)), (below, -1.0, range(rows - 1, rows - 5, -1))):
         deep = [jnp.broadcast_to(depth[t : t + 1], (members, cols)) for t in at]
@@ -100,6 +100,8 @@
         out[4 * members : 4 * members + 8] = jnp.concatenate(
             [deep[0][0:1], deep[1][0:1], jnp.zeros((6, cols), F32)], axis=0
         )
+    for copy in copies[3:]:
+        copy.wait()
     rim = 4 * members + 8
     slots = seen.shape[1]
     places = [own, above.at[rim : rim + slots], below.at[rim : rim + slots]] + list(held)

time: 48.6 us -> 48.6 us (level)
  no operation moved by 1% of the time
where the time goes in v9:
time: 48.6 us; the launch traced here: 48.4 us
  Pallas kernels  20.1 us (41%)
  starting transfers between devices  18.6 us (38%)
  waiting for transfers between devices  7.66 us (16%)
  local copies, waits for them, and re-layouts  1.89 us (4%)
    ppermute x12, starting transfers between devices, swap(): return lax.ppermute(x, axis, [(i, i ^ bit) for i in range(count)])  7.28 us
    ppermute x1, starting transfers between devices, local(): lax.ppermute(to_above, 'space', [((i + 1) % count, i) for i in range(coun...  5.74 us
    all_to_all x1, waiting for transfers between devices, local(): lax.all_to_all(sent, ('space', 'mem'), split_axis=0, concat_axis=0, tiled...  4.88 us
    pallas_call x1, Pallas kernels, local(): pl.pallas_call(functools.partial(middle_kernel, inner_rows, outer_rows, f...  4.77 us
    pallas_call x1, Pallas kernels, local(): pl.pallas_call(functools.partial(analysis_kernel, count_mem), out_shape=j...  4.22 us
    pallas_call x1, Pallas kernels, local(): pl.pallas_call(functools.partial(near_inner_kernel, inner_rows, far), out...  3.83 us
    pallas_call x1, Pallas kernels, local(): pl.pallas_call(functools.partial(gram_kernel, outer_rows, scale, far, cou...  3.49 us
    all_to_all x1, starting transfers between devices, local(): lax.all_to_all(sent, ('space', 'mem'), split_axis=0, concat_axis=0, tiled...  3.24 us
  transfers between devices with their start and end apart: 17, of which 4 were waited for; matrix products, arithmetic and copies ran while one was open for 4% of the time, Pallas kernels for 27%

profile of v9, /device:TPU:0, one launch (start us, length us, event | category | flops | bytes accessed | tf_op | source)
XLA Modules:
  0.0 48.4 jit_solution(12221308925711520345)
XLA Ops:
  0.0 0.0 copy-start.3
  0.0 0.0 copy-start
  0.0 2.3 %edges.1 = (f32[88,256]{1,0:T(8,128)}, f32[88,256]{1,0:T(8,128)}, f32[16,256]{1,0:T(8,128)}, f32[16,256]{1,0:T(8,128)}, f32[16,256]{1,0:T(8,128)}) custom-call(f32[16,3,16,256]{3,2,1,0:T(8,128)} %state.3, f32[16,256]{1,0:T(8,128)} %depth.2, f32[1,8,16,128]{3,2,1,0:T(8,128)} %values.1, f32[1,8,16,128]{3,2,1,0:T(8,128)} %precision.1), custom_call_target="tpu_custom_call" | custom-call | tf_op jit(solution)/shard_map/edges/pallas_call | solution.py:119
  2.3 0.0 copy-done.3
  2.3 0.0 copy-done
  2.3 0.0 copy-start.7
  2.3 0.0 copy-start.9
  2.3 0.0 copy-start.6
  2.3 0.6 %inner.1.refs_0_ = f32[10,16,256]{2,1,0:T(8,128)S(1)} custom-call(f32[16,3,16,256]{3,2,1,0:T(8,128)S(1)} %copy-done, f32[16,256]{1,0:T(8,128)S(1)} %copy-done.3), custom_call_target="tpu_custom_call" | custom-call | flops 2000000000 | bytes 786432 | tf_op jit(solution)/shard_map/inner/pallas_call | solution.py:162
  2.9 0.5 %collective-permute-start = (f32[10,16,256]{2,1,0:T(8,128)S(1)}, f32[10,16,256]{2,1,0:T(8,128)S(1)}, u32[]{:S(2)}, u32[]{:S(2)}) collective-permute-start(f32[10,16,256]{2,1,0:T(8,128)S(1)} %inner.1.refs_0_), channel_id=1, source_target_pairs={{0,1},{1,0},{2,3},{3,2},{4,5},{5,4},{6,7},{7,6},{8,9},{9,8},{10,11... | collective-permute-start | bytes 491528 | tf_op jit(solution)/shard_map/ppermute | solution.py:589
  3.4 0.0 copy-done.7
  3.4 5.7 %collective-permute-start.2 = (f32[88,256]{1,0:T(8,128)S(1)}, f32[88,256]{1,0:T(8,128)S(1)}, u32[]{:S(2)}, u32[]{:S(2)}) collective-permute-start(f32[88,256]{1,0:T(8,128)S(1)} %copy-done.7), channel_id=1, source_target_pairs={{4,0},{8,4},{12,8},{16,12},{20,16},{24,20},{28,24},{0,28},{5,1},{9... | collective-permute-start | bytes 270344 | tf_op jit(solution)/shard_map/ppermute | solution.py:609
  9.2 0.0 copy-done.9
  9.2 0.4 collective-permute-start.3
  9.6 0.0 copy-done.6
  9.6 0.0 copy-start.1
  9.6 0.0 copy-start.2
  9.6 0.6 %collective-permute-start.1 = (f32[88,256]{1,0:T(8,128)S(1)}, f32[88,256]{1,0:T(8,128)S(1)}, u32[]{:S(2)}, u32[]{:S(2)}) collective-permute-start(f32[88,256]{1,0:T(8,128)S(1)} %copy-done.6), channel_id=1, source_target_pairs={{0,4},{4,8},{8,12},{12,16},{16,20},{20,24},{24,28},{28,0},{1,5},{5... | collective-permute-start | bytes 270344 | tf_op jit(solution)/shard_map/ppermute | solution.py:610
  10.3 0.0 collective-permute-done.refs_1_
  10.3 0.0 copy-start.5
  10.3 2.3 %collective-permute-start.6 = (f32[10,16,256]{2,1,0:T(8,128)S(1)}, f32[10,16,256]{2,1,0:T(8,128)S(1)}, u32[]{:S(2)}, u32[]{:S(2)}) collective-permute-start(f32[10,16,256]{2,1,0:T(8,128)S(1)} %hold.2.refs_0_), channel_id=1, source_target_pairs={{0,2},{1,3},{2,0},{3,1},{4,6},{5,7},{6,4},{7,5},{8,10},{9,11},{10,... | collective-permute-start | bytes 491528 | tf_op jit(solution)/shard_map/ppermute | solution.py:589
  12.6 0.0 copy-done.1
  12.6 0.0 copy-done.2
  12.6 0.0 copy-done.5
  12.6 3.8 %near_inner.1 = (f32[16,32,128]{2,1,0:T(8,128)S(1)}, s32[1,64]{1,0:T(1,128)S(1)}) custom-call(f32[10,16,256]{2,1,0:T(8,128)S(1)} %hold.2.refs_0_, f32[10,16,256]{2,1,0:T(8,128)S(1)} %collective-permute-done.refs_1_, s32[4,64,128]{2,1,0:T(8,128)S(1)} %copy-done.1, f32[4,64,128]{2,1,0:T(8,128)S(1)} %copy-done.2, s32[1,64]{1,0:T(1,128)S(1)} %bitcast.4), custom_call_target="tpu_custom_call" | custom-call | flops 2684354560 | bytes 327680 | tf_op jit(solution)/shard_map/near_inner/pallas_call | solution.py:645
  16.5 0.0 collective-permute-done.2.below.refs_9_
  16.5 0.4 collective-permute-done.1.above.refs_8_
  16.9 0.0 collective-permute-done.3.refs_0_
  16.9 0.9 %forecast.1 = (f32[7,16,256]{2,1,0:T(8,128)S(1)}, f32[32,16,256]{2,1,0:T(8,128)S(1)}) custom-call(f32[16,3,16,256]{3,2,1,0:T(8,128)S(1)} %copy-done, f32[16,256]{1,0:T(8,128)S(1)} %copy-done.3, f32[88,256]{1,0:T(8,128)S(1)} %collective-permute-done.1.above.refs_8_, f32[88,256]{1,0:T(8,128)S(1)} %collective-permute-done.2.below.refs_9_, ...), custom_call_target="tpu_custom_call" | custom-call | flops 2000000000 | bytes 786432 | tf_op jit(solution)/shard_map/forecast/pallas_call | solution.py:251
  17.8 0.0 collective-permute-done.6.refs_0_
  17.8 0.0 copy-start.8
  17.8 0.0 copy-start.4
  17.8 0.1 collective-permute-start.7
  17.9 0.5 %collective-permute-start.8 = (f32[7,16,256]{2,1,0:T(8,128)S(1)}, f32[7,16,256]{2,1,0:T(8,128)S(1)}, u32[]{:S(2)}, u32[]{:S(2)}) collective-permute-start(f32[7,16,256]{2,1,0:T(8,128)S(1)} %get-tuple-element.31.refs_1_.refs_2_.refs_4_), channel_id=1, source_target_pairs={{0,1},{1,0},{2,3},{3,2},{4,5},{5,4},{6,7},{7,6},{8,9},{9,8},{10,11... | collective-permute-start | bytes 344072 | tf_op jit(solution)/shard_map/ppermute | solution.py:589
  18.4 0.8 %collective-permute-start.5 = (f32[7,16,256]{2,1,0:T(8,128)S(1)}, f32[7,16,256]{2,1,0:T(8,128)S(1)}, u32[]{:S(2)}, u32[]{:S(2)}) collective-permute-start(f32[7,16,256]{2,1,0:T(8,128)S(1)} %get-tuple-element.31.refs_1_.refs_2_.refs_4_), channel_id=1, source_target_pairs={{0,3},{1,2},{2,1},{3,0},{4,7},{5,6},{6,5},{7,4},{8,11},{9,10},{10,... | collective-permute-start | bytes 344072 | tf_op jit(solution)/shard_map/ppermute | solution.py:589
  19.3 0.9 %collective-permute-start.4 = (f32[7,16,256]{2,1,0:T(8,128)S(1)}, f32[7,16,256]{2,1,0:T(8,128)S(1)}, u32[]{:S(2)}, u32[]{:S(2)}) collective-permute-start(f32[7,16,256]{2,1,0:T(8,128)S(1)} %get-tuple-element.31.refs_1_.refs_2_.refs_4_), channel_id=1, source_target_pairs={{0,2},{1,3},{2,0},{3,1},{4,6},{5,7},{6,4},{7,5},{8,10},{9,11},{10,... | collective-permute-start | bytes 344072 | tf_op jit(solution)/shard_map/ppermute | solution.py:589
  20.1 0.0 copy-done.8
  20.1 1.2 %collective-permute-start.9 = (f32[16,256]{1,0:T(8,128)S(1)}, f32[16,256]{1,0:T(8,128)S(1)}, u32[]{:S(2)}, u32[]{:S(2)}) collective-permute-start(f32[16,256]{1,0:T(8,128)S(1)} %copy-done.8), channel_id=1, source_target_pairs={{0,16},{4,20},{8,24},{12,28},{16,0},{20,4},{24,8},{28,12},{1,17},{... | collective-permute-start | bytes 49160 | tf_op jit(solution)/shard_map/ppermute | solution.py:665
  21.3 0.0 collective-permute-done.8.refs_3_.refs_5_
  21.3 0.9 %collective-permute-start.12 = (f32[32,16,256]{2,1,0:T(8,128)S(1)}, f32[32,16,256]{2,1,0:T(8,128)}, u32[]{:S(2)}, u32[]{:S(2)}) collective-permute-start(f32[32,16,256]{2,1,0:T(8,128)S(1)} %get-tuple-element.40), channel_id=1, source_target_pairs={{0,2},{1,3},{2,0},{3,1},{4,6},{5,7},{6,4},{7,5},{8,10},{9,11},{10,... | collective-permute-start | bytes 1572872 | tf_op jit(solution)/shard_map/ppermute | solution.py:589
  22.3 0.0 collective-permute-done.7.refs_1_.refs_3_
  22.3 0.0 copy-done.4
  22.3 4.8 %middle.1 = (f32[16,32,128]{2,1,0:T(8,128)S(1)}, f32[16,32,128]{2,1,0:T(8,128)S(1)}, f32[5,16,256]{2,1,0:T(8,128)S(1)}) custom-call(f32[10,16,256]{2,1,0:T(8,128)S(1)} %hold.3.refs_0_.refs_2_, f32[10,16,256]{2,1,0:T(8,128)S(1)} %collective-permute-done.7.refs_1_.refs_3_, f32[7,16,256]{2,1,0:T(8,128)S(1)} %get-tuple-element.31.refs_1_.refs_2_.refs_4_, ...), custom_call_target="tpu_custom_call" | custom-call | flops 4294967296 | bytes 524288 | tf_op jit(solution)/shard_map/middle/pallas_call | solution.py:669
  27.1 0.0 collective-permute-done.9.refs_7_
  27.1 0.0 collective-permute-done.5.refs_1_.refs_7_
  27.1 0.0 collective-permute-done.4.refs_0_.refs_6_
  27.1 3.5 %gram.1 = (f32[9,1,128]{2,1,0:T(1,128)S(1)}, f32[9,1,128]{2,1,0:T(1,128)S(1)}) custom-call(s32[1,64]{1,0:T(1,128)S(1)} %get-tuple-element.25.owners, f32[7,16,256]{2,1,0:T(8,128)S(1)} %collective-permute-done.4.refs_0_.refs_6_, f32[7,16,256]{2,1,0:T(8,128)S(1)} %collective-permute-done.5.refs_1_.refs_7_, s32[4,64,128]{2,1,0:T(8,128)S(1)} %copy-done.1, ...), custom_call_target="tpu_custom_call" | custom-call | flops 1000 | bytes 1000 | tf_op jit(solution)/shard_map/gram/pallas_call | solution.py:698
  30.6 0.0 collective-permute-start.10
  30.7 0.6 %collective-permute-start.14 = (f32[16,16,256]{2,1,0:T(8,128)S(1)}, f32[16,16,256]{2,1,0:T(8,128)S(1)}, u32[]{:S(2)}, u32[]{:S(2)}) collective-permute-start(f32[16,16,256]{2,1,0:T(8,128)S(1)} %get-tuple-element.43.refs_12_), channel_id=1, source_target_pairs={{0,1},{1,0},{2,3},{3,2},{4,5},{5,4},{6,7},{7,6},{8,9},{9,8},{10,11... | collective-permute-start | bytes 786440 | tf_op jit(solution)/shard_map/ppermute | solution.py:589
  31.2 0.1 collective-permute-start.11
  31.3 0.5 collective-permute-done.10
  31.8 0.7 %broadcast_in_dim.3 = f32[32,9,1,128]{3,2,1,0:T(1,128)} broadcast(f32[9,128]{1,0:T(8,128)S(1)} %bitcast.5), dimensions={1,3} | broadcast | bytes 152064 | tf_op jit(solution)/shard_map/broadcast_in_dim | solution.py:712
  32.5 3.2 %all-to-all-start = ((f32[32,9,1,128]{3,2,1,0:T(1,128)}), f32[32,9,1,128]{3,2,1,0:T(1,128)S(1)}, u32[]{:S(2)}, u32[]{:S(2)}) async-start(f32[32,9,1,128]{3,2,1,0:T(1,128)} %broadcast_in_dim.3), calls=%async_computation | async-start | bytes 294912 | tf_op jit(solution)/shard_map/all_to_all | solution.py:713
  35.8 1.9 %collective-permute-done.12 = f32[32,16,256]{2,1,0:T(8,128)} collective-permute-done((f32[32,16,256]{2,1,0:T(8,128)S(1)}, f32[32,16,256]{2,1,0:T(8,128)}, u32[]{:S(2)}, u32[]{:S(2)}) %collective-permute-start.12) | collective-permute-done | bytes 524320 | tf_op jit(solution)/shard_map/ppermute | solution.py:589
  37.7 1.1 %fusion = (f32[16,16,256]{2,1,0:T(8,128)S(1)}, f32[16,16,256]{2,1,0:T(8,128)S(1)}) fusion(f32[32,16,256]{2,1,0:T(8,128)} %collective-permute-done.12), kind=kLoop, calls=%fused_computation.1 | loop fusion | bytes 1048576 | tf_op jit(solution)/shard_map/slice | solution.py:688
  38.7 0.1 collective-permute-start.15
  38.8 0.5 %collective-permute-start.13 = (f32[16,16,256]{2,1,0:T(8,128)S(1)}, f32[16,16,256]{2,1,0:T(8,128)S(1)}, u32[]{:S(2)}, u32[]{:S(2)}) collective-permute-start(f32[16,16,256]{2,1,0:T(8,128)S(1)} %get-tuple-element.42.refs_10_), channel_id=1, source_target_pairs={{0,1},{1,0},{2,3},{3,2},{4,5},{5,4},{6,7},{7,6},{8,9},{9,8},{10,11... | collective-permute-start | bytes 786440 | tf_op jit(solution)/shard_map/ppermute | solution.py:589
  39.3 0.0 collective-permute-done.14.refs_13_
  39.3 0.0 collective-permute-done.11.refs_9_
  39.3 4.9 %all-to-all-done.sums = f32[32,9,1,128]{3,2,1,0:T(1,128)S(1)} async-done(((f32[32,9,1,128]{3,2,1,0:T(1,128)}), f32[32,9,1,128]{3,2,1,0:T(1,128)S(1)}, u32[]{:S(2)}, u32[]{:S(2)}) %all-to-all-start) | async-done | bytes 147488 | tf_op jit(solution)/shard_map/all_to_all | solution.py:713
  44.2 0.0 collective-permute-done.15.refs_15_
  44.2 0.0 collective-permute-done.13.refs_11_
  44.2 4.2 %analysis.1 = f32[16,3,16,256]{3,2,1,0:T(8,128)} custom-call(f32[32,9,1,128]{3,2,1,0:T(1,128)S(1)} %all-to-all-done.sums, f32[10,16,256]{2,1,0:T(8,128)S(1)} %hold.2.refs_0_, f32[10,16,256]{2,1,0:T(8,128)S(1)} %collective-permute-done.refs_1_, f32[10,16,256]{2,1,0:T(8,128)S(1)} %hold.3.refs_0_.refs_2_, ...), custom_call_target="tpu_custom_call" | custom-call | tf_op jit(solution)/shard_map/analysis/pallas_call | solution.py:715
  (5 shorter events, 0.1 us)
Async XLA Ops:
  0.0 2.3 %copy-start.3 = (f32[16,256]{1,0:T(8,128)S(1)}, f32[16,256]{1,0:T(8,128)}, u32[]{:S(2)}) copy-start(f32[16,256]{1,0:T(8,128)} %depth.2) | copy-start | bytes 49156
  0.0 2.3 %copy-start = (f32[16,3,16,256]{3,2,1,0:T(8,128)S(1)}, f32[16,3,16,256]{3,2,1,0:T(8,128)}, u32[]{:S(2)}) copy-start(f32[16,3,16,256]{3,2,1,0:T(8,128)} %state.3) | copy-start | bytes 2359300
  2.3 1.1 %copy-start.7 = (f32[88,256]{1,0:T(8,128)S(1)}, f32[88,256]{1,0:T(8,128)}, u32[]{:S(2)}) copy-start(f32[88,256]{1,0:T(8,128)} %get-tuple-element.23) | copy-start | bytes 270340
  2.3 6.9 %copy-start.9 = (f32[16,256]{1,0:T(8,128)S(1)}, f32[16,256]{1,0:T(8,128)}, u32[]{:S(2)}) copy-start(f32[16,256]{1,0:T(8,128)} %get-tuple-element.30) | copy-start | bytes 49156
  2.3 7.3 %copy-start.6 = (f32[88,256]{1,0:T(8,128)S(1)}, f32[88,256]{1,0:T(8,128)}, u32[]{:S(2)}) copy-start(f32[88,256]{1,0:T(8,128)} %get-tuple-element.26) | copy-start | bytes 270340
  2.9 7.4 %collective-permute-start = (f32[10,16,256]{2,1,0:T(8,128)S(1)}, f32[10,16,256]{2,1,0:T(8,128)S(1)}, u32[]{:S(2)}, u32[]{:S(2)}) collective-permute-start(f32[10,16,256]{2,1,0:T(8,128)S(1)} %inner.1.refs_0_), channel_id=1, source_target_pairs={{0,1},{1,0},{2,3},{3,2},{4,5},{5,4},{6,7},{7,6},{8,9},{9,8},{10,11... | collective-permute-start | bytes 491528 | tf_op jit(solution)/shard_map/ppermute | solution.py:589
  3.4 13.0 %collective-permute-start.2 = (f32[88,256]{1,0:T(8,128)S(1)}, f32[88,256]{1,0:T(8,128)S(1)}, u32[]{:S(2)}, u32[]{:S(2)}) collective-permute-start(f32[88,256]{1,0:T(8,128)S(1)} %copy-done.7), channel_id=1, source_target_pairs={{4,0},{8,4},{12,8},{16,12},{20,16},{24,20},{28,24},{0,28},{5,1},{9... | collective-permute-start | bytes 270344 | tf_op jit(solution)/shard_map/ppermute | solution.py:609
  9.2 7.7 %collective-permute-start.3 = (f32[16,256]{1,0:T(8,128)S(1)}, f32[16,256]{1,0:T(8,128)S(1)}, u32[]{:S(2)}, u32[]{:S(2)}) collective-permute-start(f32[16,256]{1,0:T(8,128)S(1)} %copy-done.9), channel_id=1, source_target_pairs={{0,24},{1,9},{2,22},{3,15},{4,28},{5,13},{6,26},{7,19},{8,0},{9,17... | collective-permute-start | bytes 49160 | tf_op jit(solution)/shard_map/ppermute | solution.py:612
  9.6 3.0 %copy-start.1 = (s32[4,64,128]{2,1,0:T(8,128)S(1)}, s32[4,64,128]{2,1,0:T(8,128)}, u32[]{:S(2)}) copy-start(s32[4,64,128]{2,1,0:T(8,128)} %refs_2_.3) | copy-start | bytes 393220
  9.6 3.0 %copy-start.2 = (f32[4,64,128]{2,1,0:T(8,128)S(1)}, f32[4,64,128]{2,1,0:T(8,128)}, u32[]{:S(2)}) copy-start(f32[4,64,128]{2,1,0:T(8,128)} %refs_3_.3) | copy-start | bytes 393220
  9.6 7.2 %collective-permute-start.1 = (f32[88,256]{1,0:T(8,128)S(1)}, f32[88,256]{1,0:T(8,128)S(1)}, u32[]{:S(2)}, u32[]{:S(2)}) collective-permute-start(f32[88,256]{1,0:T(8,128)S(1)} %copy-done.6), channel_id=1, source_target_pairs={{0,4},{4,8},{8,12},{12,16},{16,20},{20,24},{24,28},{28,0},{1,5},{5... | collective-permute-start | bytes 270344 | tf_op jit(solution)/shard_map/ppermute | solution.py:610
  10.3 2.3 %copy-start.5 = (s32[64,1]{0,1:T(1,128)S(1)}, s32[64,1]{0,1:T(1,128)}, u32[]{:S(2)}) copy-start(s32[64,1]{0,1:T(1,128)} %param.11) | copy-start | bytes 772
  10.3 7.5 %collective-permute-start.6 = (f32[10,16,256]{2,1,0:T(8,128)S(1)}, f32[10,16,256]{2,1,0:T(8,128)S(1)}, u32[]{:S(2)}, u32[]{:S(2)}) collective-permute-start(f32[10,16,256]{2,1,0:T(8,128)S(1)} %hold.2.refs_0_), channel_id=1, source_target_pairs={{0,2},{1,3},{2,0},{3,1},{4,6},{5,7},{6,4},{7,5},{8,10},{9,11},{10,... | collective-permute-start | bytes 491528 | tf_op jit(solution)/shard_map/ppermute | solution.py:589
  17.8 2.3 %copy-start.8 = (f32[16,256]{1,0:T(8,128)S(1)}, f32[16,256]{1,0:T(8,128)}, u32[]{:S(2)}) copy-start(f32[16,256]{1,0:T(8,128)} %get-tuple-element.37) | copy-start | bytes 49156
  17.8 4.5 %copy-start.4 = (f32[16,256]{1,0:T(8,128)S(1)}, f32[16,256]{1,0:T(8,128)}, u32[]{:S(2)}) copy-start(f32[16,256]{1,0:T(8,128)} %get-tuple-element.32.refs_7_) | copy-start | bytes 49156
  17.8 4.4 %collective-permute-start.7 = (f32[10,16,256]{2,1,0:T(8,128)S(1)}, f32[10,16,256]{2,1,0:T(8,128)S(1)}, u32[]{:S(2)}, u32[]{:S(2)}) collective-permute-start(f32[10,16,256]{2,1,0:T(8,128)S(1)} %hold.3.refs_0_.refs_2_), channel_id=1, source_target_pairs={{0,1},{1,0},{2,3},{3,2},{4,5},{5,4},{6,7},{7,6},{8,9},{9,8},{10,11... | collective-permute-start | bytes 491528 | tf_op jit(solution)/shard_map/ppermute | solution.py:589
  17.9 3.4 %collective-permute-start.8 = (f32[7,16,256]{2,1,0:T(8,128)S(1)}, f32[7,16,256]{2,1,0:T(8,128)S(1)}, u32[]{:S(2)}, u32[]{:S(2)}) collective-permute-start(f32[7,16,256]{2,1,0:T(8,128)S(1)} %get-tuple-element.31.refs_1_.refs_2_.refs_4_), channel_id=1, source_target_pairs={{0,1},{1,0},{2,3},{3,2},{4,5},{5,4},{6,7},{7,6},{8,9},{9,8},{10,11... | collective-permute-start | bytes 344072 | tf_op jit(solution)/shard_map/ppermute | solution.py:589
  18.4 8.7 %collective-permute-start.5 = (f32[7,16,256]{2,1,0:T(8,128)S(1)}, f32[7,16,256]{2,1,0:T(8,128)S(1)}, u32[]{:S(2)}, u32[]{:S(2)}) collective-permute-start(f32[7,16,256]{2,1,0:T(8,128)S(1)} %get-tuple-element.31.refs_1_.refs_2_.refs_4_), channel_id=1, source_target_pairs={{0,3},{1,2},{2,1},{3,0},{4,7},{5,6},{6,5},{7,4},{8,11},{9,10},{10,... | collective-permute-start | bytes 344072 | tf_op jit(solution)/shard_map/ppermute | solution.py:589
  19.3 7.8 %collective-permute-start.4 = (f32[7,16,256]{2,1,0:T(8,128)S(1)}, f32[7,16,256]{2,1,0:T(8,128)S(1)}, u32[]{:S(2)}, u32[]{:S(2)}) collective-permute-start(f32[7,16,256]{2,1,0:T(8,128)S(1)} %get-tuple-element.31.refs_1_.refs_2_.refs_4_), channel_id=1, source_target_pairs={{0,2},{1,3},{2,0},{3,1},{4,6},{5,7},{6,4},{7,5},{8,10},{9,11},{10,... | collective-permute-start | bytes 344072 | tf_op jit(solution)/shard_map/ppermute | solution.py:589
  20.1 6.9 %collective-permute-start.9 = (f32[16,256]{1,0:T(8,128)S(1)}, f32[16,256]{1,0:T(8,128)S(1)}, u32[]{:S(2)}, u32[]{:S(2)}) collective-permute-start(f32[16,256]{1,0:T(8,128)S(1)} %copy-done.8), channel_id=1, source_target_pairs={{0,16},{4,20},{8,24},{12,28},{16,0},{20,4},{24,8},{28,12},{1,17},{... | collective-permute-start | bytes 49160 | tf_op jit(solution)/shard_map/ppermute | solution.py:665
  21.3 16.3 %collective-permute-start.12 = (f32[32,16,256]{2,1,0:T(8,128)S(1)}, f32[32,16,256]{2,1,0:T(8,128)}, u32[]{:S(2)}, u32[]{:S(2)}) collective-permute-start(f32[32,16,256]{2,1,0:T(8,128)S(1)} %get-tuple-element.40), channel_id=1, source_target_pairs={{0,2},{1,3},{2,0},{3,1},{4,6},{5,7},{6,4},{7,5},{8,10},{9,11},{10,... | collective-permute-start | bytes 1572872 | tf_op jit(solution)/shard_map/ppermute | solution.py:589
  30.6 1.2 %collective-permute-start.10 = (f32[9,1,128]{2,1,0:T(1,128)S(1)}, f32[9,1,128]{2,1,0:T(1,128)S(1)}, u32[]{:S(2)}, u32[]{:S(2)}) collective-permute-start(f32[9,1,128]{2,1,0:T(1,128)S(1)} %get-tuple-element.39), channel_id=1, source_target_pairs={{0,1},{1,0},{2,3},{3,2},{4,5},{5,4},{6,7},{7,6},{8,9},{9,8},{10,11... | collective-permute-start | bytes 13832 | tf_op jit(solution)/shard_map/ppermute | solution.py:589
  30.7 8.6 %collective-permute-start.14 = (f32[16,16,256]{2,1,0:T(8,128)S(1)}, f32[16,16,256]{2,1,0:T(8,128)S(1)}, u32[]{:S(2)}, u32[]{:S(2)}) collective-permute-start(f32[16,16,256]{2,1,0:T(8,128)S(1)} %get-tuple-element.43.refs_12_), channel_id=1, source_target_pairs={{0,1},{1,0},{2,3},{3,2},{4,5},{5,4},{6,7},{7,6},{8,9},{9,8},{10,11... | collective-permute-start | bytes 786440 | tf_op jit(solution)/shard_map/ppermute | solution.py:589
  31.2 8.1 %collective-permute-start.11 = (f32[16,16,256]{2,1,0:T(8,128)S(1)}, f32[16,16,256]{2,1,0:T(8,128)S(1)}, u32[]{:S(2)}, u32[]{:S(2)}) collective-permute-start(f32[16,16,256]{2,1,0:T(8,128)S(1)} %get-tuple-element.44.refs_8_), channel_id=1, source_target_pairs={{0,1},{1,0},{2,3},{3,2},{4,5},{5,4},{6,7},{7,6},{8,9},{9,8},{10,11... | collective-permute-start | bytes 786440 | tf_op jit(solution)/shard_map/ppermute | solution.py:589
  32.5 11.7 %all-to-all-start = ((f32[32,9,1,128]{3,2,1,0:T(1,128)}), f32[32,9,1,128]{3,2,1,0:T(1,128)S(1)}, u32[]{:S(2)}, u32[]{:S(2)}) async-start(f32[32,9,1,128]{3,2,1,0:T(1,128)} %broadcast_in_dim.3), calls=%async_computation | async-start | bytes 294912 | tf_op jit(solution)/shard_map/all_to_all | solution.py:713
  38.7 5.5 %collective-permute-start.15 = (f32[16,16,256]{2,1,0:T(8,128)S(1)}, f32[16,16,256]{2,1,0:T(8,128)S(1)}, u32[]{:S(2)}, u32[]{:S(2)}) collective-permute-start(f32[16,16,256]{2,1,0:T(8,128)S(1)} %get-tuple-element.41.refs_14_), channel_id=1, source_target_pairs={{0,1},{1,0},{2,3},{3,2},{4,5},{5,4},{6,7},{7,6},{8,9},{9,8},{10,11... | collective-permute-start | bytes 786440 | tf_op jit(solution)/shard_map/ppermute | solution.py:589
  38.8 5.4 %collective-permute-start.13 = (f32[16,16,256]{2,1,0:T(8,128)S(1)}, f32[16,16,256]{2,1,0:T(8,128)S(1)}, u32[]{:S(2)}, u32[]{:S(2)}) collective-permute-start(f32[16,16,256]{2,1,0:T(8,128)S(1)} %get-tuple-element.42.refs_10_), channel_id=1, source_target_pairs={{0,1},{1,0},{2,3},{3,2},{4,5},{5,4},{6,7},{7,6},{8,9},{9,8},{10,11... | collective-permute-start | bytes 786440 | tf_op jit(solution)/shard_map/ppermute | solution.py:589
